TPU v7x, 256 devices: a whole 4x4x8 slice. The times are simulated.
256 devices in a mesh: section: 2 (over core), rep: 32 (over z, x), tp: 4 (over y).
Axes of the slice: x: 4, y: 4, z: 8, core: 2. Of those that a mesh axis runs over, the one named last changes fastest.
Arguments:
- inputs: bfloat16 [1, 32, 128, 2560], P(None, 'rep', None, 'tp'), may hold values from -50 to 50
- weights: bfloat16 [2, 2560, 2560], P('section', None, 'tp'), may hold values from -0.125 to 0.125
- wiring: int32 [1, 1, 32], replicated, may hold values from 0 to 31, as said below
- lengths: int32 [1, 32], replicated, may hold values from 1 to 128, 3072 in all within a row
- targets: bfloat16 [1, 32, 128, 2560], P(None, 'rep', None, 'tp'), may hold values from -6 to 6
Outputs:
- acts: bfloat16 [2, 1, 32, 2, 128, 2560], P('section', None, 'rep', None, None, 'tp')
- grad_w: float32 [2, 2560, 2560], P('section', 'rep', 'tp')
Inputs may be any that keep to these rules, and one draw needn't show every extreme that they name: wiring[s - 1, w, j] is the replica of segment s that holds micro-batch j of wave w. In every segment and wave no replica holds more than 2 micro-batches and some replica holds exactly 2. Two micro-batches of one wave that share a replica at segment s - 1 never share a replica at segment s.
All inputs are finite; a program needn't handle non-finite values.
Results may differ from a plain program's by a relative error of at most 0.019.
Values may be sent and summed in bfloat16 or wider, within the bound.
No kernel may reach another device: no remote copies, remote signals or barrier semaphores. Data moves between devices by JAX's collectives and lax.ppermute only.
A program may use at most 64 MiB of HBM per device.

v0:
```python
import math

import jax
import jax.numpy as jnp
from jax import lax
from jax.sharding import PartitionSpec as P

WCAP = 2


epsilon = 1e-06
root_half = 0.7071067811865476
normal_peak = 0.3989422804014327


def from_behind(value, axis, steps):
    count = lax.axis_size(axis)
    initial, last = (max(0, -steps), min(count, count - steps))
    return lax.ppermute(value, axis, [(source, source + steps) for source in range(initial, last)])


def gelu_value(mixed_now):
    return 0.5 * mixed_now * (1.0 + lax.erf(mixed_now * root_half))


def gelu_slope(mixed_now):
    return (
        0.5 * (1.0 + lax.erf(mixed_now * root_half))
        + mixed_now * jnp.exp(-0.5 * mixed_now * mixed_now) * normal_peak
    )


def pick(table, index):
    return lax.dynamic_index_in_dim(table, index, 0, keepdims=False)


def store_at(table, value, index, live):
    old_value = lax.dynamic_index_in_dim(table, index, 0, keepdims=False)
    return lax.dynamic_update_index_in_dim(table, jnp.where(live, value, old_value), index, 0)


def holder_tables(wiring, replicas):
    first_row = jnp.arange(replicas, dtype=jnp.int32)[None, None, :]
    holder = jnp.concatenate([first_row, wiring], axis=0)
    same_rep = holder[..., :, None] == holder[..., None, :]
    earlier = jnp.arange(replicas)[None, :] < jnp.arange(replicas)[:, None]
    slot_of = jnp.sum(jnp.where(same_rep & earlier, 1, 0), axis=-1).astype(jnp.int32)
    return (holder, slot_of)


def route_tables(from_rep, from_slot, to_rep, to_slot, own_rep, slot_count):
    replicas = from_rep.shape[-1]
    rep_ids = jnp.arange(replicas, dtype=jnp.int32)
    slot_ids = jnp.arange(slot_count, dtype=jnp.int32)
    sending = (
        (from_rep == own_rep)[..., None, None]
        & (to_rep[..., None, None] == rep_ids[:, None])
        & (from_slot[..., None, None] == slot_ids)
    )
    coming = (
        (to_rep == own_rep)[..., None, None]
        & (to_slot[..., None, None] == slot_ids[:, None])
        & (from_rep[..., None, None] == rep_ids)
    )
    send_map = jnp.sum(jnp.where(sending, 1.0, 0.0), axis=1).astype(jnp.bfloat16)
    come_map = jnp.sum(jnp.where(coming, 1.0, 0.0), axis=1).astype(jnp.bfloat16)
    return (send_map, come_map)


def regroup(buffer, send_map, come_map):
    outgoing = jnp.einsum(
        "wdc,wctf->dwtf", send_map, buffer, preferred_element_type=jnp.float32
    ).astype(jnp.bfloat16)
    incoming = lax.all_to_all(outgoing, "rep", split_axis=0, concat_axis=0, tiled=True)
    return jnp.einsum(
        "wcq,qwtf->wctf", come_map, incoming, preferred_element_type=jnp.float32
    ).astype(jnp.bfloat16)


def segment_move(buffer, offset):
    return from_behind(buffer, "section", offset)


def on_device(inputs, weights, wiring, lengths, targets):
    replicas = lax.axis_size("rep")
    segment_count = lax.axis_size("section")
    tp_count = lax.axis_size("tp")
    own_rep = lax.axis_index("rep")
    segment_pos = lax.axis_index("section")
    wave_count, _, tokens, local_width = inputs.shape
    weight = weights[0]
    feat_width = weight.shape[0]
    slot_count = WCAP
    step_count = segment_count + wave_count - 1
    holder, slot_of = holder_tables(wiring, replicas)
    last_rep = holder[segment_count - 1]
    last_slot = slot_of[segment_count - 1]
    start_rep = jnp.arange(replicas, dtype=jnp.int32)[None, :]
    start_slot = jnp.zeros((wave_count, replicas), jnp.int32)
    empty_slots = jnp.zeros((wave_count, slot_count - 1, tokens, local_width), jnp.bfloat16)
    entry = jnp.concatenate([inputs, empty_slots], axis=1)
    goal_send, goal_come = route_tables(
        start_rep, start_slot, last_rep, last_slot, own_rep, slot_count
    )
    goal = regroup(jnp.concatenate([targets, empty_slots], axis=1), goal_send, goal_come)
    held_here = (last_rep == own_rep)[:, :, None] & (
        last_slot[:, :, None] == jnp.arange(slot_count)
    )
    slot_length = jnp.sum(jnp.where(held_here, lengths[:, :, None], 0), axis=1)
    valid_mask = jnp.where(jnp.arange(tokens)[None, None, :] < slot_length[:, :, None], 1.0, 0.0)
    loss_scale = 1.0 / math.sqrt(wave_count * replicas * tokens)

    def crossing_maps(segment_from, segment_to, wave_at, open_gate):
        from_rep = pick(pick(holder, segment_from), wave_at)[None]
        from_slot = pick(pick(slot_of, segment_from), wave_at)[None]
        to_rep = pick(pick(holder, segment_to), wave_at)[None]
        to_slot = pick(pick(slot_of, segment_to), wave_at)[None]
        send_map, come_map = route_tables(from_rep, from_slot, to_rep, to_slot, own_rep, slot_count)
        return (send_map * open_gate.astype(jnp.bfloat16), come_map)

    def forward_block(step_index, arrived, stores):
        x_store, normed_store, mixed_store, scale_store, out_store = stores
        wave_now = step_index - segment_pos
        live = (wave_now >= 0) & (wave_now < wave_count)
        wave_at = jnp.clip(wave_now, 0, wave_count - 1)
        current = jnp.where(segment_pos == 0, pick(entry, wave_at), arrived)
        gathered = lax.all_gather(current, "tp", axis=2, tiled=True)
        wide_now = gathered.astype(jnp.float32)
        row_scale = lax.rsqrt(jnp.mean(wide_now * wide_now, axis=-1, keepdims=True) + epsilon)
        normed = (wide_now * row_scale).astype(jnp.bfloat16)
        mixed_now = jnp.einsum("ctd,dk->ctk", normed, weight, preferred_element_type=jnp.float32)
        output = (current.astype(jnp.float32) + gelu_value(mixed_now)).astype(jnp.bfloat16)
        stores = (
            store_at(x_store, current, wave_at, live),
            store_at(normed_store, normed, wave_at, live),
            store_at(mixed_store, mixed_now, wave_at, live),
            store_at(scale_store, row_scale, wave_at, live),
            store_at(out_store, output, wave_at, live),
        )
        return (output, live, wave_at, stores)

    def forward_step(step_index, state_now):
        arrived, stores = state_now
        output, live, wave_at, stores = forward_block(step_index, arrived, stores)
        send_map, come_map = crossing_maps(
            segment_pos,
            jnp.minimum(segment_pos + 1, segment_count - 1),
            wave_at,
            live & (segment_pos < segment_count - 1),
        )
        moved = regroup(output[None], send_map, come_map)[0]
        return (segment_move(moved, 1), stores)

    blank = jnp.zeros((slot_count, tokens, local_width), jnp.bfloat16)
    stores = (
        jnp.zeros((wave_count, slot_count, tokens, local_width), jnp.bfloat16),
        jnp.zeros((wave_count, slot_count, tokens, feat_width), jnp.bfloat16),
        jnp.zeros((wave_count, slot_count, tokens, local_width), jnp.float32),
        jnp.zeros((wave_count, slot_count, tokens, 1), jnp.float32),
        jnp.zeros((wave_count, slot_count, tokens, local_width), jnp.bfloat16),
    )
    arrived, stores = lax.fori_loop(0, step_count - 1, forward_step, (blank, stores))
    _, _, _, stores = forward_block(step_count - 1, arrived, stores)
    x_store, normed_store, mixed_store, scale_store, out_store = stores
    target_grad = (
        (out_store.astype(jnp.float32) - goal.astype(jnp.float32))
        * valid_mask[..., None]
        * loss_scale
    ).astype(jnp.bfloat16)

    def backward_block(step_index, arrived, sums):
        grad_total, delta_store = sums
        wave_now = step_index - (segment_count - 1 - segment_pos)
        live = (wave_now >= 0) & (wave_now < wave_count)
        wave_at = jnp.clip(wave_now, 0, wave_count - 1)
        grad_now = jnp.where(segment_pos == segment_count - 1, pick(target_grad, wave_at), arrived)
        grad_now = jnp.where(live, grad_now, jnp.zeros_like(grad_now))
        mixed_now = pick(mixed_store, wave_at)
        delta_now = (grad_now.astype(jnp.float32) * gelu_slope(mixed_now)).astype(jnp.bfloat16)
        normed = pick(normed_store, wave_at)
        grad_total = grad_total + jnp.einsum(
            "ctd,ctk->dk", normed, delta_now, preferred_element_type=jnp.float32
        )
        back_part = jnp.einsum("ctk,dk->ctd", delta_now, weight, preferred_element_type=jnp.float32)
        stat_part = (
            jnp.sum(mixed_now * delta_now.astype(jnp.float32), axis=-1, keepdims=True) / feat_width
        )
        stat_cols = jnp.broadcast_to(stat_part, (slot_count, tokens, tp_count))
        back_sum, stat_sum = (
            lax.psum_scatter(
                back_part.astype(jnp.bfloat16), "tp", scatter_dimension=2, tiled=True
            ).astype(jnp.float32),
            lax.psum_scatter(
                stat_cols.astype(jnp.bfloat16), "tp", scatter_dimension=2, tiled=True
            ).astype(jnp.float32),
        )
        row_scale = pick(scale_store, wave_at)
        wide_now = pick(x_store, wave_at).astype(jnp.float32)
        grad_next = (
            grad_now.astype(jnp.float32) + row_scale * (back_sum - wide_now * row_scale * stat_sum)
        ).astype(jnp.bfloat16)
        return (grad_next, live, wave_at, (grad_total, delta_store))

    def backward_step(step_index, state_now):
        arrived, sums = state_now
        grad_next, live, wave_at, sums = backward_block(step_index, arrived, sums)
        send_map, come_map = crossing_maps(
            segment_pos, jnp.maximum(segment_pos - 1, 0), wave_at, live & (segment_pos > 0)
        )
        moved = regroup(grad_next[None], send_map, come_map)[0]
        return (segment_move(moved, -1), sums)

    sums = (
        jnp.zeros((feat_width, local_width), jnp.float32),
        jnp.zeros((wave_count, slot_count, tokens, local_width), jnp.bfloat16),
    )
    arrived, sums = lax.fori_loop(0, step_count - 1, backward_step, (blank, sums))
    _, _, _, sums = backward_block(step_count - 1, arrived, sums)
    grad_total, delta_store = sums
    grad_rows = lax.psum_scatter(
        grad_total.astype(jnp.bfloat16), "rep", scatter_dimension=0, tiled=True
    ).astype(jnp.float32)
    acts = out_store.reshape(1, wave_count, 1, slot_count, tokens, local_width)
    return (acts, grad_rows.reshape(1, feat_width // replicas, local_width))


def solution(mesh):
    in_specs = (
        P(None, "rep", None, "tp"),
        P("section", None, "tp"),
        P(),
        P(),
        P(None, "rep", None, "tp"),
    )
    out_specs = (P("section", None, "rep", None, None, "tp"), P("section", "rep", "tp"))
    return jax.shard_map(
        on_device, mesh=mesh, in_specs=in_specs, out_specs=out_specs, check_vma=False
    )
```

profile of v0, /device:TPU:1, one launch (start us, length us, event | category | flops | bytes accessed | tf_op | source)
XLA Modules:
  0.0 704.4 jit_solution(11509540340468920055)
XLA Ops:
  7.2 0.0 copy-start
  7.2 0.0 all-gather.3.cloned.1.call-start
  7.2 1.8 bitcast_select_fusion.1
  9.1 0.0 all-gather.3.cloned.1.call-update
  9.1 0.7 pad_add_fusion
  9.8 0.2 select_reduce_fusion.6
  10.0 0.8 broadcast_compare_fusion.3
  10.8 0.1 fusion.37
  10.9 0.1 select_reduce_fusion
  11.0 29.9 %all-gather.3.cloned.1.call-done = bf16[2,128,2560]{2,1,0:T(8,128)(2,1)} async-done(((bf16[2,128,640]{2,1,0:T(8,128)(2,1)}), bf16[2,128,2560]{2,1,0:T(8,128)(2,1)}) %all-gather.3.cloned.1.call-update) | async-done | bytes 1310736 | tf_op jit(solution)/shard_map/while/body/eval_jaxpr/all_gather | solution.py:127
  40.9 1.7 fusion.15
  42.6 3.4 add_convert_fusion.1
  46.0 0.7 copy-done.11
  46.7 1.6 convert_bitcast_fusion.2
  48.3 4.1 copy.27
  52.4 9.8 %all-to-all-start = ((bf16[32,1,128,640]{3,2,1,0:T(8,128)(2,1)}), bf16[32,1,128,640]{3,2,1,0:T(8,128)(2,1)}, u32[]{:S(2)}, u32[]{:S(2)}) async-start(bf16[32,1,128,640]{3,2,1,0:T(8,128)(2,1)} %copy.27), calls=%async_computation | async-start | bytes 10485760 | tf_op jit(solution)/shard_map/while/body/eval_jaxpr/all_to_all | solution.py:74
  62.2 0.3 copy.30
  62.5 0.1 fusion.38
  62.6 0.1 select_reduce_fusion.2
  62.7 1.6 convert_bitcast_fusion.1
  64.3 4.2 copy.31
  68.4 108.0 %all-to-all-done = bf16[32,1,128,640]{3,2,1,0:T(8,128)(2,1)} async-done(((bf16[32,1,128,640]{3,2,1,0:T(8,128)(2,1)}), bf16[32,1,128,640]{3,2,1,0:T(8,128)(2,1)}, u32[]{:S(2)}, u32[]{:S(2)}) %all-to-all-start) | async-done | bytes 5242912 | tf_op jit(solution)/shard_map/while/body/eval_jaxpr/all_to_all | solution.py:74
  176.5 9.0 %all-to-all-start.1 = ((bf16[32,1,128,640]{3,2,1,0:T(8,128)(2,1)}), bf16[32,1,128,640]{3,2,1,0:T(8,128)(2,1)}, u32[]{:S(2)}, u32[]{:S(2)}) async-start(bf16[32,1,128,640]{3,2,1,0:T(8,128)(2,1)} %copy.31), calls=%async_computation.1 | async-start | bytes 10485760 | tf_op jit(solution)/shard_map/all_to_all | solution.py:74
  185.5 0.2 all-gather.5.cloned.1.call-start
  185.7 0.1 select_reduce_fusion.1
  185.9 6.1 fusion.5
  192.0 1.3 collective-permute-start
  193.3 2.5 collective-permute-done
  195.8 0.7 copy-done.5
  196.5 0.8 bitcast_select_fusion
  197.2 0.0 all-gather.5.cloned.1.call-update
  197.3 0.0 reduce-scatter.7.cloned.1.call-start
  197.3 0.1 fusion.40
  197.5 0.1 select_reduce_fusion.3
  197.6 0.1 compare_select_fusion
  197.6 102.0 %all-to-all-done.1 = bf16[32,1,128,640]{3,2,1,0:T(8,128)(2,1)} async-done(((bf16[32,1,128,640]{3,2,1,0:T(8,128)(2,1)}), bf16[32,1,128,640]{3,2,1,0:T(8,128)(2,1)}, u32[]{:S(2)}, u32[]{:S(2)}) %all-to-all-start.1) | async-done | bytes 5242912 | tf_op jit(solution)/shard_map/all_to_all | solution.py:74
  299.6 6.8 fusion.3
  306.4 1.7 fusion.17
  308.1 4.2 multiply_reduce_fusion
  312.2 0.7 copy-done.12
  312.9 2.4 convolution_convert_fusion
  315.3 3.4 copy.42
  318.7 0.0 copy-start.17
  318.7 1.3 copy.70
  320.0 0.0 reduce-scatter.7.cloned.1.call-update
  320.0 0.6 dynamic-slice.23
  320.6 8.8 %all-reduce.2 = bf16[2,128,4]{1,0,2:T(2,128)(2,1)S(1)} all-reduce(bf16[2,128,4]{1,0,2:T(2,128)(2,1)S(1)} %broadcast_in_dim.172), channel_id=3, replica_groups=mesh['section'=2,'rep'=32,'tp'=4] {'tp'}, use_global_device_ids=true, to_apply=%region_11.12.clone | all-reduce | flops 1024 | bytes 4096
  329.4 0.7 bitcast_convert_fusion.1
  330.0 20.4 %reduce-scatter.7.cloned.1.call-done = bf16[640,256]{1,0:T(8,128)(2,1)} async-done(((bf16[2560,256]{1,0:T(8,128)(2,1)}), bf16[640,256]{1,0:T(8,128)(2,1)}) %reduce-scatter.7.cloned.1.call-update) | async-done | bytes 327696
  350.4 1.1 reshape.857
  351.5 0.9 copy.43
  352.4 0.3 fusion.22
  352.7 1.6 convert_bitcast_fusion
  354.3 4.2 copy.36
  358.5 9.7 %all-to-all-start.2 = ((bf16[32,1,128,640]{3,2,1,0:T(8,128)(2,1)}), bf16[32,1,128,640]{3,2,1,0:T(8,128)(2,1)}, u32[]{:S(2)}, u32[]{:S(2)}) async-start(bf16[32,1,128,640]{3,2,1,0:T(8,128)(2,1)} %copy.36), calls=%async_computation.2 | async-start | bytes 10485760 | tf_op jit(solution)/shard_map/while/body/eval_jaxpr/all_to_all | solution.py:74
  368.1 0.0 reduce-scatter.5.cloned.1.call-start
  368.2 114.2 %all-to-all-done.2 = bf16[32,1,128,640]{3,2,1,0:T(8,128)(2,1)} async-done(((bf16[32,1,128,640]{3,2,1,0:T(8,128)(2,1)}), bf16[32,1,128,640]{3,2,1,0:T(8,128)(2,1)}, u32[]{:S(2)}, u32[]{:S(2)}) %all-to-all-start.2) | async-done | bytes 5242912 | tf_op jit(solution)/shard_map/while/body/eval_jaxpr/all_to_all | solution.py:74
  482.4 6.2 fusion.1
  488.7 5.5 collective-permute-start.1
  494.2 1.5 fusion.36
  495.8 3.7 fusion
  499.5 0.0 reduce-scatter.5.cloned.1.call-update
  499.6 196.7 %reduce-scatter.5.cloned.1.call-done = bf16[80,640]{1,0:T(8,128)(2,1)} async-done(((bf16[2560,640]{1,0:T(8,128)(2,1)}), bf16[80,640]{1,0:T(8,128)(2,1)}) %reduce-scatter.5.cloned.1.call-update) | async-done | bytes 102416 | tf_op jit(solution)/shard_map/reduce_scatter | solution.py:220
  696.2 1.6 bitcast_convert_fusion
  (48 shorter events, 0.2 us)
Async XLA Ops:
  7.2 35.4 %copy-start = (bf16[1,2560,640]{2,1,0:T(8,128)(2,1)S(1)}, bf16[1,2560,640]{2,1,0:T(8,128)(2,1)}, u32[]{:S(2)}) copy-start(bf16[1,2560,640]{2,1,0:T(8,128)(2,1)} %param.6) | copy-start | bytes 9830404
  7.2 33.7 %all-gather.3.cloned.1.call-start = ((), (), s32[]{:S(2)}) async-start(), calls=%async_computation.5 | async-start | bytes 1638400 | tf_op jit(solution)/shard_map/while/body/eval_jaxpr/all_gather | solution.py:127
  46.0 0.7 copy-start.11
  52.4 9.8 %copy-start.14 = (bf16[1,1,128,640]{3,2,1,0:T(8,128)(2,1)S(1)}, bf16[1,1,128,640]{3,2,1,0:T(8,128)(2,1)}, u32[]{:S(2)}) copy-start(bf16[1,1,128,640]{3,2,1,0:T(8,128)(2,1)} %param.9) | copy-start | bytes 491524
  52.4 10.1 %copy-start.15 = (s32[1,1,32]{2,1,0:T(1,128)S(1)}, s32[1,1,32]{2,1,0:T(1,128)}, u32[]{:S(2)}) copy-start(s32[1,1,32]{2,1,0:T(1,128)} %param.7) | copy-start | bytes 388
  52.4 124.0 %all-to-all-start = ((bf16[32,1,128,640]{3,2,1,0:T(8,128)(2,1)}), bf16[32,1,128,640]{3,2,1,0:T(8,128)(2,1)}, u32[]{:S(2)}, u32[]{:S(2)}) async-start(bf16[32,1,128,640]{3,2,1,0:T(8,128)(2,1)} %copy.27), calls=%async_computation | async-start | bytes 10485760 | tf_op jit(solution)/shard_map/while/body/eval_jaxpr/all_to_all | solution.py:74
  176.5 123.1 %all-to-all-start.1 = ((bf16[32,1,128,640]{3,2,1,0:T(8,128)(2,1)}), bf16[32,1,128,640]{3,2,1,0:T(8,128)(2,1)}, u32[]{:S(2)}, u32[]{:S(2)}) async-start(bf16[32,1,128,640]{3,2,1,0:T(8,128)(2,1)} %copy.31), calls=%async_computation.1 | async-start | bytes 10485760 | tf_op jit(solution)/shard_map/all_to_all | solution.py:74
  185.5 120.9 %all-gather.5.cloned.1.call-start = ((), (), s32[]{:S(2)}) async-start(), calls=%async_computation.6 | async-start | bytes 1638400 | tf_op jit(solution)/shard_map/all_gather | solution.py:127
  185.8 10.6 %copy-start.4 = (bf16[1,1,128,640]{3,2,1,0:T(8,128)(2,1)S(1)}, bf16[1,1,128,640]{3,2,1,0:T(8,128)(2,1)}, u32[]{:S(2)}) copy-start(bf16[1,1,128,640]{3,2,1,0:T(8,128)(2,1)} %param.5) | copy-start | bytes 491524
  185.9 11.5 %copy-start.16 = (s32[1,32]{1,0:T(1,128)S(1)}, s32[1,32]{1,0:T(1,128)}, u32[]{:S(2)}) copy-start(s32[1,32]{1,0:T(1,128)} %param.8) | copy-start | bytes 388
  192.0 3.8 collective-permute-start
  195.8 0.7 copy-start.5
  197.3 153.2 %reduce-scatter.7.cloned.1.call-start = ((), (), s32[]{:S(2)}) async-start(), calls=%async_computation.8 | async-start | bytes 1638400
  312.2 0.7 copy-start.12
  318.7 1.4 copy-start.17
  318.7 33.7 %copy-start.6 = (bf16[2,128,640]{2,1,0:T(8,128)(2,1)S(1)}, bf16[2,128,640]{2,1,0:T(8,128)(2,1)}, u32[]{:S(2)}) copy-start(bf16[2,128,640]{2,1,0:T(8,128)(2,1)} %copy-done.5) | copy-start | bytes 983044
  318.7 33.7 %copy-start.7 = (bf16[2,128,640]{2,1,0:T(8,128)(2,1)S(1)}, bf16[2,128,640]{2,1,0:T(8,128)(2,1)}, u32[]{:S(2)}) copy-start(bf16[2,128,640]{2,1,0:T(8,128)(2,1)} %get-tuple-element.64) | copy-start | bytes 983044
  358.5 123.9 %all-to-all-start.2 = ((bf16[32,1,128,640]{3,2,1,0:T(8,128)(2,1)}), bf16[32,1,128,640]{3,2,1,0:T(8,128)(2,1)}, u32[]{:S(2)}, u32[]{:S(2)}) async-start(bf16[32,1,128,640]{3,2,1,0:T(8,128)(2,1)} %copy.36), calls=%async_computation.2 | async-start | bytes 10485760 | tf_op jit(solution)/shard_map/while/body/eval_jaxpr/all_to_all | solution.py:74
  368.1 328.1 %reduce-scatter.5.cloned.1.call-start = ((), (), s32[]{:S(2)}) async-start(), calls=%async_computation.7 | async-start | bytes 3379200 | tf_op jit(solution)/shard_map/reduce_scatter | solution.py:220
  482.4 11.8 %copy-start.2 = (bf16[2,128,2560]{2,1,0:T(8,128)(2,1)S(1)}, bf16[2,128,2560]{2,1,0:T(8,128)(2,1)}, u32[]{:S(2)}) copy-start(bf16[2,128,2560]{2,1,0:T(8,128)(2,1)} %all-gather.3.cloned.1.call-done) | copy-start | bytes 3932164
  482.4 11.8 %copy-start.3 = (bf16[2,128,2560]{2,1,0:T(8,128)(2,1)S(1)}, bf16[2,128,2560]{2,1,0:T(8,128)(2,1)}, u32[]{:S(2)}) copy-start(bf16[2,128,2560]{2,1,0:T(8,128)(2,1)} %all-gather.5.cloned.1.call-done) | copy-start | bytes 3932164
  482.4 11.8 %copy-start.13 = (bf16[2,128,640]{2,1,0:T(8,128)(2,1)S(1)}, bf16[2,128,640]{2,1,0:T(8,128)(2,1)}, u32[]{:S(2)}) copy-start(bf16[2,128,640]{2,1,0:T(8,128)(2,1)} %copy-done.12) | copy-start | bytes 983044
  488.7 7.1 %copy-start.8 = (bf16[2,128,640]{2,1,0:T(8,128)(2,1)S(1)}, bf16[2,128,640]{2,1,0:T(8,128)(2,1)}, u32[]{:S(2)}) copy-start(bf16[2,128,640]{2,1,0:T(8,128)(2,1)} %get-tuple-element.64) | copy-start | bytes 983044
  488.7 7.1 %copy-start.9 = (f32[2,128,640]{2,1,0:T(8,128)S(1)}, f32[2,128,640]{2,1,0:T(8,128)}, u32[]{:S(2)}) copy-start(f32[2,128,640]{2,1,0:T(8,128)} %get-tuple-element.115) | copy-start | bytes 1966084
  488.7 7.1 %copy-start.10 = (f32[2,128,640]{2,1,0:T(8,128)S(1)}, f32[2,128,640]{2,1,0:T(8,128)}, u32[]{:S(2)}) copy-start(f32[2,128,640]{2,1,0:T(8,128)} %get-tuple-element.116) | copy-start | bytes 1966084
  488.7 7.0 %collective-permute-start.1 = (bf16[2,128,640]{2,1,0:T(8,128)(2,1)S(1)}, bf16[2,128,640]{2,1,0:T(8,128)(2,1)S(1)}, u32[]{:S(2)}, u32[]{:S(2)}) collective-permute-start(bf16[2,128,640]{2,1,0:T(8,128)(2,1)S(1)} %copy.67), channel_id=1, source_target_pairs={{128,0},{129,1},{130,2},{131,3},{132,4},{133,5},{134,6},{135,7},{1... | collective-permute-start | bytes 983048 | tf_op jit(solution)/shard_map/while/body/eval_jaxpr/ppermute | solution.py:19
  495.8 202.1 %copy-start.1 = (bf16[1,2560,640]{2,1,0:T(8,128)(2,1)S(1)}, bf16[1,2560,640]{2,1,0:T(8,128)(2,1)}, u32[]{:S(2)}) copy-start(bf16[1,2560,640]{2,1,0:T(8,128)(2,1)} %param.6) | copy-start | bytes 9830404
Sparse Core Ops, SparseCore 0:
  10.4 30.4 all-gather.2
  197.4 27.1 all-gather.4
  320.1 30.2 reduce-scatter.6
  499.7 196.5 reduce-scatter.4
where the time goes:
time: 708 us; the launch traced here: 704 us
  waiting for transfers between devices  574 us (81%)
  matrix products  38.9 us (5%)
  starting transfers between devices  35.6 us (5%)
  local copies, waits for them, and re-layouts  22.2 us (3%)
  between operations  14.2 us (2%)
  other arithmetic  10.9 us (2%)
  blocking collectives  8.76 us (1%)
    all_to_all x3, waiting for transfers between devices, regroup(): lax.all_to_all(outgoing, 'rep', split_axis=0, concat_axis=0, tiled=True)  324 us
    reduce_scatter x1, waiting for transfers between devices, on_device(): lax.psum_scatter(grad_total.astype(jnp.bfloat16), 'rep', scatter_dimensio...  197 us
    all_gather x2, waiting for transfers between devices, forward_block(): gathered = lax.all_gather(current, 'tp', axis=2, tiled=True)  29.9 us
    all_to_all x3, starting transfers between devices, regroup(): lax.all_to_all(outgoing, 'rep', split_axis=0, concat_axis=0, tiled=True)  28.5 us
    unnamed x5, waiting for transfers between devices  20.4 us
    dot_general x3, matrix products, regroup(): jnp.einsum('wcq,qwtf->wctf', come_map, incoming, preferred_element_type=j...  19.1 us
  transfers between devices with their start and end apart: 9, of which 7 were waited for; matrix products, arithmetic and copies ran while one was open for 4% of the time, Pallas kernels for 0%

commit v1 on v0

v1 whole, which is shorter than its diff:
```python
import functools
import math

import jax
import jax.numpy as jnp
from jax import lax
from jax.experimental import pallas as pl
from jax.experimental.pallas import tpu as pltpu
from jax.sharding import PartitionSpec as P

WCAP = 2
EPS = 1e-06
ROOT_HALF = 0.7071067811865476
NORMAL_PEAK = 0.3989422804014327
VMEM_LIMIT = 24 * 1024 * 1024
VM = pl.BlockSpec(memory_space=pltpu.VMEM)
SM = pl.BlockSpec(memory_space=pltpu.SMEM)
ANY = pl.BlockSpec(memory_space=pl.ANY)
BF = jnp.bfloat16
F32 = jnp.float32


def gelu_value(v):
    return 0.5 * v * (1.0 + lax.erf(v * ROOT_HALF))


def gelu_slope(v):
    return 0.5 * (1.0 + lax.erf(v * ROOT_HALF)) + v * jnp.exp(-0.5 * v * v) * NORMAL_PEAK


def call(body, out_shape, in_specs, name, scratch=(), flops=0, nbytes=0):
    many = isinstance(out_shape, (tuple, list))
    return pl.pallas_call(
        body,
        out_shape=out_shape,
        in_specs=in_specs,
        out_specs=tuple(VM for _ in out_shape) if many else VM,
        scratch_shapes=scratch,
        name=name,
        compiler_params=pltpu.CompilerParams(vmem_limit_bytes=VMEM_LIMIT),
        cost_estimate=pl.CostEstimate(flops=flops, bytes_accessed=nbytes, transcendentals=0),
    )


def rows_scale(blocks, feat):
    total = None
    for block in blocks:
        wide = block.astype(F32)
        part = jnp.sum(wide * wide, axis=-1, keepdims=True)
        total = part if total is None else total + part
    return lax.rsqrt(total / feat + EPS)


def rows_product(refs, w_ref, tp_pos, tp_count):
    width = refs[0].shape[-1]
    total = None
    for k, ref in enumerate(refs):
        start = pl.multiple_of(lax.rem(tp_pos + tp_count - k, tp_count) * width, width)
        part = jnp.dot(ref[...], w_ref[pl.ds(start, width), :], preferred_element_type=F32)
        total = part if total is None else total + part
    return total


def first_kernel(tp_count, feat, info, *refs):
    blocks, (w_ref, x1_ref, mixed_ref, scale_ref) = refs[:tp_count], refs[tp_count:]

    @pl.when(info[0] == 0)
    def _():
        scale = rows_scale([b[...] for b in blocks], feat)
        mixed = rows_product(blocks, w_ref, info[2], tp_count) * scale
        x1_ref[...] = (blocks[0][...].astype(F32) + gelu_value(mixed)).astype(BF)
        mixed_ref[...] = mixed
        scale_ref[...] = jnp.broadcast_to(scale, scale_ref.shape)


def second_kernel(tp_count, feat, loss_scale, info, lengths, *refs):
    blocks = refs[:tp_count]
    w_ref, goal_ref, x2_ref, delta_ref = refs[tp_count : tp_count + 4]
    back_refs = refs[tp_count + 4 :]

    @pl.when(info[0] == 1)
    def _():
        tp_pos = info[2]
        tokens, width = blocks[0].shape
        scale = rows_scale([b[...] for b in blocks], feat)
        mixed = rows_product(blocks, w_ref, tp_pos, tp_count) * scale
        x2 = (blocks[0][...].astype(F32) + gelu_value(mixed)).astype(BF)
        x2_ref[...] = x2
        token_ids = lax.broadcasted_iota(jnp.int32, (tokens, 1), 0)
        valid = jnp.where(token_ids < lengths[0, info[1]], loss_scale, 0.0)
        grad = ((x2.astype(F32) - goal_ref[...].astype(F32)) * valid).astype(BF)
        delta = (grad.astype(F32) * gelu_slope(mixed)).astype(BF)
        wide_delta = delta.astype(F32)
        stat = jnp.sum(mixed * wide_delta, axis=-1, keepdims=True) / feat
        delta_ref[...] = (wide_delta * scale).astype(BF)
        for k in range(tp_count):
            start = pl.multiple_of(lax.rem(tp_pos + tp_count - k, tp_count) * width, width)
            back = lax.dot_general(
                delta,
                w_ref[pl.ds(start, width), :],
                (((1,), (1,)), ((), ())),
                preferred_element_type=F32,
            )
            row = scale * (back - blocks[k][...].astype(F32) * (scale * stat))
            if k == 0:
                row = row + grad.astype(F32)
            back_refs[k][...] = row.astype(BF)


def turn_kernel(tp_count, x_count, z_count, info, *refs):
    first = refs[:tp_count]
    second = refs[tp_count : 2 * tp_count]
    mixed_ref, scale_ref, _ = refs[2 * tp_count : 2 * tp_count + 3]
    outs = refs[2 * tp_count + 3 : 2 * tp_count + 3 + x_count]
    slope_ref, turned = refs[2 * tp_count + 3 + x_count :]
    tp_pos = info[2]
    x_pos = lax.rem(info[1], x_count)
    rows = turned.shape[2]

    def put(blocks):
        for k in range(tp_count):
            source = lax.rem(tp_pos + tp_count - k, tp_count)
            flipped = blocks[k][...].T
            per = flipped.shape[0] // rows
            for i in range(per):
                place = source * (per // x_count) + i // x_count
                turned[i % x_count, place] = flipped[i * rows : (i + 1) * rows]

    @pl.when(info[0] == 0)
    def _():
        put(first)
        slope_ref[...] = gelu_slope(mixed_ref[...]) * scale_ref[:, :1]

    @pl.when(info[0] == 1)
    def _():
        put(second)

    for k in range(x_count):
        outs[k][...] = turned[lax.rem(x_pos + k, x_count)].reshape(outs[k].shape)


def delta_kernel(tp_count, info, *refs):
    back, (slope_ref, other_ref, out_ref) = refs[:tp_count], refs[tp_count:]

    @pl.when(info[0] == 0)
    def _():
        grad = back[0][...].astype(F32)
        for ref in back[1:]:
            grad = grad + ref[...].astype(F32)
        grad = grad.astype(BF).astype(F32)
        out_ref[...] = (grad * slope_ref[...]).astype(BF)

    @pl.when(info[0] != 0)
    def _():
        out_ref[...] = other_ref[...]


def part_kernel(x_count, z_count, info, *refs):
    turned, deltas = refs[:x_count], refs[x_count : 2 * x_count]
    outs = refs[2 * x_count : 2 * x_count + z_count]
    parts = refs[-1]
    left = jnp.concatenate([t[...] for t in turned], axis=1)
    right = jnp.concatenate([d[...] for d in deltas], axis=0)
    part = jnp.dot(left, right, preferred_element_type=F32).astype(BF)
    parts[...] = part.reshape(parts.shape)
    z_pos = info[1] // x_count
    for k in range(z_count):
        outs[k][...] = parts[lax.rem(z_pos + k, z_count)]


def sum_kernel(*refs):
    total = refs[0][...].astype(F32)
    for ref in refs[1:-1]:
        total = total + ref[...].astype(F32)
    refs[-1][...] = total


def make_table(wiring, table, counts, replicas):
    @pl.loop(0, replicas)
    def _(r):
        counts[r] = 0
        for c in range(WCAP):
            table[r * WCAP + c] = -1

    @pl.loop(0, replicas)
    def _(j):
        r = wiring[0, 0, j]
        table[r * WCAP + counts[r]] = j
        counts[r] = counts[r] + 1


def route_kernel(x_count, z_count, info, wiring, *refs):
    items = refs[:z_count]
    outs = refs[z_count : z_count + x_count]
    table, counts = refs[z_count + x_count :]

    @pl.when(info[0] == 1)
    def _():
        make_table(wiring, table, counts, x_count * z_count)
        x_pos = lax.rem(info[1], x_count)
        z_pos = info[1] // x_count
        for k in range(x_count):
            target = z_pos * x_count + lax.rem(x_pos + k, x_count)
            for c in range(WCAP):
                j = table[target * WCAP + c]
                here = (j >= 0) & (lax.rem(j, x_count) == x_pos)
                steps = lax.rem(z_pos + z_count - j // x_count, z_count)
                for m in range(z_count):

                    @pl.when(here & (steps == m))
                    def _(k=k, c=c, m=m):
                        outs[k][c] = items[m][...]


def place_kernel(x_count, z_count, info, wiring, x1_ref, *refs):
    slots = refs[:x_count]
    out_ref, table, counts = refs[x_count:]

    @pl.when(info[0] == 0)
    def _():
        out_ref[0] = x1_ref[...]
        for c in range(1, WCAP):
            out_ref[c] = jnp.zeros_like(x1_ref)

    @pl.when(info[0] == 1)
    def _():
        make_table(wiring, table, counts, x_count * z_count)
        x_pos = lax.rem(info[1], x_count)
        for c in range(WCAP):
            j = table[info[1] * WCAP + c]

            @pl.when(j < 0)
            def _(c=c):
                out_ref[c] = jnp.zeros_like(x1_ref)

            steps = lax.rem(x_pos + x_count - lax.rem(j, x_count), x_count)
            for k in range(x_count):

                @pl.when((j >= 0) & (steps == k))
                def _(c=c, k=k):
                    out_ref[c] = slots[k][c]


def on_device(x_count, z_count, inputs, weights, wiring, lengths, targets):
    replicas = lax.axis_size("rep")
    tp_count = lax.axis_size("tp")
    section = lax.axis_index("section")
    rep = lax.axis_index("rep")
    tp = lax.axis_index("tp")
    info = jnp.stack([section, rep, tp]).astype(jnp.int32)
    _, _, tokens, width = inputs.shape
    weight = weights[0]
    feat = weight.shape[0]
    x0 = inputs.reshape(tokens, width)
    goal = targets.reshape(tokens, width)
    rows = feat // replicas
    loss_scale = 1.0 / math.sqrt(replicas * tokens)
    like = jax.ShapeDtypeStruct((tokens, width), BF)
    wide = jax.ShapeDtypeStruct((tokens, width), F32)

    def tp_move(value, k, source, target):
        pairs = [
            (source * tp_count + y, target * tp_count + (y + k) % tp_count)
            for y in range(tp_count)
        ]
        return lax.ppermute(value, ("section", "tp"), pairs)

    def x_pairs(k):
        return [
            (z * x_count + x, z * x_count + (x + k) % x_count)
            for z in range(z_count)
            for x in range(x_count)
        ]

    def z_pairs(k):
        return [
            (z * x_count + x, ((z + k) % z_count) * x_count + x)
            for z in range(z_count)
            for x in range(x_count)
        ]

    def rep_move(value, pairs):
        return lax.ppermute(value, "rep", pairs)

    def rep_move_last(value, pairs):
        pairs = [(replicas + a, replicas + b) for a, b in pairs]
        return lax.ppermute(value, ("section", "rep"), pairs)

    flops = 2 * tokens * feat * width
    first_blocks = [x0] + [tp_move(x0, k, 0, 0) for k in range(1, tp_count)]
    x1, mixed, scale = call(
        functools.partial(first_kernel, tp_count, feat),
        (like, wide, jax.ShapeDtypeStruct((tokens, 128), F32)),
        [SM] + [VM] * (tp_count + 1),
        "first",
        flops=flops,
        nbytes=2 * feat * width,
    )(info, *first_blocks, weight)
    second_blocks = [tp_move(x1, k, 0, 1) for k in range(tp_count)]
    x2, delta1, *back = call(
        functools.partial(second_kernel, tp_count, feat, loss_scale),
        (like,) * (2 + tp_count),
        [SM, SM] + [VM] * (tp_count + 2),
        "second",
        flops=2 * flops,
        nbytes=2 * feat * width,
    )(info, lengths, *second_blocks, weight, goal)
    back_blocks = [tp_move(back[k], (tp_count - k) % tp_count, 1, 0) for k in range(tp_count)]
    flat = jax.ShapeDtypeStruct((feat // x_count, tokens), BF)
    *turned, slope = call(
        functools.partial(turn_kernel, tp_count, x_count, z_count),
        (flat,) * x_count + (wide,),
        [SM] + [VM] * (2 * tp_count + 2) + [ANY],
        "turn",
        scratch=[pltpu.VMEM((x_count, z_count, rows, tokens), BF)],
        flops=flops // 8,
        nbytes=2 * feat * tokens,
    )(info, *first_blocks, *second_blocks, mixed, scale, delta1)
    lefts = [turned[0]] + [rep_move(turned[k], x_pairs(k)) for k in range(1, x_count)]
    delta = call(
        functools.partial(delta_kernel, tp_count),
        like,
        [SM] + [VM] * (tp_count + 2),
        "delta",
        flops=tokens * width,
        nbytes=8 * tokens * width,
    )(info, *back_blocks, slope, delta1)
    rights = [delta] + [rep_move(delta, x_pairs(k)) for k in range(1, x_count)]
    chunk = jax.ShapeDtypeStruct((rows, width), BF)
    parts = call(
        functools.partial(part_kernel, x_count, z_count),
        (chunk,) * z_count,
        [SM] + [VM] * (2 * x_count),
        "part",
        scratch=[pltpu.VMEM((z_count, rows, width), BF)],
        flops=flops,
        nbytes=4 * feat * tokens,
    )(info, *lefts, *rights)
    sums = [parts[0]] + [rep_move(parts[k], z_pairs(k)) for k in range(1, z_count)]
    grad_rows = call(
        sum_kernel,
        jax.ShapeDtypeStruct((rows, width), F32),
        [VM] * z_count,
        "sum",
        flops=z_count * rows * width,
        nbytes=2 * z_count * rows * width,
    )(*sums)
    items = [x2] + [rep_move_last(x2, z_pairs(k)) for k in range(1, z_count)]
    pair = jax.ShapeDtypeStruct((WCAP, tokens, width), BF)
    tables = [pltpu.SMEM((replicas * WCAP,), jnp.int32), pltpu.SMEM((replicas,), jnp.int32)]
    slots = call(
        functools.partial(route_kernel, x_count, z_count),
        (pair,) * x_count,
        [SM, SM] + [VM] * z_count,
        "route",
        scratch=tables,
        nbytes=2 * z_count * tokens * width,
    )(info, wiring, *items)
    arrived = [slots[0]] + [rep_move_last(slots[k], x_pairs(k)) for k in range(1, x_count)]
    acts = call(
        functools.partial(place_kernel, x_count, z_count),
        pair,
        [SM, SM] + [VM] * (x_count + 1),
        "place",
        scratch=tables,
        nbytes=2 * z_count * tokens * width,
    )(info, wiring, x1, *arrived)
    return (
        acts.reshape(1, 1, 1, WCAP, tokens, width),
        grad_rows.reshape(1, rows, width),
    )


def solution(mesh):
    in_specs = (
        P(None, "rep", None, "tp"),
        P("section", None, "tp"),
        P(),
        P(),
        P(None, "rep", None, "tp"),
    )
    out_specs = (P("section", None, "rep", None, None, "tp"), P("section", "rep", "tp"))
    x_count = 4
    z_count = mesh.shape["rep"] // x_count
    return jax.shard_map(
        functools.partial(on_device, x_count, z_count),
        mesh=mesh,
        in_specs=in_specs,
        out_specs=out_specs,
        check_vma=False,
    )
```

time: 708 us -> 127 us (0.18)
  waiting for transfers between devices: 574 us -> 39.5 us
  matrix products: 38.9 us -> 0 us
  starting transfers between devices: 35.6 us -> 72.4 us
  local copies, waits for them, and re-layouts: 22.2 us -> 2.85 us
  between operations: 14.2 us -> 0.98 us
  other arithmetic: 10.9 us -> 0.08 us
  Pallas kernels: 0 us -> 10.3 us
  blocking collectives: 8.76 us -> 0 us
    all_to_all x3 -> x0, waiting for transfers between devices: 324 us -> none  [regroup(): lax.all_to_all(outgoing, 'rep', split_axis=0, concat_axis=0, tiled=True)]
    reduce_scatter x1 -> x0, waiting for transfers between devices: 197 us -> none  [on_device(): lax.psum_scatter(grad_total.astype(jnp.bfloat16), 'rep', scatter_dimensio...]
    ppermute x2 -> x34, starting transfers between devices: 6.79 us -> 72.4 us  [the longest x10 39.6 us: rep_move_last(): return lax.ppermute(value, ('section', 'rep'), pairs)]
    dot_general x11 -> x0, matrix products: 38.9 us -> none  [the longest x3 19.1 us: regroup(): jnp.einsum('wcq,qwtf->wctf', come_map, incoming, preferred_element_type=j...]
    ppermute x2 -> x34, waiting for transfers between devices: 2.47 us -> 39.5 us  [the longest x11 19.6 us: tp_move(): return lax.ppermute(value, ('section', 'tp'), pairs)]
    all_gather x2 -> x0, waiting for transfers between devices: 29.9 us -> none  [forward_block(): gathered = lax.all_gather(current, 'tp', axis=2, tiled=True)]
    all_to_all x3 -> x0, starting transfers between devices: 28.5 us -> none  [regroup(): lax.all_to_all(outgoing, 'rep', split_axis=0, concat_axis=0, tiled=True)]
    unnamed x5 -> x0, waiting for transfers between devices: 20.4 us -> none
  transfers between devices with their start and end apart: 9 -> 34, of which waited for: 7 -> 11; matrix products, arithmetic and copies ran while one was open for 4% -> 0% of each run, Pallas kernels for 0% -> 4%
where the time goes in v1:
time: 127 us; the launch traced here: 126 us
  starting transfers between devices  72.4 us (57%)
  waiting for transfers between devices  39.5 us (31%)
  Pallas kernels  10.3 us (8%)
  local copies, waits for them, and re-layouts  2.85 us (2%)
    ppermute x10, starting transfers between devices, rep_move_last(): return lax.ppermute(value, ('section', 'rep'), pairs)  39.6 us
    ppermute x13, starting transfers between devices, rep_move(): return lax.ppermute(value, 'rep', pairs)  20.3 us
    ppermute x11, waiting for transfers between devices, tp_move(): return lax.ppermute(value, ('section', 'tp'), pairs)  19.6 us
    ppermute x11, starting transfers between devices, tp_move(): return lax.ppermute(value, ('section', 'tp'), pairs)  12.5 us
    ppermute x10, waiting for transfers between devices, rep_move_last(): return lax.ppermute(value, ('section', 'rep'), pairs)  11.2 us
    ppermute x13, waiting for transfers between devices, rep_move(): return lax.ppermute(value, 'rep', pairs)  8.71 us
    unnamed x12, local copies, waits for them, and re-layouts  2.85 us
    pallas_call x1, Pallas kernels, on_device(): call(functools.partial(second_kernel, tp_count, feat, loss_scale), (like,...  2.57 us
  transfers between devices with their start and end apart: 34, of which 11 were waited for; matrix products, arithmetic and copies ran while one was open for 0% of the time, Pallas kernels for 4%

profile of v1, /device:TPU:1, one launch (start us, length us, event | category | flops | bytes accessed | tf_op | source)
XLA Modules:
  0.0 126.2 jit_solution(7700721583347679604)
XLA Ops:
  0.6 0.7 collective-permute-start.2
  1.3 0.7 collective-permute-start.1
  2.0 0.7 collective-permute-start
  2.7 0.1 pad_add_fusion.info
  2.8 0.0 collective-permute-done.2.refs_3_
  2.8 0.0 collective-permute-done.1.refs_2_
  2.8 0.0 collective-permute-done.refs_1_
  2.8 0.0 copy-start
  2.8 1.9 %copy-done = bf16[1,2560,640]{2,1,0:T(8,128)(2,1)S(1)} copy-done((bf16[1,2560,640]{2,1,0:T(8,128)(2,1)S(1)}, bf16[1,2560,640]{2,1,0:T(8,128)(2,1)}, u32[]{:S(2)}) %copy-start) | copy-done | bytes 3276824
  4.7 0.9 copy-done.2
  5.6 0.5 first.1
  6.2 1.4 %collective-permute-start.6 = (bf16[128,640]{1,0:T(8,128)(2,1)S(1)}, bf16[128,640]{1,0:T(8,128)(2,1)S(1)}, u32[]{:S(2)}, u32[]{:S(2)}) collective-permute-start(bf16[128,640]{1,0:T(8,128)(2,1)S(1)} %get-tuple-element.28.x1_ref), channel_id=1, source_target_pairs={{0,131},{1,128},{2,129},{3,130},{4,135},{5,132},{6,133},{7,134},{8... | collective-permute-start | bytes 491528 | tf_op jit(solution)/shard_map/ppermute | solution.py:266
  7.6 1.3 %collective-permute-start.5 = (bf16[128,640]{1,0:T(8,128)(2,1)S(1)}, bf16[128,640]{1,0:T(8,128)(2,1)S(1)}, u32[]{:S(2)}, u32[]{:S(2)}) collective-permute-start(bf16[128,640]{1,0:T(8,128)(2,1)S(1)} %get-tuple-element.28.x1_ref), channel_id=1, source_target_pairs={{0,130},{1,131},{2,128},{3,129},{4,134},{5,135},{6,132},{7,133},{8... | collective-permute-start | bytes 491528 | tf_op jit(solution)/shard_map/ppermute | solution.py:266
  8.9 1.3 %collective-permute-start.4 = (bf16[128,640]{1,0:T(8,128)(2,1)S(1)}, bf16[128,640]{1,0:T(8,128)(2,1)S(1)}, u32[]{:S(2)}, u32[]{:S(2)}) collective-permute-start(bf16[128,640]{1,0:T(8,128)(2,1)S(1)} %get-tuple-element.28.x1_ref), channel_id=1, source_target_pairs={{0,129},{1,130},{2,131},{3,128},{4,133},{5,134},{6,135},{7,132},{8... | collective-permute-start | bytes 491528 | tf_op jit(solution)/shard_map/ppermute | solution.py:266
  10.2 1.3 %collective-permute-start.3 = (bf16[128,640]{1,0:T(8,128)(2,1)S(1)}, bf16[128,640]{1,0:T(8,128)(2,1)S(1)}, u32[]{:S(2)}, u32[]{:S(2)}) collective-permute-start(bf16[128,640]{1,0:T(8,128)(2,1)S(1)} %get-tuple-element.28.x1_ref), channel_id=1, source_target_pairs={{0,128},{1,129},{2,130},{3,131},{4,132},{5,133},{6,134},{7,135},{8... | collective-permute-start | bytes 491528 | tf_op jit(solution)/shard_map/ppermute | solution.py:266
  11.5 14.6 %collective-permute-done.6.refs_3_.refs_7_ = bf16[128,640]{1,0:T(8,128)(2,1)S(1)} collective-permute-done((bf16[128,640]{1,0:T(8,128)(2,1)S(1)}, bf16[128,640]{1,0:T(8,128)(2,1)S(1)}, u32[]{:S(2)}, u32[]{:S(2)}) %collective-permute-start.6) | collective-permute-done | bytes 163872 | tf_op jit(solution)/shard_map/ppermute | solution.py:266
  26.1 3.3 %collective-permute-done.5.refs_2_.refs_6_ = bf16[128,640]{1,0:T(8,128)(2,1)S(1)} collective-permute-done((bf16[128,640]{1,0:T(8,128)(2,1)S(1)}, bf16[128,640]{1,0:T(8,128)(2,1)S(1)}, u32[]{:S(2)}, u32[]{:S(2)}) %collective-permute-start.5) | collective-permute-done | bytes 163872 | tf_op jit(solution)/shard_map/ppermute | solution.py:266
  29.4 1.7 %collective-permute-done.4.refs_1_.refs_5_ = bf16[128,640]{1,0:T(8,128)(2,1)S(1)} collective-permute-done((bf16[128,640]{1,0:T(8,128)(2,1)S(1)}, bf16[128,640]{1,0:T(8,128)(2,1)S(1)}, u32[]{:S(2)}, u32[]{:S(2)}) %collective-permute-start.4) | collective-permute-done | bytes 163872 | tf_op jit(solution)/shard_map/ppermute | solution.py:266
  31.2 2.6 %second.1 = (bf16[128,640]{1,0:T(8,128)(2,1)S(1)}, bf16[128,640]{1,0:T(8,128)(2,1)S(1)}, bf16[128,640]{1,0:T(8,128)(2,1)S(1)}, bf16[128,640]{1,0:T(8,128)(2,1)S(...) custom-call(s32[3]{0:T(128)S(1)} %pad_add_fusion.info, s32[1,32]{1,0:T(1,128)S(1)} %copy-done.5, ...), custom_call_target="tpu_custom_call" | custom-call | flops 838860800 | bytes 3276800 | tf_op jit(solution)/shard_map/second/pallas_call | solution.py:300
  33.7 0.0 copy-start.4
  33.7 1.3 %collective-permute-start.20 = (bf16[128,640]{1,0:T(8,128)(2,1)S(1)}, bf16[128,640]{1,0:T(8,128)(2,1)S(1)}, u32[]{:S(2)}, u32[]{:S(2)}) collective-permute-start(bf16[128,640]{1,0:T(8,128)(2,1)S(1)} %get-tuple-element.41), channel_id=1, source_target_pairs={{128,0},{129,1},{130,2},{131,3},{132,4},{133,5},{134,6},{135,7},{1... | collective-permute-start | bytes 491528 | tf_op jit(solution)/shard_map/ppermute | solution.py:266
  35.0 1.3 %collective-permute-start.21 = (bf16[128,640]{1,0:T(8,128)(2,1)S(1)}, bf16[128,640]{1,0:T(8,128)(2,1)S(1)}, u32[]{:S(2)}, u32[]{:S(2)}) collective-permute-start(bf16[128,640]{1,0:T(8,128)(2,1)S(1)} %get-tuple-element.42), channel_id=1, source_target_pairs={{128,3},{129,0},{130,1},{131,2},{132,7},{133,4},{134,5},{135,6},{1... | collective-permute-start | bytes 491528 | tf_op jit(solution)/shard_map/ppermute | solution.py:266
  36.4 1.3 %collective-permute-start.22 = (bf16[128,640]{1,0:T(8,128)(2,1)S(1)}, bf16[128,640]{1,0:T(8,128)(2,1)S(1)}, u32[]{:S(2)}, u32[]{:S(2)}) collective-permute-start(bf16[128,640]{1,0:T(8,128)(2,1)S(1)} %get-tuple-element.43), channel_id=1, source_target_pairs={{128,2},{129,3},{130,0},{131,1},{132,6},{133,7},{134,4},{135,5},{1... | collective-permute-start | bytes 491528 | tf_op jit(solution)/shard_map/ppermute | solution.py:266
  37.7 1.3 %collective-permute-start.23 = (bf16[128,640]{1,0:T(8,128)(2,1)S(1)}, bf16[128,640]{1,0:T(8,128)(2,1)S(1)}, u32[]{:S(2)}, u32[]{:S(2)}) collective-permute-start(bf16[128,640]{1,0:T(8,128)(2,1)S(1)} %get-tuple-element.44), channel_id=1, source_target_pairs={{128,1},{129,2},{130,3},{131,0},{132,5},{133,6},{134,7},{135,4},{1... | collective-permute-start | bytes 491528 | tf_op jit(solution)/shard_map/ppermute | solution.py:266
  39.0 0.8 turn.1
  39.8 1.1 collective-permute-start.17
  40.9 0.0 collective-permute-done.20.refs_0_
  40.9 2.4 %collective-permute-start.18 = (bf16[640,128]{1,0:T(8,128)(2,1)S(1)}, bf16[640,128]{1,0:T(8,128)(2,1)S(1)}, u32[]{:S(2)}, u32[]{:S(2)}) collective-permute-start(bf16[640,128]{1,0:T(8,128)(2,1)S(1)} %get-tuple-element.39), channel_id=1, source_target_pairs={{0,8},{4,12},{8,0},{12,4},{16,24},{20,28},{24,16},{28,20},{32,40},... | collective-permute-start | bytes 491528 | tf_op jit(solution)/shard_map/ppermute | solution.py:283
  43.4 1.2 collective-permute-start.19
  44.6 0.0 collective-permute-done.22.refs_2_
  44.6 7.5 %collective-permute-start.13 = (bf16[128,640]{1,0:T(8,128)(2,1)S(1)}, bf16[128,640]{1,0:T(8,128)(2,1)S(1)}, u32[]{:S(2)}, u32[]{:S(2)}) collective-permute-start(bf16[128,640]{1,0:T(8,128)(2,1)S(1)} %get-tuple-element.29.refs_0_), channel_id=1, source_target_pairs={{128,240},{132,244},{136,248},{140,252},{144,128},{148,132},{152,1... | collective-permute-start | bytes 491528 | tf_op jit(solution)/shard_map/ppermute | solution.py:287
  52.0 3.1 %collective-permute-start.12 = (bf16[128,640]{1,0:T(8,128)(2,1)S(1)}, bf16[128,640]{1,0:T(8,128)(2,1)S(1)}, u32[]{:S(2)}, u32[]{:S(2)}) collective-permute-start(bf16[128,640]{1,0:T(8,128)(2,1)S(1)} %get-tuple-element.29.refs_0_), channel_id=1, source_target_pairs={{128,224},{132,228},{136,232},{140,236},{144,240},{148,244},{152,2... | collective-permute-start | bytes 491528 | tf_op jit(solution)/shard_map/ppermute | solution.py:287
  55.1 0.6 delta.1.refs_4_
  55.7 0.0 collective-permute-done.17.refs_1_
  55.7 0.1 collective-permute-start.26
  55.8 2.1 %collective-permute-start.25 = (bf16[128,640]{1,0:T(8,128)(2,1)S(1)}, bf16[128,640]{1,0:T(8,128)(2,1)S(1)}, u32[]{:S(2)}, u32[]{:S(2)}) collective-permute-start(bf16[128,640]{1,0:T(8,128)(2,1)S(1)} %delta.1.refs_4_), channel_id=1, source_target_pairs={{0,8},{4,12},{8,0},{12,4},{16,24},{20,28},{24,16},{28,20},{32,40},... | collective-permute-start | bytes 491528 | tf_op jit(solution)/shard_map/ppermute | solution.py:283
  57.9 0.0 collective-permute-done.13.refs_7_
  57.9 2.4 %collective-permute-start.11 = (bf16[128,640]{1,0:T(8,128)(2,1)S(1)}, bf16[128,640]{1,0:T(8,128)(2,1)S(1)}, u32[]{:S(2)}, u32[]{:S(2)}) collective-permute-start(bf16[128,640]{1,0:T(8,128)(2,1)S(1)} %get-tuple-element.29.refs_0_), channel_id=1, source_target_pairs={{128,208},{132,212},{136,216},{140,220},{144,224},{148,228},{152,2... | collective-permute-start | bytes 491528 | tf_op jit(solution)/shard_map/ppermute | solution.py:287
  60.3 6.4 %collective-permute-start.10 = (bf16[128,640]{1,0:T(8,128)(2,1)S(1)}, bf16[128,640]{1,0:T(8,128)(2,1)S(1)}, u32[]{:S(2)}, u32[]{:S(2)}) collective-permute-start(bf16[128,640]{1,0:T(8,128)(2,1)S(1)} %get-tuple-element.29.refs_0_), channel_id=1, source_target_pairs={{128,192},{132,196},{136,200},{140,204},{144,208},{148,212},{152,2... | collective-permute-start | bytes 491528 | tf_op jit(solution)/shard_map/ppermute | solution.py:287
  66.7 2.8 %collective-permute-start.9 = (bf16[128,640]{1,0:T(8,128)(2,1)S(1)}, bf16[128,640]{1,0:T(8,128)(2,1)S(1)}, u32[]{:S(2)}, u32[]{:S(2)}) collective-permute-start(bf16[128,640]{1,0:T(8,128)(2,1)S(1)} %get-tuple-element.29.refs_0_), channel_id=1, source_target_pairs={{128,176},{132,180},{136,184},{140,188},{144,192},{148,196},{152,2... | collective-permute-start | bytes 491528 | tf_op jit(solution)/shard_map/ppermute | solution.py:287
  69.5 0.0 collective-permute-done.25.refs_6_
  69.5 3.1 %collective-permute-start.8 = (bf16[128,640]{1,0:T(8,128)(2,1)S(1)}, bf16[128,640]{1,0:T(8,128)(2,1)S(1)}, u32[]{:S(2)}, u32[]{:S(2)}) collective-permute-start(bf16[128,640]{1,0:T(8,128)(2,1)S(1)} %get-tuple-element.29.refs_0_), channel_id=1, source_target_pairs={{128,160},{132,164},{136,168},{140,172},{144,176},{148,180},{152,1... | collective-permute-start | bytes 491528 | tf_op jit(solution)/shard_map/ppermute | solution.py:287
  72.6 3.4 %collective-permute-start.7 = (bf16[128,640]{1,0:T(8,128)(2,1)S(1)}, bf16[128,640]{1,0:T(8,128)(2,1)S(1)}, u32[]{:S(2)}, u32[]{:S(2)}) collective-permute-start(bf16[128,640]{1,0:T(8,128)(2,1)S(1)} %get-tuple-element.29.refs_0_), channel_id=1, source_target_pairs={{128,144},{132,148},{136,152},{140,156},{144,160},{148,164},{152,1... | collective-permute-start | bytes 491528 | tf_op jit(solution)/shard_map/ppermute | solution.py:287
  76.0 1.3 %part.1 = (bf16[80,640]{1,0:T(8,128)(2,1)S(1)}, bf16[80,640]{1,0:T(8,128)(2,1)S(1)}, bf16[80,640]{1,0:T(8,128)(2,1)S(1)}, bf16[80,640]{1,0:T(8,128)(2,1)S(1)}, b...) custom-call(s32[3]{0:T(128)S(1)} %pad_add_fusion.info, ...), custom_call_target="tpu_custom_call" | custom-call | flops 419430400 | bytes 1310720 | tf_op jit(solution)/shard_map/part/pallas_call | solution.py:330
  77.3 0.8 collective-permute-start.27
  78.1 4.5 %collective-permute-done.9.refs_3_ = bf16[128,640]{1,0:T(8,128)(2,1)S(1)} collective-permute-done((bf16[128,640]{1,0:T(8,128)(2,1)S(1)}, bf16[128,640]{1,0:T(8,128)(2,1)S(1)}, u32[]{:S(2)}, u32[]{:S(2)}) %collective-permute-start.9) | collective-permute-done | bytes 163872 | tf_op jit(solution)/shard_map/ppermute | solution.py:287
  82.6 3.8 %collective-permute-done.8.refs_2_ = bf16[128,640]{1,0:T(8,128)(2,1)S(1)} collective-permute-done((bf16[128,640]{1,0:T(8,128)(2,1)S(1)}, bf16[128,640]{1,0:T(8,128)(2,1)S(1)}, u32[]{:S(2)}, u32[]{:S(2)}) %collective-permute-start.8) | collective-permute-done | bytes 163872 | tf_op jit(solution)/shard_map/ppermute | solution.py:287
  86.4 2.9 %collective-permute-done.7.refs_1_ = bf16[128,640]{1,0:T(8,128)(2,1)S(1)} collective-permute-done((bf16[128,640]{1,0:T(8,128)(2,1)S(1)}, bf16[128,640]{1,0:T(8,128)(2,1)S(1)}, u32[]{:S(2)}, u32[]{:S(2)}) %collective-permute-start.7) | collective-permute-done | bytes 163872 | tf_op jit(solution)/shard_map/ppermute | solution.py:287
  89.3 1.7 %route.1 = (bf16[2,128,640]{2,1,0:T(8,128)(2,1)S(1)}, bf16[2,128,640]{2,1,0:T(8,128)(2,1)S(1)}, bf16[2,128,640]{2,1,0:T(8,128)(2,1)S(1)}, bf16[2,128,640]{2,1,0:T(8,128)(2,1)S(1)}) custom-call(s32[3]{0:T(128)S(1)} %pad_add_fusion.info, s32[1,1,32]{2,1,0:T(1,128)S(1)} %copy-done.4, bf16[128,640]{1,0:T(8,128)(2,1)S(1)} %get-tuple-element.29.refs_0_, ...), custom_call_target="tpu_custom_call" | custom-call | bytes 1310720 | tf_op jit(solution)/shard_map/route/pallas_call | solution.py:351
  91.0 3.5 %collective-permute-start.14 = (bf16[2,128,640]{2,1,0:T(8,128)(2,1)S(1)}, bf16[2,128,640]{2,1,0:T(8,128)(2,1)S(1)}, u32[]{:S(2)}, u32[]{:S(2)}) collective-permute-start(bf16[2,128,640]{2,1,0:T(8,128)(2,1)S(1)} %get-tuple-element.31), channel_id=1, source_target_pairs={{128,132},{132,136},{136,140},{140,128},{144,148},{148,152},{152,1... | collective-permute-start | bytes 983048 | tf_op jit(solution)/shard_map/ppermute | solution.py:287
  94.5 4.0 %collective-permute-start.15 = (bf16[2,128,640]{2,1,0:T(8,128)(2,1)S(1)}, bf16[2,128,640]{2,1,0:T(8,128)(2,1)S(1)}, u32[]{:S(2)}, u32[]{:S(2)}) collective-permute-start(bf16[2,128,640]{2,1,0:T(8,128)(2,1)S(1)} %get-tuple-element.32), channel_id=1, source_target_pairs={{128,136},{132,140},{136,128},{140,132},{144,152},{148,156},{152,1... | collective-permute-start | bytes 983048 | tf_op jit(solution)/shard_map/ppermute | solution.py:287
  98.5 3.5 %collective-permute-start.16 = (bf16[2,128,640]{2,1,0:T(8,128)(2,1)S(1)}, bf16[2,128,640]{2,1,0:T(8,128)(2,1)S(1)}, u32[]{:S(2)}, u32[]{:S(2)}) collective-permute-start(bf16[2,128,640]{2,1,0:T(8,128)(2,1)S(1)} %get-tuple-element.33), channel_id=1, source_target_pairs={{128,140},{132,128},{136,132},{140,136},{144,156},{148,144},{152,1... | collective-permute-start | bytes 983048 | tf_op jit(solution)/shard_map/ppermute | solution.py:287
  102.0 2.6 %collective-permute-start.28 = (bf16[80,640]{1,0:T(8,128)(2,1)S(1)}, bf16[80,640]{1,0:T(8,128)(2,1)S(1)}, u32[]{:S(2)}, u32[]{:S(2)}) collective-permute-start(bf16[80,640]{1,0:T(8,128)(2,1)S(1)} %get-tuple-element.48), channel_id=1, source_target_pairs={{0,32},{4,36},{8,40},{12,44},{16,48},{20,52},{24,56},{28,60},{32,6... | collective-permute-start | bytes 307208 | tf_op jit(solution)/shard_map/ppermute | solution.py:283
  104.6 1.5 %collective-permute-start.29 = (bf16[80,640]{1,0:T(8,128)(2,1)S(1)}, bf16[80,640]{1,0:T(8,128)(2,1)S(1)}, u32[]{:S(2)}, u32[]{:S(2)}) collective-permute-start(bf16[80,640]{1,0:T(8,128)(2,1)S(1)} %get-tuple-element.49), channel_id=1, source_target_pairs={{0,48},{4,52},{8,56},{12,60},{16,64},{20,68},{24,72},{28,76},{32,8... | collective-permute-start | bytes 307208 | tf_op jit(solution)/shard_map/ppermute | solution.py:283
  106.2 2.6 %collective-permute-done.28.refs_2_ = bf16[80,640]{1,0:T(8,128)(2,1)S(1)} collective-permute-done((bf16[80,640]{1,0:T(8,128)(2,1)S(1)}, bf16[80,640]{1,0:T(8,128)(2,1)S(1)}, u32[]{:S(2)}, u32[]{:S(2)}) %collective-permute-start.28) | collective-permute-done | bytes 102432 | tf_op jit(solution)/shard_map/ppermute | solution.py:283
  108.7 4.4 %collective-permute-start.30 = (bf16[80,640]{1,0:T(8,128)(2,1)S(1)}, bf16[80,640]{1,0:T(8,128)(2,1)S(1)}, u32[]{:S(2)}, u32[]{:S(2)}) collective-permute-start(bf16[80,640]{1,0:T(8,128)(2,1)S(1)} %get-tuple-element.50), channel_id=1, source_target_pairs={{0,64},{4,68},{8,72},{12,76},{16,80},{20,84},{24,88},{28,92},{32,9... | collective-permute-start | bytes 307208 | tf_op jit(solution)/shard_map/ppermute | solution.py:283
  113.1 2.8 %collective-permute-start.31 = (bf16[80,640]{1,0:T(8,128)(2,1)S(1)}, bf16[80,640]{1,0:T(8,128)(2,1)S(1)}, u32[]{:S(2)}, u32[]{:S(2)}) collective-permute-start(bf16[80,640]{1,0:T(8,128)(2,1)S(1)} %get-tuple-element.51), channel_id=1, source_target_pairs={{0,80},{4,84},{8,88},{12,92},{16,96},{20,100},{24,104},{28,108},{3... | collective-permute-start | bytes 307208 | tf_op jit(solution)/shard_map/ppermute | solution.py:283
  115.9 1.9 %collective-permute-done.30.refs_4_ = bf16[80,640]{1,0:T(8,128)(2,1)S(1)} collective-permute-done((bf16[80,640]{1,0:T(8,128)(2,1)S(1)}, bf16[80,640]{1,0:T(8,128)(2,1)S(1)}, u32[]{:S(2)}, u32[]{:S(2)}) %collective-permute-start.30) | collective-permute-done | bytes 102432 | tf_op jit(solution)/shard_map/ppermute | solution.py:283
  117.8 0.6 collective-permute-done.31.refs_5_
  118.4 1.3 collective-permute-start.33
  119.7 3.0 %collective-permute-done.32.refs_6_ = bf16[80,640]{1,0:T(8,128)(2,1)S(1)} collective-permute-done((bf16[80,640]{1,0:T(8,128)(2,1)S(1)}, bf16[80,640]{1,0:T(8,128)(2,1)S(1)}, u32[]{:S(2)}, u32[]{:S(2)}) %collective-permute-start.32) | collective-permute-done | bytes 102432 | tf_op jit(solution)/shard_map/ppermute | solution.py:283
  122.7 0.6 collective-permute-done.33.refs_7_
  123.3 0.8 sum.1
  124.1 2.0 %place.1 = bf16[2,128,640]{2,1,0:T(8,128)(2,1)} custom-call(s32[3]{0:T(128)S(1)} %pad_add_fusion.info, s32[1,1,32]{2,1,0:T(1,128)S(1)} %copy-done.4, bf16[128,640]{1,0:T(8,128)(2,1)S(1)} %get-tuple-element.28.x1_ref, bf16[2,128,640]{2,1,0:T(8,128)(2,1)S(1)} %get-tuple-element.30.refs_0_, bf16[2,128,640]{2,1,0:T(8,128)(2,1)S(1)} %collective-permute-done.14.refs_1_, ...), custom_call_target="tpu_custom_call" | custom-call | bytes 1310720 | tf_op jit(solution)/shard_map/place/pallas_call | solution.py:360
  (25 shorter events, 0.1 us)
Async XLA Ops:
  0.6 30.5 %copy-start.5 = (s32[1,32]{1,0:T(1,128)S(1)}, s32[1,32]{1,0:T(1,128)}, u32[]{:S(2)}) copy-start(s32[1,32]{1,0:T(1,128)} %lengths.1) | copy-start | bytes 388
  0.6 2.1 %collective-permute-start.2 = (bf16[128,640]{1,0:T(8,128)(2,1)}, bf16[128,640]{1,0:T(8,128)(2,1)S(1)}, u32[]{:S(2)}, u32[]{:S(2)}) collective-permute-start(bf16[128,640]{1,0:T(8,128)(2,1)} %bitcast.10), channel_id=1, source_target_pairs={{0,3},{1,0},{2,1},{3,2},{4,7},{5,4},{6,5},{7,6},{8,11},{9,8},{10,9... | collective-permute-start | bytes 491528 | tf_op jit(solution)/shard_map/ppermute | solution.py:266
  1.3 1.4 %collective-permute-start.1 = (bf16[128,640]{1,0:T(8,128)(2,1)}, bf16[128,640]{1,0:T(8,128)(2,1)S(1)}, u32[]{:S(2)}, u32[]{:S(2)}) collective-permute-start(bf16[128,640]{1,0:T(8,128)(2,1)} %bitcast.11), channel_id=1, source_target_pairs={{0,2},{1,3},{2,0},{3,1},{4,6},{5,7},{6,4},{7,5},{8,10},{9,11},{10,... | collective-permute-start | bytes 491528 | tf_op jit(solution)/shard_map/ppermute | solution.py:266
  2.0 0.8 collective-permute-start
  2.8 1.9 %copy-start = (bf16[1,2560,640]{2,1,0:T(8,128)(2,1)S(1)}, bf16[1,2560,640]{2,1,0:T(8,128)(2,1)}, u32[]{:S(2)}) copy-start(bf16[1,2560,640]{2,1,0:T(8,128)(2,1)} %param.6) | copy-start | bytes 9830404
  4.7 0.9 copy-start.2
  5.6 25.5 %copy-start.1 = (bf16[1,2560,640]{2,1,0:T(8,128)(2,1)S(1)}, bf16[1,2560,640]{2,1,0:T(8,128)(2,1)}, u32[]{:S(2)}) copy-start(bf16[1,2560,640]{2,1,0:T(8,128)(2,1)} %param.6) | copy-start | bytes 9830404
  5.6 25.5 %copy-start.3 = (bf16[1,1,128,640]{3,2,1,0:T(8,128)(2,1)S(1)}, bf16[1,1,128,640]{3,2,1,0:T(8,128)(2,1)}, u32[]{:S(2)}) copy-start(bf16[1,1,128,640]{3,2,1,0:T(8,128)(2,1)} %param.9) | copy-start | bytes 491524
  6.2 20.0 %collective-permute-start.6 = (bf16[128,640]{1,0:T(8,128)(2,1)S(1)}, bf16[128,640]{1,0:T(8,128)(2,1)S(1)}, u32[]{:S(2)}, u32[]{:S(2)}) collective-permute-start(bf16[128,640]{1,0:T(8,128)(2,1)S(1)} %get-tuple-element.28.x1_ref), channel_id=1, source_target_pairs={{0,131},{1,128},{2,129},{3,130},{4,135},{5,132},{6,133},{7,134},{8... | collective-permute-start | bytes 491528 | tf_op jit(solution)/shard_map/ppermute | solution.py:266
  7.6 21.8 %collective-permute-start.5 = (bf16[128,640]{1,0:T(8,128)(2,1)S(1)}, bf16[128,640]{1,0:T(8,128)(2,1)S(1)}, u32[]{:S(2)}, u32[]{:S(2)}) collective-permute-start(bf16[128,640]{1,0:T(8,128)(2,1)S(1)} %get-tuple-element.28.x1_ref), channel_id=1, source_target_pairs={{0,130},{1,131},{2,128},{3,129},{4,134},{5,135},{6,132},{7,133},{8... | collective-permute-start | bytes 491528 | tf_op jit(solution)/shard_map/ppermute | solution.py:266
  8.9 22.2 %collective-permute-start.4 = (bf16[128,640]{1,0:T(8,128)(2,1)S(1)}, bf16[128,640]{1,0:T(8,128)(2,1)S(1)}, u32[]{:S(2)}, u32[]{:S(2)}) collective-permute-start(bf16[128,640]{1,0:T(8,128)(2,1)S(1)} %get-tuple-element.28.x1_ref), channel_id=1, source_target_pairs={{0,129},{1,130},{2,131},{3,128},{4,133},{5,134},{6,135},{7,132},{8... | collective-permute-start | bytes 491528 | tf_op jit(solution)/shard_map/ppermute | solution.py:266
  10.2 20.9 %collective-permute-start.3 = (bf16[128,640]{1,0:T(8,128)(2,1)S(1)}, bf16[128,640]{1,0:T(8,128)(2,1)S(1)}, u32[]{:S(2)}, u32[]{:S(2)}) collective-permute-start(bf16[128,640]{1,0:T(8,128)(2,1)S(1)} %get-tuple-element.28.x1_ref), channel_id=1, source_target_pairs={{0,128},{1,129},{2,130},{3,131},{4,132},{5,133},{6,134},{7,135},{8... | collective-permute-start | bytes 491528 | tf_op jit(solution)/shard_map/ppermute | solution.py:266
  33.7 55.6 %copy-start.4 = (s32[1,1,32]{2,1,0:T(1,128)S(1)}, s32[1,1,32]{2,1,0:T(1,128)}, u32[]{:S(2)}) copy-start(s32[1,1,32]{2,1,0:T(1,128)} %wiring.3) | copy-start | bytes 388
  33.7 7.2 %collective-permute-start.20 = (bf16[128,640]{1,0:T(8,128)(2,1)S(1)}, bf16[128,640]{1,0:T(8,128)(2,1)S(1)}, u32[]{:S(2)}, u32[]{:S(2)}) collective-permute-start(bf16[128,640]{1,0:T(8,128)(2,1)S(1)} %get-tuple-element.41), channel_id=1, source_target_pairs={{128,0},{129,1},{130,2},{131,3},{132,4},{133,5},{134,6},{135,7},{1... | collective-permute-start | bytes 491528 | tf_op jit(solution)/shard_map/ppermute | solution.py:266
  35.0 8.4 %collective-permute-start.21 = (bf16[128,640]{1,0:T(8,128)(2,1)S(1)}, bf16[128,640]{1,0:T(8,128)(2,1)S(1)}, u32[]{:S(2)}, u32[]{:S(2)}) collective-permute-start(bf16[128,640]{1,0:T(8,128)(2,1)S(1)} %get-tuple-element.42), channel_id=1, source_target_pairs={{128,3},{129,0},{130,1},{131,2},{132,7},{133,4},{134,5},{135,6},{1... | collective-permute-start | bytes 491528 | tf_op jit(solution)/shard_map/ppermute | solution.py:266
  36.4 8.2 %collective-permute-start.22 = (bf16[128,640]{1,0:T(8,128)(2,1)S(1)}, bf16[128,640]{1,0:T(8,128)(2,1)S(1)}, u32[]{:S(2)}, u32[]{:S(2)}) collective-permute-start(bf16[128,640]{1,0:T(8,128)(2,1)S(1)} %get-tuple-element.43), channel_id=1, source_target_pairs={{128,2},{129,3},{130,0},{131,1},{132,6},{133,7},{134,4},{135,5},{1... | collective-permute-start | bytes 491528 | tf_op jit(solution)/shard_map/ppermute | solution.py:266
  37.7 14.4 %collective-permute-start.23 = (bf16[128,640]{1,0:T(8,128)(2,1)S(1)}, bf16[128,640]{1,0:T(8,128)(2,1)S(1)}, u32[]{:S(2)}, u32[]{:S(2)}) collective-permute-start(bf16[128,640]{1,0:T(8,128)(2,1)S(1)} %get-tuple-element.44), channel_id=1, source_target_pairs={{128,1},{129,2},{130,3},{131,0},{132,5},{133,6},{134,7},{135,4},{1... | collective-permute-start | bytes 491528 | tf_op jit(solution)/shard_map/ppermute | solution.py:266
  39.8 15.9 %collective-permute-start.17 = (bf16[640,128]{1,0:T(8,128)(2,1)S(1)}, bf16[640,128]{1,0:T(8,128)(2,1)S(1)}, u32[]{:S(2)}, u32[]{:S(2)}) collective-permute-start(bf16[640,128]{1,0:T(8,128)(2,1)S(1)} %get-tuple-element.38), channel_id=1, source_target_pairs={{0,4},{4,8},{8,12},{12,0},{16,20},{20,24},{24,28},{28,16},{32,36},... | collective-permute-start | bytes 491528 | tf_op jit(solution)/shard_map/ppermute | solution.py:283
  40.9 14.9 %collective-permute-start.18 = (bf16[640,128]{1,0:T(8,128)(2,1)S(1)}, bf16[640,128]{1,0:T(8,128)(2,1)S(1)}, u32[]{:S(2)}, u32[]{:S(2)}) collective-permute-start(bf16[640,128]{1,0:T(8,128)(2,1)S(1)} %get-tuple-element.39), channel_id=1, source_target_pairs={{0,8},{4,12},{8,0},{12,4},{16,24},{20,28},{24,16},{28,20},{32,40},... | collective-permute-start | bytes 491528 | tf_op jit(solution)/shard_map/ppermute | solution.py:283
  43.4 14.5 %collective-permute-start.19 = (bf16[640,128]{1,0:T(8,128)(2,1)S(1)}, bf16[640,128]{1,0:T(8,128)(2,1)S(1)}, u32[]{:S(2)}, u32[]{:S(2)}) collective-permute-start(bf16[640,128]{1,0:T(8,128)(2,1)S(1)} %get-tuple-element.40), channel_id=1, source_target_pairs={{0,12},{4,0},{8,4},{12,8},{16,28},{20,16},{24,20},{28,24},{32,44},... | collective-permute-start | bytes 491528 | tf_op jit(solution)/shard_map/ppermute | solution.py:283
  44.6 13.4 %collective-permute-start.13 = (bf16[128,640]{1,0:T(8,128)(2,1)S(1)}, bf16[128,640]{1,0:T(8,128)(2,1)S(1)}, u32[]{:S(2)}, u32[]{:S(2)}) collective-permute-start(bf16[128,640]{1,0:T(8,128)(2,1)S(1)} %get-tuple-element.29.refs_0_), channel_id=1, source_target_pairs={{128,240},{132,244},{136,248},{140,252},{144,128},{148,132},{152,1... | collective-permute-start | bytes 491528 | tf_op jit(solution)/shard_map/ppermute | solution.py:287
  52.0 8.2 %collective-permute-start.12 = (bf16[128,640]{1,0:T(8,128)(2,1)S(1)}, bf16[128,640]{1,0:T(8,128)(2,1)S(1)}, u32[]{:S(2)}, u32[]{:S(2)}) collective-permute-start(bf16[128,640]{1,0:T(8,128)(2,1)S(1)} %get-tuple-element.29.refs_0_), channel_id=1, source_target_pairs={{128,224},{132,228},{136,232},{140,236},{144,240},{148,244},{152,2... | collective-permute-start | bytes 491528 | tf_op jit(solution)/shard_map/ppermute | solution.py:287
  55.7 11.0 %collective-permute-start.26 = (bf16[128,640]{1,0:T(8,128)(2,1)S(1)}, bf16[128,640]{1,0:T(8,128)(2,1)S(1)}, u32[]{:S(2)}, u32[]{:S(2)}) collective-permute-start(bf16[128,640]{1,0:T(8,128)(2,1)S(1)} %delta.1.refs_4_), channel_id=1, source_target_pairs={{0,12},{4,0},{8,4},{12,8},{16,28},{20,16},{24,20},{28,24},{32,44},... | collective-permute-start | bytes 491528 | tf_op jit(solution)/shard_map/ppermute | solution.py:283
  55.8 13.7 %collective-permute-start.25 = (bf16[128,640]{1,0:T(8,128)(2,1)S(1)}, bf16[128,640]{1,0:T(8,128)(2,1)S(1)}, u32[]{:S(2)}, u32[]{:S(2)}) collective-permute-start(bf16[128,640]{1,0:T(8,128)(2,1)S(1)} %delta.1.refs_4_), channel_id=1, source_target_pairs={{0,8},{4,12},{8,0},{12,4},{16,24},{20,28},{24,16},{28,20},{32,40},... | collective-permute-start | bytes 491528 | tf_op jit(solution)/shard_map/ppermute | solution.py:283
  57.9 14.7 %collective-permute-start.24 = (bf16[128,640]{1,0:T(8,128)(2,1)S(1)}, bf16[128,640]{1,0:T(8,128)(2,1)S(1)}, u32[]{:S(2)}, u32[]{:S(2)}) collective-permute-start(bf16[128,640]{1,0:T(8,128)(2,1)S(1)} %delta.1.refs_4_), channel_id=1, source_target_pairs={{0,4},{4,8},{8,12},{12,0},{16,20},{20,24},{24,28},{28,16},{32,36},... | collective-permute-start | bytes 491528 | tf_op jit(solution)/shard_map/ppermute | solution.py:283
  57.9 19.4 %collective-permute-start.11 = (bf16[128,640]{1,0:T(8,128)(2,1)S(1)}, bf16[128,640]{1,0:T(8,128)(2,1)S(1)}, u32[]{:S(2)}, u32[]{:S(2)}) collective-permute-start(bf16[128,640]{1,0:T(8,128)(2,1)S(1)} %get-tuple-element.29.refs_0_), channel_id=1, source_target_pairs={{128,208},{132,212},{136,216},{140,220},{144,224},{148,228},{152,2... | collective-permute-start | bytes 491528 | tf_op jit(solution)/shard_map/ppermute | solution.py:287
  60.3 17.8 %collective-permute-start.10 = (bf16[128,640]{1,0:T(8,128)(2,1)S(1)}, bf16[128,640]{1,0:T(8,128)(2,1)S(1)}, u32[]{:S(2)}, u32[]{:S(2)}) collective-permute-start(bf16[128,640]{1,0:T(8,128)(2,1)S(1)} %get-tuple-element.29.refs_0_), channel_id=1, source_target_pairs={{128,192},{132,196},{136,200},{140,204},{144,208},{148,212},{152,2... | collective-permute-start | bytes 491528 | tf_op jit(solution)/shard_map/ppermute | solution.py:287
  66.7 15.9 %collective-permute-start.9 = (bf16[128,640]{1,0:T(8,128)(2,1)S(1)}, bf16[128,640]{1,0:T(8,128)(2,1)S(1)}, u32[]{:S(2)}, u32[]{:S(2)}) collective-permute-start(bf16[128,640]{1,0:T(8,128)(2,1)S(1)} %get-tuple-element.29.refs_0_), channel_id=1, source_target_pairs={{128,176},{132,180},{136,184},{140,188},{144,192},{148,196},{152,2... | collective-permute-start | bytes 491528 | tf_op jit(solution)/shard_map/ppermute | solution.py:287
  69.5 16.9 %collective-permute-start.8 = (bf16[128,640]{1,0:T(8,128)(2,1)S(1)}, bf16[128,640]{1,0:T(8,128)(2,1)S(1)}, u32[]{:S(2)}, u32[]{:S(2)}) collective-permute-start(bf16[128,640]{1,0:T(8,128)(2,1)S(1)} %get-tuple-element.29.refs_0_), channel_id=1, source_target_pairs={{128,160},{132,164},{136,168},{140,172},{144,176},{148,180},{152,1... | collective-permute-start | bytes 491528 | tf_op jit(solution)/shard_map/ppermute | solution.py:287
  72.6 16.7 %collective-permute-start.7 = (bf16[128,640]{1,0:T(8,128)(2,1)S(1)}, bf16[128,640]{1,0:T(8,128)(2,1)S(1)}, u32[]{:S(2)}, u32[]{:S(2)}) collective-permute-start(bf16[128,640]{1,0:T(8,128)(2,1)S(1)} %get-tuple-element.29.refs_0_), channel_id=1, source_target_pairs={{128,144},{132,148},{136,152},{140,156},{144,160},{148,164},{152,1... | collective-permute-start | bytes 491528 | tf_op jit(solution)/shard_map/ppermute | solution.py:287
  77.3 27.3 %collective-permute-start.27 = (bf16[80,640]{1,0:T(8,128)(2,1)S(1)}, bf16[80,640]{1,0:T(8,128)(2,1)S(1)}, u32[]{:S(2)}, u32[]{:S(2)}) collective-permute-start(bf16[80,640]{1,0:T(8,128)(2,1)S(1)} %get-tuple-element.47), channel_id=1, source_target_pairs={{0,16},{4,20},{8,24},{12,28},{16,32},{20,36},{24,40},{28,44},{32,4... | collective-permute-start | bytes 307208 | tf_op jit(solution)/shard_map/ppermute | solution.py:283
  91.0 33.1 %collective-permute-start.14 = (bf16[2,128,640]{2,1,0:T(8,128)(2,1)S(1)}, bf16[2,128,640]{2,1,0:T(8,128)(2,1)S(1)}, u32[]{:S(2)}, u32[]{:S(2)}) collective-permute-start(bf16[2,128,640]{2,1,0:T(8,128)(2,1)S(1)} %get-tuple-element.31), channel_id=1, source_target_pairs={{128,132},{132,136},{136,140},{140,128},{144,148},{148,152},{152,1... | collective-permute-start | bytes 983048 | tf_op jit(solution)/shard_map/ppermute | solution.py:287
  94.5 29.6 %collective-permute-start.15 = (bf16[2,128,640]{2,1,0:T(8,128)(2,1)S(1)}, bf16[2,128,640]{2,1,0:T(8,128)(2,1)S(1)}, u32[]{:S(2)}, u32[]{:S(2)}) collective-permute-start(bf16[2,128,640]{2,1,0:T(8,128)(2,1)S(1)} %get-tuple-element.32), channel_id=1, source_target_pairs={{128,136},{132,140},{136,128},{140,132},{144,152},{148,156},{152,1... | collective-permute-start | bytes 983048 | tf_op jit(solution)/shard_map/ppermute | solution.py:287
  98.5 25.6 %collective-permute-start.16 = (bf16[2,128,640]{2,1,0:T(8,128)(2,1)S(1)}, bf16[2,128,640]{2,1,0:T(8,128)(2,1)S(1)}, u32[]{:S(2)}, u32[]{:S(2)}) collective-permute-start(bf16[2,128,640]{2,1,0:T(8,128)(2,1)S(1)} %get-tuple-element.33), channel_id=1, source_target_pairs={{128,140},{132,128},{136,132},{140,136},{144,156},{148,144},{152,1... | collective-permute-start | bytes 983048 | tf_op jit(solution)/shard_map/ppermute | solution.py:287
  102.0 6.7 %collective-permute-start.28 = (bf16[80,640]{1,0:T(8,128)(2,1)S(1)}, bf16[80,640]{1,0:T(8,128)(2,1)S(1)}, u32[]{:S(2)}, u32[]{:S(2)}) collective-permute-start(bf16[80,640]{1,0:T(8,128)(2,1)S(1)} %get-tuple-element.48), channel_id=1, source_target_pairs={{0,32},{4,36},{8,40},{12,44},{16,48},{20,52},{24,56},{28,60},{32,6... | collective-permute-start | bytes 307208 | tf_op jit(solution)/shard_map/ppermute | solution.py:283
  104.6 8.5 %collective-permute-start.29 = (bf16[80,640]{1,0:T(8,128)(2,1)S(1)}, bf16[80,640]{1,0:T(8,128)(2,1)S(1)}, u32[]{:S(2)}, u32[]{:S(2)}) collective-permute-start(bf16[80,640]{1,0:T(8,128)(2,1)S(1)} %get-tuple-element.49), channel_id=1, source_target_pairs={{0,48},{4,52},{8,56},{12,60},{16,64},{20,68},{24,72},{28,76},{32,8... | collective-permute-start | bytes 307208 | tf_op jit(solution)/shard_map/ppermute | solution.py:283
  108.7 9.1 %collective-permute-start.30 = (bf16[80,640]{1,0:T(8,128)(2,1)S(1)}, bf16[80,640]{1,0:T(8,128)(2,1)S(1)}, u32[]{:S(2)}, u32[]{:S(2)}) collective-permute-start(bf16[80,640]{1,0:T(8,128)(2,1)S(1)} %get-tuple-element.50), channel_id=1, source_target_pairs={{0,64},{4,68},{8,72},{12,76},{16,80},{20,84},{24,88},{28,92},{32,9... | collective-permute-start | bytes 307208 | tf_op jit(solution)/shard_map/ppermute | solution.py:283
  113.1 5.3 %collective-permute-start.31 = (bf16[80,640]{1,0:T(8,128)(2,1)S(1)}, bf16[80,640]{1,0:T(8,128)(2,1)S(1)}, u32[]{:S(2)}, u32[]{:S(2)}) collective-permute-start(bf16[80,640]{1,0:T(8,128)(2,1)S(1)} %get-tuple-element.51), channel_id=1, source_target_pairs={{0,80},{4,84},{8,88},{12,92},{16,96},{20,100},{24,104},{28,108},{3... | collective-permute-start | bytes 307208 | tf_op jit(solution)/shard_map/ppermute | solution.py:283
  117.8 4.9 %collective-permute-start.32 = (bf16[80,640]{1,0:T(8,128)(2,1)S(1)}, bf16[80,640]{1,0:T(8,128)(2,1)S(1)}, u32[]{:S(2)}, u32[]{:S(2)}) collective-permute-start(bf16[80,640]{1,0:T(8,128)(2,1)S(1)} %get-tuple-element.52), channel_id=1, source_target_pairs={{0,96},{4,100},{8,104},{12,108},{16,112},{20,116},{24,120},{28,124... | collective-permute-start | bytes 307208 | tf_op jit(solution)/shard_map/ppermute | solution.py:283
  118.4 4.9 %collective-permute-start.33 = (bf16[80,640]{1,0:T(8,128)(2,1)S(1)}, bf16[80,640]{1,0:T(8,128)(2,1)S(1)}, u32[]{:S(2)}, u32[]{:S(2)}) collective-permute-start(bf16[80,640]{1,0:T(8,128)(2,1)S(1)} %get-tuple-element.53), channel_id=1, source_target_pairs={{0,112},{4,116},{8,120},{12,124},{16,0},{20,4},{24,8},{28,12},{32,... | collective-permute-start | bytes 307208 | tf_op jit(solution)/shard_map/ppermute | solution.py:283

commit v2 on v1

v2 whole, which is shorter than its diff:
```python
import functools
import math

import jax
import jax.numpy as jnp
from jax import lax
from jax.experimental import pallas as pl
from jax.experimental.pallas import tpu as pltpu
from jax.sharding import PartitionSpec as P

WCAP = 2
EPS = 1e-06
ROOT_HALF = 0.7071067811865476
NORMAL_PEAK = 0.3989422804014327
VMEM_LIMIT = 12 * 1024 * 1024
VM = pl.BlockSpec(memory_space=pltpu.VMEM)
SM = pl.BlockSpec(memory_space=pltpu.SMEM)
AWAY = ((0, 0), (1, 0), (2, 1), (0, 1), (1, 1), (0, 2), (1, 2), (2, 0))
BF = jnp.bfloat16
F32 = jnp.float32


def gelu_value(v):
    return 0.5 * v * (1.0 + lax.erf(v * ROOT_HALF))


def gelu_slope(v):
    return 0.5 * (1.0 + lax.erf(v * ROOT_HALF)) + v * jnp.exp(-0.5 * v * v) * NORMAL_PEAK


def call(body, out_shape, in_specs, name, scratch=(), flops=0, nbytes=0):
    many = isinstance(out_shape, (tuple, list))
    return pl.pallas_call(
        body,
        out_shape=out_shape,
        in_specs=in_specs,
        out_specs=tuple(VM for _ in out_shape) if many else VM,
        scratch_shapes=scratch,
        name=name,
        compiler_params=pltpu.CompilerParams(vmem_limit_bytes=VMEM_LIMIT),
        cost_estimate=pl.CostEstimate(flops=flops, bytes_accessed=nbytes, transcendentals=0),
    )


def rows_scale(blocks, feat):
    total = None
    for block in blocks:
        wide = block[...].astype(F32)
        part = jnp.sum(wide * wide, axis=-1, keepdims=True)
        total = part if total is None else total + part
    return lax.rsqrt(total / feat + EPS)


def weight_rows(w_ref, k, tp_pos, tp_count, width):
    start = pl.multiple_of(lax.rem(tp_pos + tp_count - k, tp_count) * width, width)
    return w_ref[pl.ds(start, width), :]


def rows_product(refs, w_ref, tp_pos, tp_count):
    width = refs[0].shape[-1]
    total = None
    for k, ref in enumerate(refs):
        part = jnp.dot(
            ref[...], weight_rows(w_ref, k, tp_pos, tp_count, width), preferred_element_type=F32
        )
        total = part if total is None else total + part
    return total


def first_kernel(tp_count, feat, info, _, *refs):
    blocks = refs[:tp_count]
    own_ref, other_ref, x1_ref, mixed_ref, scale_ref = refs[tp_count:]

    def run(w_ref):
        scale = rows_scale(blocks, feat)
        mixed = rows_product(blocks, w_ref, info[2], tp_count) * scale
        x1_ref[...] = (blocks[0][...].astype(F32) + gelu_value(mixed)).astype(BF)
        mixed_ref[...] = mixed
        scale_ref[...] = jnp.broadcast_to(scale, scale_ref.shape)

    @pl.when(info[0] == 0)
    def _():
        run(own_ref)

    @pl.when(info[0] == 1)
    def _():
        run(other_ref)


def second_kernel(tp_count, feat, loss_scale, info, lengths, *refs):
    early = refs[:tp_count]
    blocks = refs[tp_count : 2 * tp_count]
    own_ref, other_ref, goal_ref, x2_ref, delta_ref, pack_ref = refs[2 * tp_count : 2 * tp_count + 6]
    back_refs = refs[2 * tp_count + 6 :]
    tokens, width = blocks[0].shape
    tp_pos = info[2]

    def run(w_ref, base):
        scale = rows_scale(blocks, feat)
        mixed = rows_product(blocks, w_ref, tp_pos, tp_count) * scale
        x2 = (blocks[0][...].astype(F32) + gelu_value(mixed)).astype(BF)
        x2_ref[...] = x2
        token_ids = lax.broadcasted_iota(jnp.int32, (tokens, 1), 0) + base
        valid = jnp.where(token_ids < lengths[0, info[1]], loss_scale, 0.0)
        goal = goal_ref[base : base + tokens]
        grad = ((x2.astype(F32) - goal.astype(F32)) * valid).astype(BF)
        delta = (grad.astype(F32) * gelu_slope(mixed)).astype(BF)
        wide_delta = delta.astype(F32)
        stat = jnp.sum(mixed * wide_delta, axis=-1, keepdims=True) / feat
        delta_ref[...] = (wide_delta * scale).astype(BF)
        for k in range(tp_count):
            back = lax.dot_general(
                delta,
                weight_rows(w_ref, k, tp_pos, tp_count, width),
                (((1,), (1,)), ((), ())),
                preferred_element_type=F32,
            )
            row = scale * (back - blocks[k][...].astype(F32) * (scale * stat))
            if k == 0:
                row = row + grad.astype(F32)
            back_refs[k][...] = row.astype(BF)

    def pack(source):
        for k in range(tp_count):
            pack_ref[:, k * width : (k + 1) * width] = source[k][...]

    @pl.when(info[0] == 0)
    def _():
        run(other_ref, 0)
        pack(blocks)

    @pl.when(info[0] == 1)
    def _():
        run(own_ref, tokens)
        pack(early)


def turn_kernel(tp_count, x_count, info, *refs):
    first = refs[:tp_count]
    second = refs[tp_count : 2 * tp_count]
    other_ref, mixed_ref, scale_ref = refs[2 * tp_count : 2 * tp_count + 3]
    outs = refs[2 * tp_count + 3 : 2 * tp_count + 3 + x_count]
    slope_ref, turned = refs[2 * tp_count + 3 + x_count :]
    tp_pos = info[2]
    x_pos = lax.rem(info[1], x_count)
    rows = turned.shape[2]
    width = first[0].shape[1]

    def put(blocks):
        for k in range(tp_count):
            source = lax.rem(tp_pos + tp_count - k, tp_count)
            both = jnp.concatenate(
                [blocks[k][...], other_ref[:, k * width : (k + 1) * width]], axis=0
            )
            flipped = both.T
            per = width // rows
            for i in range(per):
                place = source * (per // x_count) + i // x_count
                turned[i % x_count, place] = flipped[i * rows : (i + 1) * rows]

    @pl.when(info[0] == 0)
    def _():
        put(first)

    @pl.when(info[0] == 1)
    def _():
        put(second)

    slope_ref[...] = gelu_slope(mixed_ref[...]) * scale_ref[:, :1]
    for k in range(x_count):
        outs[k][...] = turned[lax.rem(x_pos + k, x_count)].reshape(outs[k].shape)


def delta_kernel(tp_count, info, *refs):
    back, (slope_ref, last_ref, keep_ref, send_ref) = refs[:tp_count], refs[tp_count:]
    grad = back[0][...].astype(F32)
    for ref in back[1:]:
        grad = grad + ref[...].astype(F32)
    grad = grad.astype(BF).astype(F32)
    delta = (grad * slope_ref[...]).astype(BF)

    @pl.when(info[0] == 0)
    def _():
        keep_ref[...] = delta
        send_ref[...] = last_ref[...]

    @pl.when(info[0] == 1)
    def _():
        keep_ref[...] = last_ref[...]
        send_ref[...] = delta


def stack_kernel(*refs):
    for k, ref in enumerate(refs[:-1]):
        refs[-1][k] = ref[...]


def join_kernel(a_ref, b_ref, out_ref):
    half = a_ref.shape[0]
    out_ref[:half] = a_ref[...]
    out_ref[half:] = b_ref[...]


def part_kernel(x_count, z_count, info, *refs):
    turned, deltas = refs[:x_count], refs[x_count : 2 * x_count]
    own_ref, plus_ref, minus_ref, far_ref, wide_ref, parts = refs[2 * x_count :]
    left = jnp.concatenate([t[...] for t in turned], axis=1)
    right = jnp.concatenate([d[...] for d in deltas], axis=0)
    part = jnp.dot(left, right, preferred_element_type=F32).astype(BF)
    parts[...] = part.reshape(parts.shape)
    z_pos = info[1] // x_count

    def chunk(k):
        return parts[lax.rem(z_pos + z_count + k, z_count)]

    own_ref[...] = chunk(0)
    for i, k in enumerate((1, 4, -2)):
        plus_ref[i] = chunk(k)
    for i, k in enumerate((-1, 2)):
        minus_ref[i] = chunk(k)
    far_ref[...] = chunk(3)
    wide_ref[...] = chunk(-3)


def middle_kernel(plus_ref, minus_ref, far_ref, wide_ref, up_ref, down_ref):
    up = far_ref[...].astype(F32) + plus_ref[1].astype(F32) + minus_ref[1].astype(F32)
    up_ref[...] = up.astype(BF)
    down_ref[...] = (wide_ref[...].astype(F32) + plus_ref[2].astype(F32)).astype(BF)


def sum_kernel(own_ref, plus_ref, minus_ref, up_ref, down_ref, out_ref):
    total = own_ref[...].astype(F32) + plus_ref[0].astype(F32) + minus_ref[0].astype(F32)
    out_ref[...] = total + up_ref[...].astype(F32) + down_ref[...].astype(F32)


def table_kernel(x_count, z_count, info, wiring, _, out, table, counts):
    replicas = x_count * z_count
    fill_table(wiring, table, counts, replicas)
    x_pos = lax.rem(info[1], x_count)
    z_pos = info[1] // x_count
    for k in range(x_count):
        target = z_pos * x_count + lax.rem(x_pos + k, x_count)
        for c in range(WCAP):
            j = table[target * WCAP + c]
            here = (j >= 0) & (lax.rem(j, x_count) == x_pos)
            steps = lax.rem(z_pos + z_count - j // x_count, z_count)
            out[k * WCAP + c] = jnp.where(here, steps, -1)
    for c in range(WCAP):
        j = table[info[1] * WCAP + c]
        steps = lax.rem(x_pos + x_count - lax.rem(j, x_count), x_count)
        out[x_count * WCAP + c] = jnp.where(j >= 0, steps, -1)


def fill_table(wiring, table, counts, replicas):
    @pl.loop(0, replicas)
    def _(r):
        counts[r] = 0
        for c in range(WCAP):
            table[r * WCAP + c] = -1

    @pl.loop(0, replicas)
    def _(j):
        r = wiring[0, 0, j]
        table[r * WCAP + counts[r]] = j
        counts[r] = counts[r] + 1


def route_kernel(x_count, z_count, plan, *refs):
    near, outs = refs[:3], refs[3:]
    for k in range(x_count):
        for c in range(WCAP):
            steps = plan[k * WCAP + c]
            for m, (group, place) in enumerate(AWAY):

                @pl.when(steps == m)
                def _(k=k, c=c, group=group, place=place):
                    outs[k][c] = near[group][place]


def pick_kernel(x_count, info, plan, x1_ref, *refs):
    slots, (keep_ref, send_ref) = refs[:x_count], refs[x_count:]

    def place(out_ref):
        for c in range(WCAP):
            steps = plan[x_count * WCAP + c]

            @pl.when(steps < 0)
            def _(c=c):
                out_ref[c] = jnp.zeros_like(x1_ref)

            for k in range(x_count):

                @pl.when(steps == k)
                def _(c=c, k=k):
                    out_ref[c] = slots[k][c]

    def entry(out_ref):
        out_ref[0] = x1_ref[...]
        for c in range(1, WCAP):
            out_ref[c] = jnp.zeros_like(x1_ref)

    @pl.when(info[0] == 0)
    def _():
        entry(keep_ref)
        place(send_ref)

    @pl.when(info[0] == 1)
    def _():
        place(keep_ref)
        entry(send_ref)


def acts_kernel(info, keep_ref, come_ref, out_ref):
    half = keep_ref.shape[1]

    @pl.when(info[0] == 0)
    def _():
        out_ref[:, :half] = keep_ref[...]
        out_ref[:, half:] = come_ref[...]

    @pl.when(info[0] == 1)
    def _():
        out_ref[:, :half] = come_ref[...]
        out_ref[:, half:] = keep_ref[...]


def on_device(x_count, z_count, inputs, weights, wiring, lengths, targets):
    replicas = lax.axis_size("rep")
    tp_count = lax.axis_size("tp")
    section = lax.axis_index("section")
    rep = lax.axis_index("rep")
    tp = lax.axis_index("tp")
    info = jnp.stack([section, rep, tp]).astype(jnp.int32)
    _, _, tokens, width = inputs.shape
    half = tokens // 2
    weight = weights[0]
    feat = weight.shape[0]
    goal = targets.reshape(tokens, width)
    rows = feat // replicas
    loss_scale = 1.0 / math.sqrt(replicas * tokens)

    def swap(value):
        return lax.ppermute(value, "section", [(0, 1), (1, 0)])

    def tp_move(value, k):
        return lax.ppermute(value, "tp", [(y, (y + k) % tp_count) for y in range(tp_count)])

    def x_move(value, k):
        pairs = [
            (z * x_count + x, z * x_count + (x + k) % x_count)
            for z in range(z_count)
            for x in range(x_count)
        ]
        return lax.ppermute(value, "rep", pairs)

    def z_move(value, k):
        pairs = [
            (z * x_count + x, ((z + k) % z_count) * x_count + x)
            for z in range(z_count)
            for x in range(x_count)
        ]
        return lax.ppermute(value, "rep", pairs)

    def shape(*dims, dtype=BF):
        return jax.ShapeDtypeStruct(dims, dtype)

    flops = 2 * half * feat * width
    other_weight = swap(weight)
    plan = pl.pallas_call(
        functools.partial(table_kernel, x_count, z_count),
        out_shape=shape(x_count * WCAP + WCAP, dtype=jnp.int32),
        in_specs=[SM, SM, VM],
        out_specs=SM,
        scratch_shapes=[
            pltpu.SMEM((replicas * WCAP,), jnp.int32),
            pltpu.SMEM((replicas,), jnp.int32),
        ],
        name="table",
        compiler_params=pltpu.CompilerParams(vmem_limit_bytes=VMEM_LIMIT),
    )(info, wiring, weight)
    x0 = lax.dynamic_slice(inputs.reshape(tokens, width), (section * half, 0), (half, width))
    first_blocks = [x0] + [tp_move(x0, k) for k in range(1, tp_count)]
    x1, mixed, scale = call(
        functools.partial(first_kernel, tp_count, feat),
        (shape(half, width), shape(half, width, dtype=F32), shape(half, 128, dtype=F32)),
        [SM, SM] + [VM] * (tp_count + 2),
        "first",
        flops=flops,
        nbytes=2 * feat * width,
    )(info, plan, *first_blocks, weight, other_weight)
    second_blocks = [x1] + [tp_move(x1, k) for k in range(1, tp_count)]
    x2, delta1, packed, *back = call(
        functools.partial(second_kernel, tp_count, feat, loss_scale),
        (shape(half, width), shape(half, width), shape(half, feat))
        + (shape(half, width),) * tp_count,
        [SM, SM] + [VM] * (2 * tp_count + 3),
        "second",
        flops=2 * flops,
        nbytes=2 * feat * width,
    )(info, lengths, *first_blocks, *second_blocks, weight, other_weight, goal)
    back_blocks = [back[0]] + [tp_move(back[k], tp_count - k) for k in range(1, tp_count)]
    far = [x2, z_move(x2, 3), z_move(x2, z_count - 3)]
    trio = call(stack_kernel, shape(3, half, width), [VM] * 3, "trio")(*far)
    near = [trio, z_move(trio, 1), z_move(trio, z_count - 1)]
    other_pack = swap(packed)
    *turned, slope = call(
        functools.partial(turn_kernel, tp_count, x_count),
        (shape(feat // x_count, tokens),) * x_count + (shape(half, width, dtype=F32),),
        [SM] + [VM] * (2 * tp_count + 3),
        "turn",
        scratch=[pltpu.VMEM((x_count, z_count, rows, tokens), BF)],
        flops=flops // 4,
        nbytes=2 * feat * tokens,
    )(info, *first_blocks, *second_blocks, other_pack, mixed, scale)
    lefts = [turned[0]] + [x_move(turned[k], k) for k in range(1, x_count)]
    keep, send = call(
        functools.partial(delta_kernel, tp_count),
        (shape(half, width),) * 2,
        [SM] + [VM] * (tp_count + 2),
        "delta",
        flops=half * width,
        nbytes=8 * half * width,
    )(info, *back_blocks, slope, delta1)
    come = swap(send)
    delta = call(join_kernel, shape(tokens, width), [VM, VM], "join")(keep, come)
    rights = [delta] + [x_move(delta, k) for k in range(1, x_count)]
    chunk = shape(rows, width)
    own, plus, minus, far_part, wide_part = call(
        functools.partial(part_kernel, x_count, z_count),
        (chunk, shape(3, rows, width), shape(2, rows, width), chunk, chunk),
        [SM] + [VM] * (2 * x_count),
        "part",
        scratch=[pltpu.VMEM((z_count, rows, width), BF)],
        flops=2 * flops,
        nbytes=4 * feat * tokens,
    )(info, *lefts, *rights)
    plus, minus = z_move(plus, 1), z_move(minus, z_count - 1)
    up, down = call(middle_kernel, (chunk, chunk), [VM] * 4, "middle")(
        plus, minus, far_part, wide_part
    )
    grad_rows = call(sum_kernel, shape(rows, width, dtype=F32), [VM] * 5, "sum")(
        own, plus, minus, z_move(up, 3), z_move(down, z_count - 3)
    )
    pair = shape(WCAP, half, width)
    slots = call(
        functools.partial(route_kernel, x_count, z_count),
        (pair,) * x_count,
        [SM] + [VM] * 3,
        "route",
        nbytes=2 * z_count * half * width,
    )(plan, *near)
    arrived = [slots[0]] + [x_move(slots[k], k) for k in range(1, x_count)]
    held, sent = call(
        functools.partial(pick_kernel, x_count),
        (pair, pair),
        [SM, SM] + [VM] * (x_count + 1),
        "pick",
        nbytes=2 * z_count * half * width,
    )(info, plan, x1, *arrived)
    acts = call(acts_kernel, shape(WCAP, tokens, width), [SM, VM, VM], "acts")(
        info, held, swap(sent)
    )
    return (
        acts.reshape(1, 1, 1, WCAP, tokens, width),
        grad_rows.reshape(1, rows, width),
    )


def solution(mesh):
    in_specs = (
        P(None, "rep", None, "tp"),
        P("section", None, "tp"),
        P(),
        P(),
        P(None, "rep", None, "tp"),
    )
    out_specs = (P("section", None, "rep", None, None, "tp"), P("section", "rep", "tp"))
    x_count = 4
    z_count = mesh.shape["rep"] // x_count
    return jax.shard_map(
        functools.partial(on_device, x_count, z_count),
        mesh=mesh,
        in_specs=in_specs,
        out_specs=out_specs,
        check_vma=False,
    )
```

time: 127 us -> 95 us (0.75)
  starting transfers between devices: 72.4 us -> 39 us
  Pallas kernels: 10.3 us -> 13.1 us
    ppermute x34 -> x30, starting transfers between devices: 72.4 us -> 39 us  [the longest x8 15.3 us: z_move(): return lax.ppermute(value, 'rep', pairs)]
    pallas_call x7 -> x12, Pallas kernels: 8.65 us -> 12.2 us  [the longest x1 2.73 us: on_device(): call(functools.partial(second_kernel, tp_count, feat, loss_scale), (shape...]
    ppermute x34 -> x30, waiting for transfers between devices: 39.5 us -> 39.1 us  [the longest x8 14.8 us: z_move(): return lax.ppermute(value, 'rep', pairs)]
  transfers between devices with their start and end apart: 34 -> 30, of which waited for: 11 -> 13; matrix products, arithmetic and copies ran while one was open for 0% -> 0% of each run, Pallas kernels for 4% -> 8%
where the time goes in v2:
time: 95 us; the launch traced here: 94.7 us
  waiting for transfers between devices  39.1 us (41%)
  starting transfers between devices  39 us (41%)
  Pallas kernels  13.1 us (14%)
  local copies, waits for them, and re-layouts  2.62 us (3%)
    ppermute x8, starting transfers between devices, z_move(): return lax.ppermute(value, 'rep', pairs)  15.3 us
    ppermute x8, waiting for transfers between devices, z_move(): return lax.ppermute(value, 'rep', pairs)  14.8 us
    ppermute x9, waiting for transfers between devices, x_move(): return lax.ppermute(value, 'rep', pairs)  13.8 us
    ppermute x9, waiting for transfers between devices, tp_move(): lax.ppermute(value, 'tp', [(y, (y + k) % tp_count) for y in range(tp_coun...  10.5 us
    ppermute x4, starting transfers between devices, swap(): return lax.ppermute(value, 'section', [(0, 1), (1, 0)])  9.19 us
    ppermute x9, starting transfers between devices, x_move(): return lax.ppermute(value, 'rep', pairs)  8.11 us
    ppermute x9, starting transfers between devices, tp_move(): lax.ppermute(value, 'tp', [(y, (y + k) % tp_count) for y in range(tp_coun...  6.4 us
    pallas_call x1, Pallas kernels, on_device(): call(functools.partial(second_kernel, tp_count, feat, loss_scale), (shape...  2.73 us
  transfers between devices with their start and end apart: 30, of which 13 were waited for; matrix products, arithmetic and copies ran while one was open for 0% of the time, Pallas kernels for 8%

profile of v2, /device:TPU:1, one launch (start us, length us, event | category | flops | bytes accessed | tf_op | source)
XLA Modules:
  0.0 94.7 jit_solution(3971486099578675968)
XLA Ops:
  0.6 0.0 copy-start
  0.6 3.3 %collective-permute-start.3 = (bf16[2560,640]{1,0:T(8,128)(2,1)}, bf16[2560,640]{1,0:T(8,128)(2,1)S(1)}, u32[]{:S(2)}, u32[]{:S(2)}) collective-permute-start(bf16[2560,640]{1,0:T(8,128)(2,1)} %bitcast.9), channel_id=1, source_target_pairs={{0,128},{128,0},{1,129},{129,1},{2,130},{130,2},{3,131},{131,3},{4... | collective-permute-start | bytes 9830408 | tf_op jit(solution)/shard_map/ppermute | solution.py:343
  4.0 1.2 %collective-permute-start.2 = (bf16[64,640]{1,0:T(8,128)(2,1)S(1)}, bf16[64,640]{1,0:T(8,128)(2,1)}, u32[]{:S(2)}, u32[]{:S(2)}) collective-permute-start(bf16[64,640]{1,0:T(8,128)(2,1)S(1)} %dynamic-slice_bitcast_fusion.refs_0_), channel_id=1, source_target_pairs={{0,3},{1,0},{2,1},{3,2},{4,7},{5,4},{6,5},{7,6},{8,11},{9,8},{10,9... | collective-permute-start | bytes 245768 | tf_op jit(solution)/shard_map/ppermute | solution.py:346
  5.2 0.3 collective-permute-start.1
  5.6 0.7 collective-permute-start
  6.2 0.1 pad_add_fusion.info
  6.3 1.9 %copy-done.1 = bf16[1,2560,640]{2,1,0:T(8,128)(2,1)S(1)} copy-done((bf16[1,2560,640]{2,1,0:T(8,128)(2,1)S(1)}, bf16[1,2560,640]{2,1,0:T(8,128)(2,1)}, u32[]{:S(2)}) %copy-start.1) | copy-done | bytes 3276824
  8.3 0.7 copy-done.4
  8.9 1.9 %table.1._.plan = s32[10]{0:T(128)S(1)} custom-call(s32[3]{0:T(128)S(1)} %pad_add_fusion.info, s32[1,1,32]{2,1,0:T(1,128)S(1)} %copy-done.4, bf16[2560,640]{1,0:T(8,128)(2,1)S(1)} %bitcast.10), custom_call_target="tpu_custom_call" | custom-call | tf_op jit(solution)/shard_map/table/pallas_call | solution.py:369
  10.8 0.0 copy-start.3
  10.8 0.0 copy-start.5
  10.8 0.0 collective-permute-done.1.refs_2_
  10.9 1.4 %collective-permute-done.refs_1_ = bf16[64,640]{1,0:T(8,128)(2,1)} collective-permute-done((bf16[64,640]{1,0:T(8,128)(2,1)S(1)}, bf16[64,640]{1,0:T(8,128)(2,1)}, u32[]{:S(2)}, u32[]{:S(2)}) %collective-permute-start) | collective-permute-done | bytes 81952 | tf_op jit(solution)/shard_map/ppermute | solution.py:346
  12.3 0.0 collective-permute-done.3.refs_5_.refs_9_
  12.3 1.6 %first.1 = (bf16[64,640]{1,0:T(8,128)(2,1)S(1)}, f32[64,640]{1,0:T(8,128)S(1)}, f32[64,128]{1,0:T(8,128)S(1)}) custom-call(s32[3]{0:T(128)S(1)} %pad_add_fusion.info, s32[10]{0:T(128)S(1)} %table.1._.plan, bf16[64,640]{1,0:T(8,128)(2,1)S(1)} %dynamic-slice_bitcast_fusion.refs_0_, bf16[64,640]{1,0:T(8,128)(2,1)} %collective-permute-done.refs_1_, ...), custom_call_target="tpu_custom_call" | custom-call | flops 209715200 | bytes 3276800 | tf_op jit(solution)/shard_map/first/pallas_call | solution.py:383
  13.9 0.6 collective-permute-start.6
  14.6 1.4 %collective-permute-start.5 = (bf16[64,640]{1,0:T(8,128)(2,1)S(1)}, bf16[64,640]{1,0:T(8,128)(2,1)S(1)}, u32[]{:S(2)}, u32[]{:S(2)}) collective-permute-start(bf16[64,640]{1,0:T(8,128)(2,1)S(1)} %get-tuple-element.32.refs_4_.x1_ref), channel_id=1, source_target_pairs={{0,2},{1,3},{2,0},{3,1},{4,6},{5,7},{6,4},{7,5},{8,10},{9,11},{10,... | collective-permute-start | bytes 245768 | tf_op jit(solution)/shard_map/ppermute | solution.py:346
  16.0 0.3 collective-permute-start.4
  16.3 1.0 %collective-permute-done.6.refs_7_ = bf16[64,640]{1,0:T(8,128)(2,1)S(1)} collective-permute-done((bf16[64,640]{1,0:T(8,128)(2,1)S(1)}, bf16[64,640]{1,0:T(8,128)(2,1)S(1)}, u32[]{:S(2)}, u32[]{:S(2)}) %collective-permute-start.6) | collective-permute-done | bytes 81952 | tf_op jit(solution)/shard_map/ppermute | solution.py:346
  17.3 2.1 %collective-permute-done.5.refs_6_ = bf16[64,640]{1,0:T(8,128)(2,1)S(1)} collective-permute-done((bf16[64,640]{1,0:T(8,128)(2,1)S(1)}, bf16[64,640]{1,0:T(8,128)(2,1)S(1)}, u32[]{:S(2)}, u32[]{:S(2)}) %collective-permute-start.5) | collective-permute-done | bytes 81952 | tf_op jit(solution)/shard_map/ppermute | solution.py:346
  19.4 1.1 %collective-permute-done.4.refs_5_ = bf16[64,640]{1,0:T(8,128)(2,1)S(1)} collective-permute-done((bf16[64,640]{1,0:T(8,128)(2,1)S(1)}, bf16[64,640]{1,0:T(8,128)(2,1)S(1)}, u32[]{:S(2)}, u32[]{:S(2)}) %collective-permute-start.4) | collective-permute-done | bytes 81952 | tf_op jit(solution)/shard_map/ppermute | solution.py:346
  20.5 2.7 %second.1 = (bf16[64,640]{1,0:T(8,128)(2,1)S(1)}, bf16[64,640]{1,0:T(8,128)(2,1)S(1)}, bf16[64,2560]{1,0:T(8,128)(2,1)S(1)}, bf16[64,640]{1,0:T(8,128)(2,1)S(1)}...) custom-call(s32[3]{0:T(128)S(1)} %pad_add_fusion.info, ...), custom_call_target="tpu_custom_call" | custom-call | flops 419430400 | bytes 3276800 | tf_op jit(solution)/shard_map/second/pallas_call | solution.py:392
  23.2 3.3 %collective-permute-start.15 = (bf16[64,2560]{1,0:T(8,128)(2,1)S(1)}, bf16[64,2560]{1,0:T(8,128)(2,1)S(1)}, u32[]{:S(2)}, u32[]{:S(2)}) collective-permute-start(bf16[64,2560]{1,0:T(8,128)(2,1)S(1)} %get-tuple-element.40), channel_id=1, source_target_pairs={{0,128},{128,0},{1,129},{129,1},{2,130},{130,2},{3,131},{131,3},{4... | collective-permute-start | bytes 983048 | tf_op jit(solution)/shard_map/ppermute | solution.py:343
  26.6 0.3 collective-permute-start.19
  26.9 0.9 collective-permute-start.20
  27.8 0.6 collective-permute-start.21
  28.3 0.0 collective-permute-done.15.refs_8_
  28.3 1.3 %turn.1 = (bf16[640,128]{1,0:T(8,128)(2,1)S(1)}, bf16[640,128]{1,0:T(8,128)(2,1)S(1)}, bf16[640,128]{1,0:T(8,128)(2,1)S(1)}, bf16[640,128]{1,0:T(8,128)(2,1)S(1)}, f32[64,640]{1,0:T(8,128)S(1)}) custom-call(s32[3]{0:T(128)S(1)} %pad_add_fusion.info, bf16[64,640]{1,0:T(8,128)(2,1)S(1)} %dynamic-slice_bitcast_fusion.refs_0_, ...), custom_call_target="tpu_custom_call" | custom-call | flops 52428800 | bytes 655360 | tf_op jit(solution)/shard_map/turn/pallas_call | solution.py:406
  29.6 0.9 collective-permute-done.19.refs_1_
  30.6 1.5 %collective-permute-done.20.refs_2_ = bf16[64,640]{1,0:T(8,128)(2,1)S(1)} collective-permute-done((bf16[64,640]{1,0:T(8,128)(2,1)S(1)}, bf16[64,640]{1,0:T(8,128)(2,1)S(1)}, u32[]{:S(2)}, u32[]{:S(2)}) %collective-permute-start.20) | collective-permute-done | bytes 81952 | tf_op jit(solution)/shard_map/ppermute | solution.py:346
  32.0 2.4 %collective-permute-done.21.refs_3_ = bf16[64,640]{1,0:T(8,128)(2,1)S(1)} collective-permute-done((bf16[64,640]{1,0:T(8,128)(2,1)S(1)}, bf16[64,640]{1,0:T(8,128)(2,1)S(1)}, u32[]{:S(2)}, u32[]{:S(2)}) %collective-permute-start.21) | collective-permute-done | bytes 81952 | tf_op jit(solution)/shard_map/ppermute | solution.py:346
  34.5 0.6 delta.1
  35.1 0.8 collective-permute-start.22
  35.9 1.2 %collective-permute-start.16 = (bf16[640,128]{1,0:T(8,128)(2,1)S(1)}, bf16[640,128]{1,0:T(8,128)(2,1)S(1)}, u32[]{:S(2)}, u32[]{:S(2)}) collective-permute-start(bf16[640,128]{1,0:T(8,128)(2,1)S(1)} %get-tuple-element.44), channel_id=1, source_target_pairs={{0,4},{4,8},{8,12},{12,0},{16,20},{20,24},{24,28},{28,16},{32,36},... | collective-permute-start | bytes 491528 | tf_op jit(solution)/shard_map/ppermute | solution.py:354
  37.1 2.5 %collective-permute-start.17 = (bf16[640,128]{1,0:T(8,128)(2,1)S(1)}, bf16[640,128]{1,0:T(8,128)(2,1)S(1)}, u32[]{:S(2)}, u32[]{:S(2)}) collective-permute-start(bf16[640,128]{1,0:T(8,128)(2,1)S(1)} %get-tuple-element.45), channel_id=1, source_target_pairs={{0,8},{4,12},{8,0},{12,4},{16,24},{20,28},{24,16},{28,20},{32,40},... | collective-permute-start | bytes 491528 | tf_op jit(solution)/shard_map/ppermute | solution.py:354
  39.6 1.1 %collective-permute-start.18 = (bf16[640,128]{1,0:T(8,128)(2,1)S(1)}, bf16[640,128]{1,0:T(8,128)(2,1)S(1)}, u32[]{:S(2)}, u32[]{:S(2)}) collective-permute-start(bf16[640,128]{1,0:T(8,128)(2,1)S(1)} %get-tuple-element.46), channel_id=1, source_target_pairs={{0,12},{4,0},{8,4},{12,8},{16,28},{20,16},{24,20},{28,24},{32,44},... | collective-permute-start | bytes 491528 | tf_op jit(solution)/shard_map/ppermute | solution.py:354
  40.7 6.5 %collective-permute-start.8 = (bf16[64,640]{1,0:T(8,128)(2,1)S(1)}, bf16[64,640]{1,0:T(8,128)(2,1)S(1)}, u32[]{:S(2)}, u32[]{:S(2)}) collective-permute-start(bf16[64,640]{1,0:T(8,128)(2,1)S(1)} %get-tuple-element.33.refs_0_), channel_id=1, source_target_pairs={{0,80},{4,84},{8,88},{12,92},{16,96},{20,100},{24,104},{28,108},{3... | collective-permute-start | bytes 245768 | tf_op jit(solution)/shard_map/ppermute | solution.py:362
  47.2 0.0 collective-permute-done.22.b_ref
  47.2 0.0 collective-permute-start.7
  47.2 5.0 %collective-permute-done.8.refs_2_ = bf16[64,640]{1,0:T(8,128)(2,1)S(1)} collective-permute-done((bf16[64,640]{1,0:T(8,128)(2,1)S(1)}, bf16[64,640]{1,0:T(8,128)(2,1)S(1)}, u32[]{:S(2)}, u32[]{:S(2)}) %collective-permute-start.8) | collective-permute-done | bytes 81952 | tf_op jit(solution)/shard_map/ppermute | solution.py:362
  52.2 0.0 collective-permute-start.25
  52.2 4.8 %collective-permute-done.7.refs_1_ = bf16[64,640]{1,0:T(8,128)(2,1)S(1)} collective-permute-done((bf16[64,640]{1,0:T(8,128)(2,1)S(1)}, bf16[64,640]{1,0:T(8,128)(2,1)S(1)}, u32[]{:S(2)}, u32[]{:S(2)}) %collective-permute-start.7) | collective-permute-done | bytes 81952 | tf_op jit(solution)/shard_map/ppermute | solution.py:362
  57.0 0.2 collective-permute-start.24
  57.2 0.3 collective-permute-start.23
  57.5 0.1 collective-permute-start.10
  57.6 1.4 %collective-permute-start.9 = (bf16[3,64,640]{2,1,0:T(8,128)(2,1)S(1)}, bf16[3,64,640]{2,1,0:T(8,128)(2,1)S(1)}, u32[]{:S(2)}, u32[]{:S(2)}) collective-permute-start(bf16[3,64,640]{2,1,0:T(8,128)(2,1)S(1)} %trio.1.refs_0_), channel_id=1, source_target_pairs={{0,16},{4,20},{8,24},{12,28},{16,32},{20,36},{24,40},{28,44},{32,4... | collective-permute-start | bytes 737288 | tf_op jit(solution)/shard_map/ppermute | solution.py:362
  59.1 4.2 %collective-permute-done.24.refs_6_ = bf16[128,640]{1,0:T(8,128)(2,1)S(1)} collective-permute-done((bf16[128,640]{1,0:T(8,128)(2,1)S(1)}, bf16[128,640]{1,0:T(8,128)(2,1)S(1)}, u32[]{:S(2)}, u32[]{:S(2)}) %collective-permute-start.24) | collective-permute-done | bytes 163872 | tf_op jit(solution)/shard_map/ppermute | solution.py:354
  63.3 4.7 %collective-permute-done.23.refs_5_ = bf16[128,640]{1,0:T(8,128)(2,1)S(1)} collective-permute-done((bf16[128,640]{1,0:T(8,128)(2,1)S(1)}, bf16[128,640]{1,0:T(8,128)(2,1)S(1)}, u32[]{:S(2)}, u32[]{:S(2)}) %collective-permute-start.23) | collective-permute-done | bytes 163872 | tf_op jit(solution)/shard_map/ppermute | solution.py:354
  67.9 1.3 %part.1 = (bf16[80,640]{1,0:T(8,128)(2,1)S(1)}, bf16[3,80,640]{2,1,0:T(8,128)(2,1)S(1)}, bf16[2,80,640]{2,1,0:T(8,128)(2,1)S(1)}, bf16[80,640]{1,0:T(8,128)(2,1)S(1)}, bf16[80,640]{1,0:T(8,128)(2,1)S(1)}) custom-call(s32[3]{0:T(128)S(1)} %pad_add_fusion.info, bf16[640,128]{1,0:T(8,128)(2,1)S(1)} %get-tuple-element.43.refs_0_, ...), custom_call_target="tpu_custom_call" | custom-call | flops 419430400 | bytes 1310720 | tf_op jit(solution)/shard_map/part/pallas_call | solution.py:428
  69.2 0.1 collective-permute-start.26
  69.3 0.9 route.1
  70.2 0.1 collective-permute-start.11
  70.3 0.4 collective-permute-start.12
  70.8 2.2 %collective-permute-start.13 = (bf16[2,64,640]{2,1,0:T(8,128)(2,1)S(1)}, bf16[2,64,640]{2,1,0:T(8,128)(2,1)S(1)}, u32[]{:S(2)}, u32[]{:S(2)}) collective-permute-start(bf16[2,64,640]{2,1,0:T(8,128)(2,1)S(1)} %get-tuple-element.37), channel_id=1, source_target_pairs={{0,12},{4,0},{8,4},{12,8},{16,28},{20,16},{24,20},{28,24},{32,44},... | collective-permute-start | bytes 491528 | tf_op jit(solution)/shard_map/ppermute | solution.py:354
  73.0 2.6 %collective-permute-start.27 = (bf16[2,80,640]{2,1,0:T(8,128)(2,1)S(1)}, bf16[2,80,640]{2,1,0:T(8,128)(2,1)S(1)}, u32[]{:S(2)}, u32[]{:S(2)}) collective-permute-start(bf16[2,80,640]{2,1,0:T(8,128)(2,1)S(1)} %get-tuple-element.57), channel_id=1, source_target_pairs={{0,112},{4,116},{8,120},{12,124},{16,0},{20,4},{24,8},{28,12},{32,... | collective-permute-start | bytes 614408 | tf_op jit(solution)/shard_map/ppermute | solution.py:362
  75.6 4.9 %collective-permute-done.11.refs_1_ = bf16[2,64,640]{2,1,0:T(8,128)(2,1)S(1)} collective-permute-done((bf16[2,64,640]{2,1,0:T(8,128)(2,1)S(1)}, bf16[2,64,640]{2,1,0:T(8,128)(2,1)S(1)}, u32[]{:S(2)}, u32[]{:S(2)}) %collective-permute-start.11) | collective-permute-done | bytes 163872 | tf_op jit(solution)/shard_map/ppermute | solution.py:354
  80.6 0.6 pick.1
  81.2 1.8 %collective-permute-start.14 = (bf16[2,64,640]{2,1,0:T(8,128)(2,1)S(1)}, bf16[2,64,640]{2,1,0:T(8,128)(2,1)S(1)}, u32[]{:S(2)}, u32[]{:S(2)}) collective-permute-start(bf16[2,64,640]{2,1,0:T(8,128)(2,1)S(1)} %get-tuple-element.39), channel_id=1, source_target_pairs={{0,128},{128,0},{1,129},{129,1},{2,130},{130,2},{3,131},{131,3},{4... | collective-permute-start | bytes 491528 | tf_op jit(solution)/shard_map/ppermute | solution.py:343
  83.0 0.1 middle.1
  83.1 0.1 collective-permute-start.28
  83.2 4.5 %collective-permute-start.29 = (bf16[80,640]{1,0:T(8,128)(2,1)S(1)}, bf16[80,640]{1,0:T(8,128)(2,1)S(1)}, u32[]{:S(2)}, u32[]{:S(2)}) collective-permute-start(bf16[80,640]{1,0:T(8,128)(2,1)S(1)} %get-tuple-element.61), channel_id=1, source_target_pairs={{0,80},{4,84},{8,88},{12,92},{16,96},{20,100},{24,104},{28,108},{3... | collective-permute-start | bytes 307208 | tf_op jit(solution)/shard_map/ppermute | solution.py:362
  87.6 1.3 %acts.1 = bf16[2,128,640]{2,1,0:T(8,128)(2,1)} custom-call(s32[3]{0:T(128)S(1)} %pad_add_fusion.info, bf16[2,64,640]{2,1,0:T(8,128)(2,1)S(1)} %get-tuple-element.38.keep_ref, bf16[2,64,640]{2,1,0:T(8,128)(2,1)S(1)} %collective-permute-done.14.come_ref), custom_call_target="tpu_custom_call" | custom-call | tf_op jit(solution)/shard_map/acts/pallas_call | solution.py:460
  88.9 5.0 %collective-permute-done.28.up_ref = bf16[80,640]{1,0:T(8,128)(2,1)S(1)} collective-permute-done((bf16[80,640]{1,0:T(8,128)(2,1)S(1)}, bf16[80,640]{1,0:T(8,128)(2,1)S(1)}, u32[]{:S(2)}, u32[]{:S(2)}) %collective-permute-start.28) | collective-permute-done | bytes 102432 | tf_op jit(solution)/shard_map/ppermute | solution.py:362
  94.0 0.8 sum.1
  (23 shorter events, 0.1 us)
Async XLA Ops:
  0.6 3.3 %copy-start = (bf16[1,1,128,640]{3,2,1,0:T(8,128)(2,1)S(1)}, bf16[1,1,128,640]{3,2,1,0:T(8,128)(2,1)}, u32[]{:S(2)}) copy-start(bf16[1,1,128,640]{3,2,1,0:T(8,128)(2,1)} %param.5) | copy-start | bytes 491524
  0.6 11.7 %collective-permute-start.3 = (bf16[2560,640]{1,0:T(8,128)(2,1)}, bf16[2560,640]{1,0:T(8,128)(2,1)S(1)}, u32[]{:S(2)}, u32[]{:S(2)}) collective-permute-start(bf16[2560,640]{1,0:T(8,128)(2,1)} %bitcast.9), channel_id=1, source_target_pairs={{0,128},{128,0},{1,129},{129,1},{2,130},{130,2},{3,131},{131,3},{4... | collective-permute-start | bytes 9830408 | tf_op jit(solution)/shard_map/ppermute | solution.py:343
  4.0 6.8 %collective-permute-start.2 = (bf16[64,640]{1,0:T(8,128)(2,1)S(1)}, bf16[64,640]{1,0:T(8,128)(2,1)}, u32[]{:S(2)}, u32[]{:S(2)}) collective-permute-start(bf16[64,640]{1,0:T(8,128)(2,1)S(1)} %dynamic-slice_bitcast_fusion.refs_0_), channel_id=1, source_target_pairs={{0,3},{1,0},{2,1},{3,2},{4,7},{5,4},{6,5},{7,6},{8,11},{9,8},{10,9... | collective-permute-start | bytes 245768 | tf_op jit(solution)/shard_map/ppermute | solution.py:346
  5.2 5.6 %collective-permute-start.1 = (bf16[64,640]{1,0:T(8,128)(2,1)S(1)}, bf16[64,640]{1,0:T(8,128)(2,1)}, u32[]{:S(2)}, u32[]{:S(2)}) collective-permute-start(bf16[64,640]{1,0:T(8,128)(2,1)S(1)} %dynamic-slice_bitcast_fusion.refs_0_), channel_id=1, source_target_pairs={{0,2},{1,3},{2,0},{3,1},{4,6},{5,7},{6,4},{7,5},{8,10},{9,11},{10,... | collective-permute-start | bytes 245768 | tf_op jit(solution)/shard_map/ppermute | solution.py:346
  5.6 6.7 %collective-permute-start = (bf16[64,640]{1,0:T(8,128)(2,1)S(1)}, bf16[64,640]{1,0:T(8,128)(2,1)}, u32[]{:S(2)}, u32[]{:S(2)}) collective-permute-start(bf16[64,640]{1,0:T(8,128)(2,1)S(1)} %dynamic-slice_bitcast_fusion.refs_0_), channel_id=1, source_target_pairs={{0,1},{1,2},{2,3},{3,0},{4,5},{5,6},{6,7},{7,4},{8,9},{9,10},{10,1... | collective-permute-start | bytes 245768 | tf_op jit(solution)/shard_map/ppermute | solution.py:346
  6.3 1.9 %copy-start.1 = (bf16[1,2560,640]{2,1,0:T(8,128)(2,1)S(1)}, bf16[1,2560,640]{2,1,0:T(8,128)(2,1)}, u32[]{:S(2)}) copy-start(bf16[1,2560,640]{2,1,0:T(8,128)(2,1)} %param.6) | copy-start | bytes 9830404
  8.2 0.7 copy-start.4
  8.9 3.4 %copy-start.2 = (bf16[1,2560,640]{2,1,0:T(8,128)(2,1)S(1)}, bf16[1,2560,640]{2,1,0:T(8,128)(2,1)}, u32[]{:S(2)}) copy-start(bf16[1,2560,640]{2,1,0:T(8,128)(2,1)} %param.6) | copy-start | bytes 9830404
  10.8 9.7 %copy-start.3 = (bf16[1,1,128,640]{3,2,1,0:T(8,128)(2,1)S(1)}, bf16[1,1,128,640]{3,2,1,0:T(8,128)(2,1)}, u32[]{:S(2)}) copy-start(bf16[1,1,128,640]{3,2,1,0:T(8,128)(2,1)} %param.9) | copy-start | bytes 491524
  10.8 9.7 %copy-start.5 = (s32[1,32]{1,0:T(1,128)S(1)}, s32[1,32]{1,0:T(1,128)}, u32[]{:S(2)}) copy-start(s32[1,32]{1,0:T(1,128)} %lengths.1) | copy-start | bytes 388
  13.9 3.4 %collective-permute-start.6 = (bf16[64,640]{1,0:T(8,128)(2,1)S(1)}, bf16[64,640]{1,0:T(8,128)(2,1)S(1)}, u32[]{:S(2)}, u32[]{:S(2)}) collective-permute-start(bf16[64,640]{1,0:T(8,128)(2,1)S(1)} %get-tuple-element.32.refs_4_.x1_ref), channel_id=1, source_target_pairs={{0,3},{1,0},{2,1},{3,2},{4,7},{5,4},{6,5},{7,6},{8,11},{9,8},{10,9... | collective-permute-start | bytes 245768 | tf_op jit(solution)/shard_map/ppermute | solution.py:346
  14.6 4.8 %collective-permute-start.5 = (bf16[64,640]{1,0:T(8,128)(2,1)S(1)}, bf16[64,640]{1,0:T(8,128)(2,1)S(1)}, u32[]{:S(2)}, u32[]{:S(2)}) collective-permute-start(bf16[64,640]{1,0:T(8,128)(2,1)S(1)} %get-tuple-element.32.refs_4_.x1_ref), channel_id=1, source_target_pairs={{0,2},{1,3},{2,0},{3,1},{4,6},{5,7},{6,4},{7,5},{8,10},{9,11},{10,... | collective-permute-start | bytes 245768 | tf_op jit(solution)/shard_map/ppermute | solution.py:346
  16.0 4.5 %collective-permute-start.4 = (bf16[64,640]{1,0:T(8,128)(2,1)S(1)}, bf16[64,640]{1,0:T(8,128)(2,1)S(1)}, u32[]{:S(2)}, u32[]{:S(2)}) collective-permute-start(bf16[64,640]{1,0:T(8,128)(2,1)S(1)} %get-tuple-element.32.refs_4_.x1_ref), channel_id=1, source_target_pairs={{0,1},{1,2},{2,3},{3,0},{4,5},{5,6},{6,7},{7,4},{8,9},{9,10},{10,1... | collective-permute-start | bytes 245768 | tf_op jit(solution)/shard_map/ppermute | solution.py:346
  23.2 5.1 %collective-permute-start.15 = (bf16[64,2560]{1,0:T(8,128)(2,1)S(1)}, bf16[64,2560]{1,0:T(8,128)(2,1)S(1)}, u32[]{:S(2)}, u32[]{:S(2)}) collective-permute-start(bf16[64,2560]{1,0:T(8,128)(2,1)S(1)} %get-tuple-element.40), channel_id=1, source_target_pairs={{0,128},{128,0},{1,129},{129,1},{2,130},{130,2},{3,131},{131,3},{4... | collective-permute-start | bytes 983048 | tf_op jit(solution)/shard_map/ppermute | solution.py:343
  26.6 4.0 %collective-permute-start.19 = (bf16[64,640]{1,0:T(8,128)(2,1)S(1)}, bf16[64,640]{1,0:T(8,128)(2,1)S(1)}, u32[]{:S(2)}, u32[]{:S(2)}) collective-permute-start(bf16[64,640]{1,0:T(8,128)(2,1)S(1)} %get-tuple-element.48), channel_id=1, source_target_pairs={{0,3},{1,0},{2,1},{3,2},{4,7},{5,4},{6,5},{7,6},{8,11},{9,8},{10,9... | collective-permute-start | bytes 245768 | tf_op jit(solution)/shard_map/ppermute | solution.py:346
  26.9 5.2 %collective-permute-start.20 = (bf16[64,640]{1,0:T(8,128)(2,1)S(1)}, bf16[64,640]{1,0:T(8,128)(2,1)S(1)}, u32[]{:S(2)}, u32[]{:S(2)}) collective-permute-start(bf16[64,640]{1,0:T(8,128)(2,1)S(1)} %get-tuple-element.49), channel_id=1, source_target_pairs={{0,2},{1,3},{2,0},{3,1},{4,6},{5,7},{6,4},{7,5},{8,10},{9,11},{10,... | collective-permute-start | bytes 245768 | tf_op jit(solution)/shard_map/ppermute | solution.py:346
  27.8 6.7 %collective-permute-start.21 = (bf16[64,640]{1,0:T(8,128)(2,1)S(1)}, bf16[64,640]{1,0:T(8,128)(2,1)S(1)}, u32[]{:S(2)}, u32[]{:S(2)}) collective-permute-start(bf16[64,640]{1,0:T(8,128)(2,1)S(1)} %get-tuple-element.50), channel_id=1, source_target_pairs={{0,1},{1,2},{2,3},{3,0},{4,5},{5,6},{6,7},{7,4},{8,9},{9,10},{10,1... | collective-permute-start | bytes 245768 | tf_op jit(solution)/shard_map/ppermute | solution.py:346
  35.1 12.1 %collective-permute-start.22 = (bf16[64,640]{1,0:T(8,128)(2,1)S(1)}, bf16[64,640]{1,0:T(8,128)(2,1)S(1)}, u32[]{:S(2)}, u32[]{:S(2)}) collective-permute-start(bf16[64,640]{1,0:T(8,128)(2,1)S(1)} %get-tuple-element.54), channel_id=1, source_target_pairs={{0,128},{128,0},{1,129},{129,1},{2,130},{130,2},{3,131},{131,3},{4... | collective-permute-start | bytes 245768 | tf_op jit(solution)/shard_map/ppermute | solution.py:343
  35.9 21.3 %collective-permute-start.16 = (bf16[640,128]{1,0:T(8,128)(2,1)S(1)}, bf16[640,128]{1,0:T(8,128)(2,1)S(1)}, u32[]{:S(2)}, u32[]{:S(2)}) collective-permute-start(bf16[640,128]{1,0:T(8,128)(2,1)S(1)} %get-tuple-element.44), channel_id=1, source_target_pairs={{0,4},{4,8},{8,12},{12,0},{16,20},{20,24},{24,28},{28,16},{32,36},... | collective-permute-start | bytes 491528 | tf_op jit(solution)/shard_map/ppermute | solution.py:354
  37.1 20.4 %collective-permute-start.17 = (bf16[640,128]{1,0:T(8,128)(2,1)S(1)}, bf16[640,128]{1,0:T(8,128)(2,1)S(1)}, u32[]{:S(2)}, u32[]{:S(2)}) collective-permute-start(bf16[640,128]{1,0:T(8,128)(2,1)S(1)} %get-tuple-element.45), channel_id=1, source_target_pairs={{0,8},{4,12},{8,0},{12,4},{16,24},{20,28},{24,16},{28,20},{32,40},... | collective-permute-start | bytes 491528 | tf_op jit(solution)/shard_map/ppermute | solution.py:354
  39.6 18.1 %collective-permute-start.18 = (bf16[640,128]{1,0:T(8,128)(2,1)S(1)}, bf16[640,128]{1,0:T(8,128)(2,1)S(1)}, u32[]{:S(2)}, u32[]{:S(2)}) collective-permute-start(bf16[640,128]{1,0:T(8,128)(2,1)S(1)} %get-tuple-element.46), channel_id=1, source_target_pairs={{0,12},{4,0},{8,4},{12,8},{16,28},{20,16},{24,20},{28,24},{32,44},... | collective-permute-start | bytes 491528 | tf_op jit(solution)/shard_map/ppermute | solution.py:354
  40.7 11.5 %collective-permute-start.8 = (bf16[64,640]{1,0:T(8,128)(2,1)S(1)}, bf16[64,640]{1,0:T(8,128)(2,1)S(1)}, u32[]{:S(2)}, u32[]{:S(2)}) collective-permute-start(bf16[64,640]{1,0:T(8,128)(2,1)S(1)} %get-tuple-element.33.refs_0_), channel_id=1, source_target_pairs={{0,80},{4,84},{8,88},{12,92},{16,96},{20,100},{24,104},{28,108},{3... | collective-permute-start | bytes 245768 | tf_op jit(solution)/shard_map/ppermute | solution.py:362
  47.2 9.8 %collective-permute-start.7 = (bf16[64,640]{1,0:T(8,128)(2,1)S(1)}, bf16[64,640]{1,0:T(8,128)(2,1)S(1)}, u32[]{:S(2)}, u32[]{:S(2)}) collective-permute-start(bf16[64,640]{1,0:T(8,128)(2,1)S(1)} %get-tuple-element.33.refs_0_), channel_id=1, source_target_pairs={{0,48},{4,52},{8,56},{12,60},{16,64},{20,68},{24,72},{28,76},{32,8... | collective-permute-start | bytes 245768 | tf_op jit(solution)/shard_map/ppermute | solution.py:362
  52.2 6.9 %collective-permute-start.25 = (bf16[128,640]{1,0:T(8,128)(2,1)S(1)}, bf16[128,640]{1,0:T(8,128)(2,1)S(1)}, u32[]{:S(2)}, u32[]{:S(2)}) collective-permute-start(bf16[128,640]{1,0:T(8,128)(2,1)S(1)} %join.1.refs_4_), channel_id=1, source_target_pairs={{0,12},{4,0},{8,4},{12,8},{16,28},{20,16},{24,20},{28,24},{32,44},... | collective-permute-start | bytes 491528 | tf_op jit(solution)/shard_map/ppermute | solution.py:354
  57.0 6.3 %collective-permute-start.24 = (bf16[128,640]{1,0:T(8,128)(2,1)S(1)}, bf16[128,640]{1,0:T(8,128)(2,1)S(1)}, u32[]{:S(2)}, u32[]{:S(2)}) collective-permute-start(bf16[128,640]{1,0:T(8,128)(2,1)S(1)} %join.1.refs_4_), channel_id=1, source_target_pairs={{0,8},{4,12},{8,0},{12,4},{16,24},{20,28},{24,16},{28,20},{32,40},... | collective-permute-start | bytes 491528 | tf_op jit(solution)/shard_map/ppermute | solution.py:354
  57.2 10.8 %collective-permute-start.23 = (bf16[128,640]{1,0:T(8,128)(2,1)S(1)}, bf16[128,640]{1,0:T(8,128)(2,1)S(1)}, u32[]{:S(2)}, u32[]{:S(2)}) collective-permute-start(bf16[128,640]{1,0:T(8,128)(2,1)S(1)} %join.1.refs_4_), channel_id=1, source_target_pairs={{0,4},{4,8},{8,12},{12,0},{16,20},{20,24},{24,28},{28,16},{32,36},... | collective-permute-start | bytes 491528 | tf_op jit(solution)/shard_map/ppermute | solution.py:354
  57.5 11.8 %collective-permute-start.10 = (bf16[3,64,640]{2,1,0:T(8,128)(2,1)S(1)}, bf16[3,64,640]{2,1,0:T(8,128)(2,1)S(1)}, u32[]{:S(2)}, u32[]{:S(2)}) collective-permute-start(bf16[3,64,640]{2,1,0:T(8,128)(2,1)S(1)} %trio.1.refs_0_), channel_id=1, source_target_pairs={{0,112},{4,116},{8,120},{12,124},{16,0},{20,4},{24,8},{28,12},{32,... | collective-permute-start | bytes 737288 | tf_op jit(solution)/shard_map/ppermute | solution.py:362
  57.6 11.7 %collective-permute-start.9 = (bf16[3,64,640]{2,1,0:T(8,128)(2,1)S(1)}, bf16[3,64,640]{2,1,0:T(8,128)(2,1)S(1)}, u32[]{:S(2)}, u32[]{:S(2)}) collective-permute-start(bf16[3,64,640]{2,1,0:T(8,128)(2,1)S(1)} %trio.1.refs_0_), channel_id=1, source_target_pairs={{0,16},{4,20},{8,24},{12,28},{16,32},{20,36},{24,40},{28,44},{32,4... | collective-permute-start | bytes 737288 | tf_op jit(solution)/shard_map/ppermute | solution.py:362
  69.2 13.7 %collective-permute-start.26 = (bf16[3,80,640]{2,1,0:T(8,128)(2,1)S(1)}, bf16[3,80,640]{2,1,0:T(8,128)(2,1)S(1)}, u32[]{:S(2)}, u32[]{:S(2)}) collective-permute-start(bf16[3,80,640]{2,1,0:T(8,128)(2,1)S(1)} %get-tuple-element.56), channel_id=1, source_target_pairs={{0,16},{4,20},{8,24},{12,28},{16,32},{20,36},{24,40},{28,44},{32,4... | collective-permute-start | bytes 921608 | tf_op jit(solution)/shard_map/ppermute | solution.py:362
  70.2 10.3 %collective-permute-start.11 = (bf16[2,64,640]{2,1,0:T(8,128)(2,1)S(1)}, bf16[2,64,640]{2,1,0:T(8,128)(2,1)S(1)}, u32[]{:S(2)}, u32[]{:S(2)}) collective-permute-start(bf16[2,64,640]{2,1,0:T(8,128)(2,1)S(1)} %get-tuple-element.35), channel_id=1, source_target_pairs={{0,4},{4,8},{8,12},{12,0},{16,20},{20,24},{24,28},{28,16},{32,36},... | collective-permute-start | bytes 491528 | tf_op jit(solution)/shard_map/ppermute | solution.py:354
  70.3 10.2 %collective-permute-start.12 = (bf16[2,64,640]{2,1,0:T(8,128)(2,1)S(1)}, bf16[2,64,640]{2,1,0:T(8,128)(2,1)S(1)}, u32[]{:S(2)}, u32[]{:S(2)}) collective-permute-start(bf16[2,64,640]{2,1,0:T(8,128)(2,1)S(1)} %get-tuple-element.36), channel_id=1, source_target_pairs={{0,8},{4,12},{8,0},{12,4},{16,24},{20,28},{24,16},{28,20},{32,40},... | collective-permute-start | bytes 491528 | tf_op jit(solution)/shard_map/ppermute | solution.py:354
  70.8 9.8 %collective-permute-start.13 = (bf16[2,64,640]{2,1,0:T(8,128)(2,1)S(1)}, bf16[2,64,640]{2,1,0:T(8,128)(2,1)S(1)}, u32[]{:S(2)}, u32[]{:S(2)}) collective-permute-start(bf16[2,64,640]{2,1,0:T(8,128)(2,1)S(1)} %get-tuple-element.37), channel_id=1, source_target_pairs={{0,12},{4,0},{8,4},{12,8},{16,28},{20,16},{24,20},{28,24},{32,44},... | collective-permute-start | bytes 491528 | tf_op jit(solution)/shard_map/ppermute | solution.py:354
  73.0 10.0 %collective-permute-start.27 = (bf16[2,80,640]{2,1,0:T(8,128)(2,1)S(1)}, bf16[2,80,640]{2,1,0:T(8,128)(2,1)S(1)}, u32[]{:S(2)}, u32[]{:S(2)}) collective-permute-start(bf16[2,80,640]{2,1,0:T(8,128)(2,1)S(1)} %get-tuple-element.57), channel_id=1, source_target_pairs={{0,112},{4,116},{8,120},{12,124},{16,0},{20,4},{24,8},{28,12},{32,... | collective-permute-start | bytes 614408 | tf_op jit(solution)/shard_map/ppermute | solution.py:362
  81.2 6.4 %collective-permute-start.14 = (bf16[2,64,640]{2,1,0:T(8,128)(2,1)S(1)}, bf16[2,64,640]{2,1,0:T(8,128)(2,1)S(1)}, u32[]{:S(2)}, u32[]{:S(2)}) collective-permute-start(bf16[2,64,640]{2,1,0:T(8,128)(2,1)S(1)} %get-tuple-element.39), channel_id=1, source_target_pairs={{0,128},{128,0},{1,129},{129,1},{2,130},{130,2},{3,131},{131,3},{4... | collective-permute-start | bytes 491528 | tf_op jit(solution)/shard_map/ppermute | solution.py:343
  83.1 10.9 %collective-permute-start.28 = (bf16[80,640]{1,0:T(8,128)(2,1)S(1)}, bf16[80,640]{1,0:T(8,128)(2,1)S(1)}, u32[]{:S(2)}, u32[]{:S(2)}) collective-permute-start(bf16[80,640]{1,0:T(8,128)(2,1)S(1)} %get-tuple-element.60), channel_id=1, source_target_pairs={{0,48},{4,52},{8,56},{12,60},{16,64},{20,68},{24,72},{28,76},{32,8... | collective-permute-start | bytes 307208 | tf_op jit(solution)/shard_map/ppermute | solution.py:362
  83.2 10.8 %collective-permute-start.29 = (bf16[80,640]{1,0:T(8,128)(2,1)S(1)}, bf16[80,640]{1,0:T(8,128)(2,1)S(1)}, u32[]{:S(2)}, u32[]{:S(2)}) collective-permute-start(bf16[80,640]{1,0:T(8,128)(2,1)S(1)} %get-tuple-element.61), channel_id=1, source_target_pairs={{0,80},{4,84},{8,88},{12,92},{16,96},{20,100},{24,104},{28,108},{3... | collective-permute-start | bytes 307208 | tf_op jit(solution)/shard_map/ppermute | solution.py:362

commit v3 on v2

--- a/solution.py
+++ b/solution.py
@@ -168,11 +168,13 @@
 
     slope_ref[...] = gelu_slope(mixed_ref[...]) * scale_ref[:, :1]
     for k in range(x_count):
-        outs[k][...] = turned[lax.rem(x_pos + k, x_count)].reshape(outs[k].shape)
+        chunk = turned[lax.rem(x_pos + k, x_count)]
+        outs[k][: chunk.shape[0] * rows] = chunk.reshape(-1, chunk.shape[2])
 
 
 def delta_kernel(tp_count, info, *refs):
-    back, (slope_ref, last_ref, keep_ref, send_ref) = refs[:tp_count], refs[tp_count:]
+    back = refs[:tp_count]
+    slope_ref, last_ref, keep_ref, send_ref = refs[tp_count:]
     grad = back[0][...].astype(F32)
     for ref in back[1:]:
         grad = grad + ref[...].astype(F32)
@@ -190,12 +192,13 @@
         send_ref[...] = delta
 
 
-def stack_kernel(*refs):
-    for k, ref in enumerate(refs[:-1]):
-        refs[-1][k] = ref[...]
-
-
-def join_kernel(a_ref, b_ref, out_ref):
+def trio_kernel(a_ref, b_ref, c_ref, _, out_ref):
+    for k, ref in enumerate((a_ref, b_ref, c_ref)):
+        out_ref[k] = ref[...]
+
+
+def join_kernel(a_ref, b_ref, *refs):
+    out_ref = refs[-1]
     half = a_ref.shape[0]
     out_ref[:half] = a_ref[...]
     out_ref[half:] = b_ref[...]
@@ -213,60 +216,65 @@
     def chunk(k):
         return parts[lax.rem(z_pos + z_count + k, z_count)]
 
+    width = far_ref.shape[1]
+    split = plus_ref.shape[1] - 2 * width
     own_ref[...] = chunk(0)
-    for i, k in enumerate((1, 4, -2)):
-        plus_ref[i] = chunk(k)
-    for i, k in enumerate((-1, 2)):
-        minus_ref[i] = chunk(k)
     far_ref[...] = chunk(3)
     wide_ref[...] = chunk(-3)
-
-
-def middle_kernel(plus_ref, minus_ref, far_ref, wide_ref, up_ref, down_ref):
-    up = far_ref[...].astype(F32) + plus_ref[1].astype(F32) + minus_ref[1].astype(F32)
-    up_ref[...] = up.astype(BF)
-    down_ref[...] = (wide_ref[...].astype(F32) + plus_ref[2].astype(F32)).astype(BF)
-
-
-def sum_kernel(own_ref, plus_ref, minus_ref, up_ref, down_ref, out_ref):
-    total = own_ref[...].astype(F32) + plus_ref[0].astype(F32) + minus_ref[0].astype(F32)
+    plus_ref[:, :width] = chunk(1)
+    plus_ref[:, width : 2 * width] = chunk(-2)
+    plus_ref[:, 2 * width :] = chunk(4)[:, :split]
+    minus_ref[:, :width] = chunk(-1)
+    minus_ref[:, width : 2 * width] = chunk(2)
+    minus_ref[:, 2 * width :] = chunk(4)[:, split:]
+
+
+def middle_kernel(plus_ref, minus_ref, far_ref, wide_ref, _, up_ref, down_ref):
+    width = far_ref.shape[1]
+    split = plus_ref.shape[1] - 2 * width
+    up = far_ref[...].astype(F32) + minus_ref[:, width : 2 * width].astype(F32)
+    down = wide_ref[...].astype(F32) + plus_ref[:, width : 2 * width].astype(F32)
+    up_ref[:, :split] = (up[:, :split] + plus_ref[:, 2 * width :].astype(F32)).astype(BF)
+    up_ref[:, split:] = up[:, split:].astype(BF)
+    down_ref[:, :split] = down[:, :split].astype(BF)
+    down_ref[:, split:] = (down[:, split:] + minus_ref[:, 2 * width :].astype(F32)).astype(BF)
+
+
+def sum_kernel(own_ref, plus_ref, minus_ref, up_ref, down_ref, _, out_ref):
+    width = own_ref.shape[1]
+    total = own_ref[...].astype(F32) + plus_ref[:, :width].astype(F32)
+    total = total + minus_ref[:, :width].astype(F32)
     out_ref[...] = total + up_ref[...].astype(F32) + down_ref[...].astype(F32)
 
 
-def table_kernel(x_count, z_count, info, wiring, _, out, table, counts):
-    replicas = x_count * z_count
-    fill_table(wiring, table, counts, replicas)
+def plan_kernel(x_count, z_count, info, wiring, _, plan, counts):
     x_pos = lax.rem(info[1], x_count)
     z_pos = info[1] // x_count
-    for k in range(x_count):
-        target = z_pos * x_count + lax.rem(x_pos + k, x_count)
-        for c in range(WCAP):
-            j = table[target * WCAP + c]
-            here = (j >= 0) & (lax.rem(j, x_count) == x_pos)
-            steps = lax.rem(z_pos + z_count - j // x_count, z_count)
-            out[k * WCAP + c] = jnp.where(here, steps, -1)
-    for c in range(WCAP):
-        j = table[info[1] * WCAP + c]
-        steps = lax.rem(x_pos + x_count - lax.rem(j, x_count), x_count)
-        out[x_count * WCAP + c] = jnp.where(j >= 0, steps, -1)
-
-
-def fill_table(wiring, table, counts, replicas):
-    @pl.loop(0, replicas)
-    def _(r):
-        counts[r] = 0
-        for c in range(WCAP):
-            table[r * WCAP + c] = -1
-
-    @pl.loop(0, replicas)
-    def _(j):
+    for i in range(x_count * WCAP + WCAP):
+        plan[i] = -1
+    for i in range(x_count):
+        counts[i] = 0
+    for j in range(x_count * z_count):
         r = wiring[0, 0, j]
-        table[r * WCAP + counts[r]] = j
-        counts[r] = counts[r] + 1
+
+        @pl.when(r // x_count == z_pos)
+        def _(j=j, r=r):
+            column = lax.rem(r, x_count)
+            slot = jnp.minimum(counts[column], WCAP - 1)
+            counts[column] = slot + 1
+
+            @pl.when(x_pos == j % x_count)
+            def _():
+                shift = lax.rem(column + x_count - x_pos, x_count)
+                plan[shift * WCAP + slot] = lax.rem(z_pos + z_count - j // x_count, z_count)
+
+            @pl.when(column == x_pos)
+            def _():
+                plan[x_count * WCAP + slot] = lax.rem(x_pos + x_count - j % x_count, x_count)
 
 
 def route_kernel(x_count, z_count, plan, *refs):
-    near, outs = refs[:3], refs[3:]
+    near, outs = refs[:3], refs[-x_count:]
     for k in range(x_count):
         for c in range(WCAP):
             steps = plan[k * WCAP + c]
@@ -278,50 +286,66 @@
 
 
 def pick_kernel(x_count, info, plan, x1_ref, *refs):
-    slots, (keep_ref, send_ref) = refs[:x_count], refs[x_count:]
-
-    def place(out_ref):
+    slots, send_ref = refs[:x_count], refs[-1]
+
+    @pl.when(info[0] == 0)
+    def _():
         for c in range(WCAP):
             steps = plan[x_count * WCAP + c]
+            for k in range(x_count):
+
+                @pl.when(steps == k)
+                def _(c=c, k=k):
+                    send_ref[c] = slots[k][c]
 
             @pl.when(steps < 0)
             def _(c=c):
-                out_ref[c] = jnp.zeros_like(x1_ref)
-
+                send_ref[c] = jnp.zeros_like(x1_ref)
+
+    @pl.when(info[0] == 1)
+    def _():
+        send_ref[0] = x1_ref[...]
+        for c in range(1, WCAP):
+            send_ref[c] = jnp.zeros_like(x1_ref)
+
+
+def acts_kernel(x_count, info, plan, x1_ref, come_ref, *refs):
+    slots, (out_ref, blank, sems) = refs[:x_count], refs[x_count:]
+    half = x1_ref.shape[0]
+
+    def put(source, c, own):
+        base = own * half
+        place = out_ref.at[c, pl.ds(base, half), :]
+        return pltpu.make_async_copy(source, place, sems.at[c * 2 + own])
+
+    blank[...] = jnp.zeros_like(blank)
+
+    @pl.when(info[0] == 0)
+    def _():
+        put(x1_ref, 0, 0).start()
+        for c in range(1, WCAP):
+            put(blank, c, 0).start()
+        for c in range(WCAP):
+            put(come_ref.at[c], c, 1).start()
+
+    @pl.when(info[0] == 1)
+    def _():
+        for c in range(WCAP):
+            put(come_ref.at[c], c, 0).start()
+            steps = plan[x_count * WCAP + c]
             for k in range(x_count):
 
                 @pl.when(steps == k)
                 def _(c=c, k=k):
-                    out_ref[c] = slots[k][c]
-
-    def entry(out_ref):
-        out_ref[0] = x1_ref[...]
-        for c in range(1, WCAP):
-            out_ref[c] = jnp.zeros_like(x1_ref)
-
-    @pl.when(info[0] == 0)
-    def _():
-        entry(keep_ref)
-        place(send_ref)
-
-    @pl.when(info[0] == 1)
-    def _():
-        place(keep_ref)
-        entry(send_ref)
-
-
-def acts_kernel(info, keep_ref, come_ref, out_ref):
-    half = keep_ref.shape[1]
-
-    @pl.when(info[0] == 0)
-    def _():
-        out_ref[:, :half] = keep_ref[...]
-        out_ref[:, half:] = come_ref[...]
-
-    @pl.when(info[0] == 1)
-    def _():
-        out_ref[:, :half] = come_ref[...]
-        out_ref[:, half:] = keep_ref[...]
+                    put(slots[k].at[c], c, 1).start()
+
+            @pl.when(steps < 0)
+            def _(c=c):
+                put(blank, c, 1).start()
+
+    for c in range(WCAP):
+        for own in range(2):
+            put(blank, c, own).wait()
 
 
 def on_device(x_count, z_count, inputs, weights, wiring, lengths, targets):
@@ -339,47 +363,49 @@
     rows = feat // replicas
     loss_scale = 1.0 / math.sqrt(replicas * tokens)
 
-    def swap(value):
-        return lax.ppermute(value, "section", [(0, 1), (1, 0)])
-
-    def tp_move(value, k):
-        return lax.ppermute(value, "tp", [(y, (y + k) % tp_count) for y in range(tp_count)])
-
-    def x_move(value, k):
+    def swap(value, label):
+        with jax.named_scope(label):
+            return lax.ppermute(value, "section", [(0, 1), (1, 0)])
+
+    def tp_move(value, k, label):
+        pairs = [(y, (y + k) % tp_count) for y in range(tp_count)]
+        with jax.named_scope(label):
+            return lax.ppermute(value, "tp", pairs)
+
+    def x_move(value, k, label):
         pairs = [
             (z * x_count + x, z * x_count + (x + k) % x_count)
             for z in range(z_count)
             for x in range(x_count)
         ]
-        return lax.ppermute(value, "rep", pairs)
-
-    def z_move(value, k):
+        with jax.named_scope(label):
+            return lax.ppermute(value, "rep", pairs)
+
+    def z_move(value, k, label):
         pairs = [
             (z * x_count + x, ((z + k) % z_count) * x_count + x)
             for z in range(z_count)
             for x in range(x_count)
         ]
-        return lax.ppermute(value, "rep", pairs)
+        with jax.named_scope(label):
+            return lax.ppermute(value, "rep", pairs)
 
     def shape(*dims, dtype=BF):
         return jax.ShapeDtypeStruct(dims, dtype)
 
     flops = 2 * half * feat * width
-    other_weight = swap(weight)
+    other_weight = swap(weight, "swap_weight")
     plan = pl.pallas_call(
-        functools.partial(table_kernel, x_count, z_count),
+        functools.partial(plan_kernel, x_count, z_count),
         out_shape=shape(x_count * WCAP + WCAP, dtype=jnp.int32),
         in_specs=[SM, SM, VM],
         out_specs=SM,
-        scratch_shapes=[
-            pltpu.SMEM((replicas * WCAP,), jnp.int32),
-            pltpu.SMEM((replicas,), jnp.int32),
-        ],
-        name="table",
+        scratch_shapes=[pltpu.SMEM((x_count,), jnp.int32)],
+        name="plan",
         compiler_params=pltpu.CompilerParams(vmem_limit_bytes=VMEM_LIMIT),
     )(info, wiring, weight)
     x0 = lax.dynamic_slice(inputs.reshape(tokens, width), (section * half, 0), (half, width))
-    first_blocks = [x0] + [tp_move(x0, k) for k in range(1, tp_count)]
+    first_blocks = [x0] + [tp_move(x0, k, "gather_x0") for k in range(1, tp_count)]
     x1, mixed, scale = call(
         functools.partial(first_kernel, tp_count, feat),
         (shape(half, width), shape(half, width, dtype=F32), shape(half, 128, dtype=F32)),
@@ -388,7 +414,7 @@
         flops=flops,
         nbytes=2 * feat * width,
     )(info, plan, *first_blocks, weight, other_weight)
-    second_blocks = [x1] + [tp_move(x1, k) for k in range(1, tp_count)]
+    second_blocks = [x1] + [tp_move(x1, k, "gather_x1") for k in range(1, tp_count)]
     x2, delta1, packed, *back = call(
         functools.partial(second_kernel, tp_count, feat, loss_scale),
         (shape(half, width), shape(half, width), shape(half, feat))
@@ -398,11 +424,8 @@
         flops=2 * flops,
         nbytes=2 * feat * width,
     )(info, lengths, *first_blocks, *second_blocks, weight, other_weight, goal)
-    back_blocks = [back[0]] + [tp_move(back[k], tp_count - k) for k in range(1, tp_count)]
-    far = [x2, z_move(x2, 3), z_move(x2, z_count - 3)]
-    trio = call(stack_kernel, shape(3, half, width), [VM] * 3, "trio")(*far)
-    near = [trio, z_move(trio, 1), z_move(trio, z_count - 1)]
-    other_pack = swap(packed)
+    back_blocks = [back[0]] + [tp_move(back[k], tp_count - k, "sum_back") for k in range(1, tp_count)]
+    other_pack = swap(packed, "swap_rows")
     *turned, slope = call(
         functools.partial(turn_kernel, tp_count, x_count),
         (shape(feat // x_count, tokens),) * x_count + (shape(half, width, dtype=F32),),
@@ -412,35 +435,27 @@
         flops=flops // 4,
         nbytes=2 * feat * tokens,
     )(info, *first_blocks, *second_blocks, other_pack, mixed, scale)
-    lefts = [turned[0]] + [x_move(turned[k], k) for k in range(1, x_count)]
+    far = [x2, z_move(x2, 3, "route_far"), z_move(x2, z_count - 3, "route_far")]
+    lefts = [turned[0]] + [x_move(turned[k], k, "spread_rows") for k in range(1, x_count)]
     keep, send = call(
         functools.partial(delta_kernel, tp_count),
-        (shape(half, width),) * 2,
+        (shape(half, width), shape(half, width)),
         [SM] + [VM] * (tp_count + 2),
         "delta",
         flops=half * width,
         nbytes=8 * half * width,
     )(info, *back_blocks, slope, delta1)
-    come = swap(send)
-    delta = call(join_kernel, shape(tokens, width), [VM, VM], "join")(keep, come)
-    rights = [delta] + [x_move(delta, k) for k in range(1, x_count)]
-    chunk = shape(rows, width)
-    own, plus, minus, far_part, wide_part = call(
-        functools.partial(part_kernel, x_count, z_count),
-        (chunk, shape(3, rows, width), shape(2, rows, width), chunk, chunk),
-        [SM] + [VM] * (2 * x_count),
-        "part",
-        scratch=[pltpu.VMEM((z_count, rows, width), BF)],
-        flops=2 * flops,
-        nbytes=4 * feat * tokens,
-    )(info, *lefts, *rights)
-    plus, minus = z_move(plus, 1), z_move(minus, z_count - 1)
-    up, down = call(middle_kernel, (chunk, chunk), [VM] * 4, "middle")(
-        plus, minus, far_part, wide_part
-    )
-    grad_rows = call(sum_kernel, shape(rows, width, dtype=F32), [VM] * 5, "sum")(
-        own, plus, minus, z_move(up, 3), z_move(down, z_count - 3)
-    )
+    come = swap(send, "swap_delta")
+    delta = call(join_kernel, shape(tokens, width), [VM] * (4 + x_count), "join")(
+        keep, come, *far, *lefts[1:]
+    )
+    rights = [delta] + [x_move(delta, k, "gather_delta") for k in range(1, x_count)]
+    trio = call(trio_kernel, shape(3, half, width), [VM] * 4, "trio")(*far, rights[1])
+    near = [
+        trio,
+        z_move(trio, 1, "route_near"),
+        z_move(trio, z_count - 1, "route_near"),
+    ]
     pair = shape(WCAP, half, width)
     slots = call(
         functools.partial(route_kernel, x_count, z_count),
@@ -449,17 +464,45 @@
         "route",
         nbytes=2 * z_count * half * width,
     )(plan, *near)
-    arrived = [slots[0]] + [x_move(slots[k], k) for k in range(1, x_count)]
-    held, sent = call(
+    chunk = shape(rows, width)
+    split = -(-width // 256) * 128
+    own, plus, minus, far_part, wide_part = call(
+        functools.partial(part_kernel, x_count, z_count),
+        (chunk, shape(rows, 2 * width + split), shape(rows, 3 * width - split), chunk, chunk),
+        [SM] + [VM] * (2 * x_count),
+        "part",
+        scratch=[pltpu.VMEM((z_count, rows, width), BF)],
+        flops=2 * flops,
+        nbytes=4 * feat * tokens,
+    )(info, *lefts, *rights)
+    plus, minus = z_move(plus, 1, "part_near"), z_move(minus, z_count - 1, "part_near")
+    up, down = call(middle_kernel, (chunk, chunk), [VM] * 5, "middle")(
+        plus, minus, far_part, wide_part, slots[0]
+    )
+    up, down = z_move(up, 3, "part_far"), z_move(down, z_count - 3, "part_far")
+    arrived = [slots[0]] + [x_move(slots[k], k, "route_x") for k in range(1, x_count)]
+    sent = call(
         functools.partial(pick_kernel, x_count),
-        (pair, pair),
-        [SM, SM] + [VM] * (x_count + 1),
+        pair,
+        [SM, SM] + [VM] * (x_count + 3),
         "pick",
         nbytes=2 * z_count * half * width,
-    )(info, plan, x1, *arrived)
-    acts = call(acts_kernel, shape(WCAP, tokens, width), [SM, VM, VM], "acts")(
-        info, held, swap(sent)
-    )
+    )(info, plan, x1, *arrived, up, down)
+    grad_rows = call(sum_kernel, shape(rows, width, dtype=F32), [VM] * 6, "sum")(
+        own, plus, minus, up, down, sent
+    )
+    acts = pl.pallas_call(
+        functools.partial(acts_kernel, x_count),
+        out_shape=shape(WCAP, tokens, width),
+        in_specs=[SM, SM] + [VM] * (x_count + 2),
+        out_specs=pl.BlockSpec(memory_space=pl.ANY),
+        scratch_shapes=[
+            pltpu.VMEM((half, width), BF),
+            pltpu.SemaphoreType.DMA((2 * WCAP,)),
+        ],
+        name="acts",
+        compiler_params=pltpu.CompilerParams(vmem_limit_bytes=VMEM_LIMIT),
+    )(info, plan, x1, swap(sent, "swap_acts"), *arrived)
     return (
         acts.reshape(1, 1, 1, WCAP, tokens, width),
         grad_rows.reshape(1, rows, width),

time: 95 us -> 87.8 us (0.924)
  waiting for transfers between devices: 39.1 us -> 22.6 us
  starting transfers between devices: 39 us -> 48.5 us
    ppermute x9, waiting for transfers between devices: 13.8 us -> 5.26 us  [x_move(): return lax.ppermute(value, 'rep', pairs)]
    ppermute x4, starting transfers between devices: 9.19 us -> 16.4 us  [swap(): return lax.ppermute(value, 'section', [(0, 1), (1, 0)])]
    ppermute x9, waiting for transfers between devices: 10.5 us -> 5.97 us  [tp_move(): return lax.ppermute(value, 'tp', pairs)]
    ppermute x8, waiting for transfers between devices: 14.8 us -> 11.1 us  [z_move(): return lax.ppermute(value, 'rep', pairs)]
    ppermute x9, starting transfers between devices: 8.11 us -> 10.4 us  [x_move(): return lax.ppermute(value, 'rep', pairs)]
  transfers between devices with their start and end apart: 30 -> 30, of which waited for: 13 -> 11; matrix products, arithmetic and copies ran while one was open for 0% -> 0% of each run, Pallas kernels for 8% -> 7%
where the time goes in v3:
time: 87.8 us; the launch traced here: 87.5 us
  starting transfers between devices  48.5 us (55%)
  waiting for transfers between devices  22.6 us (26%)
  Pallas kernels  12.7 us (14%)
  local copies, waits for them, and re-layouts  2.62 us (3%)
  between operations  0.99 us (1%)
    ppermute x4, starting transfers between devices, swap(): return lax.ppermute(value, 'section', [(0, 1), (1, 0)])  16.4 us
    ppermute x8, starting transfers between devices, z_move(): return lax.ppermute(value, 'rep', pairs)  15.3 us
    ppermute x8, waiting for transfers between devices, z_move(): return lax.ppermute(value, 'rep', pairs)  11.1 us
    ppermute x9, starting transfers between devices, x_move(): return lax.ppermute(value, 'rep', pairs)  10.4 us
    ppermute x9, starting transfers between devices, tp_move(): return lax.ppermute(value, 'tp', pairs)  6.35 us
    ppermute x9, waiting for transfers between devices, tp_move(): return lax.ppermute(value, 'tp', pairs)  5.97 us
    ppermute x9, waiting for transfers between devices, x_move(): return lax.ppermute(value, 'rep', pairs)  5.26 us
    pallas_call x1, Pallas kernels, on_device(): call(functools.partial(second_kernel, tp_count, feat, loss_scale), (shape...  2.74 us
  transfers between devices with their start and end apart: 30, of which 11 were waited for; matrix products, arithmetic and copies ran while one was open for 0% of the time, Pallas kernels for 7%

profile of v3, /device:TPU:1, one launch (start us, length us, event | category | flops | bytes accessed | tf_op | source)
XLA Modules:
  0.0 87.5 jit_solution(10611439403074915380)
XLA Ops:
  0.6 0.0 copy-start
  0.6 3.3 %collective-permute-start.3 = (bf16[2560,640]{1,0:T(8,128)(2,1)}, bf16[2560,640]{1,0:T(8,128)(2,1)S(1)}, u32[]{:S(2)}, u32[]{:S(2)}) collective-permute-start(bf16[2560,640]{1,0:T(8,128)(2,1)} %bitcast.9), channel_id=1, source_target_pairs={{0,128},{128,0},{1,129},{129,1},{2,130},{130,2},{3,131},{131,3},{4... | collective-permute-start | bytes 9830408 | tf_op jit(solution)/shard_map/swap_weight/ppermute | solution.py:368
  4.0 1.2 %collective-permute-start.2 = (bf16[64,640]{1,0:T(8,128)(2,1)S(1)}, bf16[64,640]{1,0:T(8,128)(2,1)}, u32[]{:S(2)}, u32[]{:S(2)}) collective-permute-start(bf16[64,640]{1,0:T(8,128)(2,1)S(1)} %dynamic-slice_bitcast_fusion.refs_0_), channel_id=1, source_target_pairs={{0,3},{1,0},{2,1},{3,2},{4,7},{5,4},{6,5},{7,6},{8,11},{9,8},{10,9... | collective-permute-start | bytes 245768 | tf_op jit(solution)/shard_map/gather_x0/ppermute | solution.py:373
  5.2 0.3 collective-permute-start.1
  5.6 0.7 collective-permute-start
  6.2 0.1 pad_add_fusion.info
  6.3 1.9 %copy-done.1 = bf16[1,2560,640]{2,1,0:T(8,128)(2,1)S(1)} copy-done((bf16[1,2560,640]{2,1,0:T(8,128)(2,1)S(1)}, bf16[1,2560,640]{2,1,0:T(8,128)(2,1)}, u32[]{:S(2)}) %copy-start.1) | copy-done | bytes 3276824
  8.3 0.7 copy-done.4
  8.9 1.6 %plan.1._ = s32[10]{0:T(128)S(1)} custom-call(s32[3]{0:T(128)S(1)} %pad_add_fusion.info, s32[1,1,32]{2,1,0:T(1,128)S(1)} %copy-done.4, bf16[2560,640]{1,0:T(8,128)(2,1)S(1)} %bitcast.10), custom_call_target="tpu_custom_call" | custom-call | tf_op jit(solution)/shard_map/plan/pallas_call | solution.py:398
  10.5 0.0 copy-start.3
  10.5 0.0 copy-start.5
  10.5 0.0 collective-permute-done.1.refs_2_
  10.5 1.8 %collective-permute-done.refs_1_ = bf16[64,640]{1,0:T(8,128)(2,1)} collective-permute-done((bf16[64,640]{1,0:T(8,128)(2,1)S(1)}, bf16[64,640]{1,0:T(8,128)(2,1)}, u32[]{:S(2)}, u32[]{:S(2)}) %collective-permute-start) | collective-permute-done | bytes 81952 | tf_op jit(solution)/shard_map/gather_x0/ppermute | solution.py:373
  12.3 0.0 collective-permute-done.3.refs_5_.refs_9_
  12.3 1.6 %first.1 = (bf16[64,640]{1,0:T(8,128)(2,1)S(1)}, f32[64,640]{1,0:T(8,128)S(1)}, f32[64,128]{1,0:T(8,128)S(1)}) custom-call(s32[3]{0:T(128)S(1)} %pad_add_fusion.info, s32[10]{0:T(128)S(1)} %plan.1._, bf16[64,640]{1,0:T(8,128)(2,1)S(1)} %dynamic-slice_bitcast_fusion.refs_0_, bf16[64,640]{1,0:T(8,128)(2,1)} %collective-permute-done.refs_1_, ...), custom_call_target="tpu_custom_call" | custom-call | flops 209715200 | bytes 3276800 | tf_op jit(solution)/shard_map/first/pallas_call | solution.py:409
  13.9 0.6 collective-permute-start.6
  14.5 1.4 %collective-permute-start.5 = (bf16[64,640]{1,0:T(8,128)(2,1)S(1)}, bf16[64,640]{1,0:T(8,128)(2,1)S(1)}, u32[]{:S(2)}, u32[]{:S(2)}) collective-permute-start(bf16[64,640]{1,0:T(8,128)(2,1)S(1)} %get-tuple-element.30.refs_4_.x1_ref), channel_id=1, source_target_pairs={{0,2},{1,3},{2,0},{3,1},{4,6},{5,7},{6,4},{7,5},{8,10},{9,11},{10,... | collective-permute-start | bytes 245768 | tf_op jit(solution)/shard_map/gather_x1/ppermute | solution.py:373
  15.9 0.3 collective-permute-start.4
  16.3 1.0 %collective-permute-done.6.refs_7_ = bf16[64,640]{1,0:T(8,128)(2,1)S(1)} collective-permute-done((bf16[64,640]{1,0:T(8,128)(2,1)S(1)}, bf16[64,640]{1,0:T(8,128)(2,1)S(1)}, u32[]{:S(2)}, u32[]{:S(2)}) %collective-permute-start.6) | collective-permute-done | bytes 81952 | tf_op jit(solution)/shard_map/gather_x1/ppermute | solution.py:373
  17.3 2.0 %collective-permute-done.5.refs_6_ = bf16[64,640]{1,0:T(8,128)(2,1)S(1)} collective-permute-done((bf16[64,640]{1,0:T(8,128)(2,1)S(1)}, bf16[64,640]{1,0:T(8,128)(2,1)S(1)}, u32[]{:S(2)}, u32[]{:S(2)}) %collective-permute-start.5) | collective-permute-done | bytes 81952 | tf_op jit(solution)/shard_map/gather_x1/ppermute | solution.py:373
  19.3 1.1 %collective-permute-done.4.refs_5_ = bf16[64,640]{1,0:T(8,128)(2,1)S(1)} collective-permute-done((bf16[64,640]{1,0:T(8,128)(2,1)S(1)}, bf16[64,640]{1,0:T(8,128)(2,1)S(1)}, u32[]{:S(2)}, u32[]{:S(2)}) %collective-permute-start.4) | collective-permute-done | bytes 81952 | tf_op jit(solution)/shard_map/gather_x1/ppermute | solution.py:373
  20.4 2.7 %second.1 = (bf16[64,640]{1,0:T(8,128)(2,1)S(1)}, bf16[64,640]{1,0:T(8,128)(2,1)S(1)}, bf16[64,2560]{1,0:T(8,128)(2,1)S(1)}, bf16[64,640]{1,0:T(8,128)(2,1)S(1)}...) custom-call(s32[3]{0:T(128)S(1)} %pad_add_fusion.info, ...), custom_call_target="tpu_custom_call" | custom-call | flops 419430400 | bytes 3276800 | tf_op jit(solution)/shard_map/second/pallas_call | solution.py:418
  23.2 3.3 %collective-permute-start.12 = (bf16[64,2560]{1,0:T(8,128)(2,1)S(1)}, bf16[64,2560]{1,0:T(8,128)(2,1)S(1)}, u32[]{:S(2)}, u32[]{:S(2)}) collective-permute-start(bf16[64,2560]{1,0:T(8,128)(2,1)S(1)} %get-tuple-element.36), channel_id=1, source_target_pairs={{0,128},{128,0},{1,129},{129,1},{2,130},{130,2},{3,131},{131,3},{4... | collective-permute-start | bytes 983048 | tf_op jit(solution)/shard_map/swap_rows/ppermute | solution.py:368
  26.5 0.4 collective-permute-start.9
  26.9 0.8 collective-permute-start.10
  27.7 0.6 collective-permute-start.11
  28.3 6.5 %collective-permute-start.8 = (bf16[64,640]{1,0:T(8,128)(2,1)S(1)}, bf16[64,640]{1,0:T(8,128)(2,1)S(1)}, u32[]{:S(2)}, u32[]{:S(2)}) collective-permute-start(bf16[64,640]{1,0:T(8,128)(2,1)S(1)} %get-tuple-element.31.refs_0_.a_ref), channel_id=1, source_target_pairs={{0,80},{4,84},{8,88},{12,92},{16,96},{20,100},{24,104},{28,108},{3... | collective-permute-start | bytes 245768 | tf_op jit(solution)/shard_map/route_far/ppermute | solution.py:391
  34.7 0.0 collective-permute-done.12.refs_8_
  34.8 1.3 %turn.1 = (bf16[640,128]{1,0:T(8,128)(2,1)S(1)}, bf16[640,128]{1,0:T(8,128)(2,1)S(1)}, bf16[640,128]{1,0:T(8,128)(2,1)S(1)}, bf16[640,128]{1,0:T(8,128)(2,1)S(1)}, f32[64,640]{1,0:T(8,128)S(1)}) custom-call(s32[3]{0:T(128)S(1)} %pad_add_fusion.info, bf16[64,640]{1,0:T(8,128)(2,1)S(1)} %dynamic-slice_bitcast_fusion.refs_0_, ...), custom_call_target="tpu_custom_call" | custom-call | flops 52428800 | bytes 655360 | tf_op jit(solution)/shard_map/turn/pallas_call | solution.py:429
  36.1 1.3 %collective-permute-start.14 = (bf16[640,128]{1,0:T(8,128)(2,1)S(1)}, bf16[640,128]{1,0:T(8,128)(2,1)S(1)}, u32[]{:S(2)}, u32[]{:S(2)}) collective-permute-start(bf16[640,128]{1,0:T(8,128)(2,1)S(1)} %get-tuple-element.43), channel_id=1, source_target_pairs={{0,4},{4,8},{8,12},{12,0},{16,20},{20,24},{24,28},{28,16},{32,36},... | collective-permute-start | bytes 491528 | tf_op jit(solution)/shard_map/spread_rows/ppermute | solution.py:382
  37.4 0.0 collective-permute-done.9.refs_1_
  37.4 2.5 %collective-permute-start.15 = (bf16[640,128]{1,0:T(8,128)(2,1)S(1)}, bf16[640,128]{1,0:T(8,128)(2,1)S(1)}, u32[]{:S(2)}, u32[]{:S(2)}) collective-permute-start(bf16[640,128]{1,0:T(8,128)(2,1)S(1)} %get-tuple-element.44), channel_id=1, source_target_pairs={{0,8},{4,12},{8,0},{12,4},{16,24},{20,28},{24,16},{28,20},{32,40},... | collective-permute-start | bytes 491528 | tf_op jit(solution)/shard_map/spread_rows/ppermute | solution.py:382
  39.8 1.1 %collective-permute-start.16 = (bf16[640,128]{1,0:T(8,128)(2,1)S(1)}, bf16[640,128]{1,0:T(8,128)(2,1)S(1)}, u32[]{:S(2)}, u32[]{:S(2)}) collective-permute-start(bf16[640,128]{1,0:T(8,128)(2,1)S(1)} %get-tuple-element.45), channel_id=1, source_target_pairs={{0,12},{4,0},{8,4},{12,8},{16,28},{20,16},{24,20},{28,24},{32,44},... | collective-permute-start | bytes 491528 | tf_op jit(solution)/shard_map/spread_rows/ppermute | solution.py:382
  41.0 0.6 delta.1
  41.6 0.0 collective-permute-done.8.refs_2_.c_ref
  41.6 2.1 %collective-permute-start.13 = (bf16[64,640]{1,0:T(8,128)(2,1)S(1)}, bf16[64,640]{1,0:T(8,128)(2,1)S(1)}, u32[]{:S(2)}, u32[]{:S(2)}) collective-permute-start(bf16[64,640]{1,0:T(8,128)(2,1)S(1)} %get-tuple-element.42), channel_id=1, source_target_pairs={{0,128},{128,0},{1,129},{129,1},{2,130},{130,2},{3,131},{131,3},{4... | collective-permute-start | bytes 245768 | tf_op jit(solution)/shard_map/swap_delta/ppermute | solution.py:368
  43.7 5.1 %collective-permute-done.7.refs_1_.b_ref = bf16[64,640]{1,0:T(8,128)(2,1)S(1)} collective-permute-done((bf16[64,640]{1,0:T(8,128)(2,1)S(1)}, bf16[64,640]{1,0:T(8,128)(2,1)S(1)}, u32[]{:S(2)}, u32[]{:S(2)}) %collective-permute-start.7) | collective-permute-done | bytes 81952 | tf_op jit(solution)/shard_map/route_far/ppermute | solution.py:391
  48.8 0.0 collective-permute-done.14.refs_3_.refs_1_
  48.8 0.0 collective-permute-done.15.refs_4_.refs_2_
  48.8 0.0 collective-permute-done.16.refs_5_.refs_3_
  48.8 0.8 collective-permute-start.17
  49.6 2.0 %collective-permute-start.24 = (bf16[128,640]{1,0:T(8,128)(2,1)S(1)}, bf16[128,640]{1,0:T(8,128)(2,1)S(1)}, u32[]{:S(2)}, u32[]{:S(2)}) collective-permute-start(bf16[128,640]{1,0:T(8,128)(2,1)S(1)} %join.1.refs_4_), channel_id=1, source_target_pairs={{0,12},{4,0},{8,4},{12,8},{16,28},{20,16},{24,20},{28,24},{32,44},... | collective-permute-start | bytes 491528 | tf_op jit(solution)/shard_map/gather_delta/ppermute | solution.py:382
  51.6 2.7 %collective-permute-done.17._.refs_5_ = bf16[128,640]{1,0:T(8,128)(2,1)S(1)} collective-permute-done((bf16[128,640]{1,0:T(8,128)(2,1)S(1)}, bf16[128,640]{1,0:T(8,128)(2,1)S(1)}, u32[]{:S(2)}, u32[]{:S(2)}) %collective-permute-start.17) | collective-permute-done | bytes 163872 | tf_op jit(solution)/shard_map/gather_delta/ppermute | solution.py:382
  54.3 0.1 collective-permute-start.19
  54.4 1.5 %collective-permute-start.18 = (bf16[3,64,640]{2,1,0:T(8,128)(2,1)S(1)}, bf16[3,64,640]{2,1,0:T(8,128)(2,1)S(1)}, u32[]{:S(2)}, u32[]{:S(2)}) collective-permute-start(bf16[3,64,640]{2,1,0:T(8,128)(2,1)S(1)} %trio.1.refs_0_), channel_id=1, source_target_pairs={{0,16},{4,20},{8,24},{12,28},{16,32},{20,36},{24,40},{28,44},{32,4... | collective-permute-start | bytes 737288 | tf_op jit(solution)/shard_map/route_near/ppermute | solution.py:391
  55.8 2.5 %collective-permute-done.23.refs_6_ = bf16[128,640]{1,0:T(8,128)(2,1)S(1)} collective-permute-done((bf16[128,640]{1,0:T(8,128)(2,1)S(1)}, bf16[128,640]{1,0:T(8,128)(2,1)S(1)}, u32[]{:S(2)}, u32[]{:S(2)}) %collective-permute-start.23) | collective-permute-done | bytes 163872 | tf_op jit(solution)/shard_map/gather_delta/ppermute | solution.py:382
  58.4 1.3 %part.1 = (bf16[80,640]{1,0:T(8,128)(2,1)S(1)}, bf16[80,1664]{1,0:T(8,128)(2,1)S(1)}, bf16[80,1536]{1,0:T(8,128)(2,1)S(1)}, bf16[80,640]{1,0:T(8,128)(2,1)S(1)}, bf16[80,640]{1,0:T(8,128)(2,1)S(1)}) custom-call(s32[3]{0:T(128)S(1)} %pad_add_fusion.info, bf16[640,128]{1,0:T(8,128)(2,1)S(1)} %get-tuple-element.50.refs_0_, ...), custom_call_target="tpu_custom_call" | custom-call | flops 419430400 | bytes 1310720 | tf_op jit(solution)/shard_map/part/pallas_call | solution.py:469
  59.7 0.3 collective-permute-start.25
  60.0 2.4 %collective-permute-start.26 = (bf16[80,1536]{1,0:T(8,128)(2,1)S(1)}, bf16[80,1536]{1,0:T(8,128)(2,1)S(1)}, u32[]{:S(2)}, u32[]{:S(2)}) collective-permute-start(bf16[80,1536]{1,0:T(8,128)(2,1)S(1)} %get-tuple-element.52), channel_id=1, source_target_pairs={{0,112},{4,116},{8,120},{12,124},{16,0},{20,4},{24,8},{28,12},{32,... | collective-permute-start | bytes 737288 | tf_op jit(solution)/shard_map/part_near/ppermute | solution.py:391
  62.4 0.9 route.1
  63.3 0.1 collective-permute-start.20
  63.4 1.5 %collective-permute-start.21 = (bf16[2,64,640]{2,1,0:T(8,128)(2,1)S(1)}, bf16[2,64,640]{2,1,0:T(8,128)(2,1)S(1)}, u32[]{:S(2)}, u32[]{:S(2)}) collective-permute-start(bf16[2,64,640]{2,1,0:T(8,128)(2,1)S(1)} %get-tuple-element.48), channel_id=1, source_target_pairs={{0,8},{4,12},{8,0},{12,4},{16,24},{20,28},{24,16},{28,20},{32,40},... | collective-permute-start | bytes 491528 | tf_op jit(solution)/shard_map/route_x/ppermute | solution.py:382
  64.9 1.2 %collective-permute-start.22 = (bf16[2,64,640]{2,1,0:T(8,128)(2,1)S(1)}, bf16[2,64,640]{2,1,0:T(8,128)(2,1)S(1)}, u32[]{:S(2)}, u32[]{:S(2)}) collective-permute-start(bf16[2,64,640]{2,1,0:T(8,128)(2,1)S(1)} %get-tuple-element.49), channel_id=1, source_target_pairs={{0,12},{4,0},{8,4},{12,8},{16,28},{20,16},{24,20},{28,24},{32,44},... | collective-permute-start | bytes 491528 | tf_op jit(solution)/shard_map/route_x/ppermute | solution.py:382
  66.1 1.5 %collective-permute-done.26.minus_ref = bf16[80,1536]{1,0:T(8,128)(2,1)S(1)} collective-permute-done((bf16[80,1536]{1,0:T(8,128)(2,1)S(1)}, bf16[80,1536]{1,0:T(8,128)(2,1)S(1)}, u32[]{:S(2)}, u32[]{:S(2)}) %collective-permute-start.26) | collective-permute-done | bytes 245792 | tf_op jit(solution)/shard_map/part_near/ppermute | solution.py:391
  67.6 1.0 %collective-permute-done.25.plus_ref = bf16[80,1664]{1,0:T(8,128)(2,1)S(1)} collective-permute-done((bf16[80,1664]{1,0:T(8,128)(2,1)S(1)}, bf16[80,1664]{1,0:T(8,128)(2,1)S(1)}, u32[]{:S(2)}, u32[]{:S(2)}) %collective-permute-start.25) | collective-permute-done | bytes 266272 | tf_op jit(solution)/shard_map/part_near/ppermute | solution.py:391
  68.6 0.1 middle.1
  68.6 1.1 %collective-permute-start.27 = (bf16[80,640]{1,0:T(8,128)(2,1)S(1)}, bf16[80,640]{1,0:T(8,128)(2,1)S(1)}, u32[]{:S(2)}, u32[]{:S(2)}) collective-permute-start(bf16[80,640]{1,0:T(8,128)(2,1)S(1)} %get-tuple-element.55), channel_id=1, source_target_pairs={{0,48},{4,52},{8,56},{12,60},{16,64},{20,68},{24,72},{28,76},{32,8... | collective-permute-start | bytes 307208 | tf_op jit(solution)/shard_map/part_far/ppermute | solution.py:391
  69.8 3.4 %collective-permute-start.28 = (bf16[80,640]{1,0:T(8,128)(2,1)S(1)}, bf16[80,640]{1,0:T(8,128)(2,1)S(1)}, u32[]{:S(2)}, u32[]{:S(2)}) collective-permute-start(bf16[80,640]{1,0:T(8,128)(2,1)S(1)} %get-tuple-element.56), channel_id=1, source_target_pairs={{0,80},{4,84},{8,88},{12,92},{16,96},{20,100},{24,104},{28,108},{3... | collective-permute-start | bytes 307208 | tf_op jit(solution)/shard_map/part_far/ppermute | solution.py:391
  73.2 3.5 %collective-permute-done.27.refs_4_.up_ref = bf16[80,640]{1,0:T(8,128)(2,1)S(1)} collective-permute-done((bf16[80,640]{1,0:T(8,128)(2,1)S(1)}, bf16[80,640]{1,0:T(8,128)(2,1)S(1)}, u32[]{:S(2)}, u32[]{:S(2)}) %collective-permute-start.27) | collective-permute-done | bytes 102432 | tf_op jit(solution)/shard_map/part_far/ppermute | solution.py:391
  76.7 0.6 pick.1._
  77.3 7.7 %collective-permute-start.29 = (bf16[2,64,640]{2,1,0:T(8,128)(2,1)S(1)}, bf16[2,64,640]{2,1,0:T(8,128)(2,1)S(1)}, u32[]{:S(2)}, u32[]{:S(2)}) collective-permute-start(bf16[2,64,640]{2,1,0:T(8,128)(2,1)S(1)} %pick.1._), channel_id=1, source_target_pairs={{0,128},{128,0},{1,129},{129,1},{2,130},{130,2},{3,131},{131,3},{4... | collective-permute-start | bytes 491528 | tf_op jit(solution)/shard_map/swap_acts/ppermute | solution.py:368
  85.0 0.7 sum.1
  85.7 0.3 collective-permute-done.29.come_ref
  86.0 1.3 %acts.1 = bf16[2,128,640]{2,1,0:T(8,128)(2,1)} custom-call(s32[3]{0:T(128)S(1)} %pad_add_fusion.info, s32[10]{0:T(128)S(1)} %plan.1._, bf16[64,640]{1,0:T(8,128)(2,1)S(1)} %get-tuple-element.30.refs_4_.x1_ref, bf16[2,64,640]{2,1,0:T(8,128)(2,1)S(1)} %collective-permute-done.29.come_ref, bf16[2,64,640]{2,1,0:T(8,128)(2,1)S(1)} %get-tuple-element.46._.refs_0_, ...), custom_call_target="tpu_custom_call" | custom-call | tf_op jit(solution)/shard_map/acts/pallas_call | solution.py:494
  (23 shorter events, 0.1 us)
Async XLA Ops:
  0.6 3.3 %copy-start = (bf16[1,1,128,640]{3,2,1,0:T(8,128)(2,1)S(1)}, bf16[1,1,128,640]{3,2,1,0:T(8,128)(2,1)}, u32[]{:S(2)}) copy-start(bf16[1,1,128,640]{3,2,1,0:T(8,128)(2,1)} %param.5) | copy-start | bytes 491524
  0.6 11.7 %collective-permute-start.3 = (bf16[2560,640]{1,0:T(8,128)(2,1)}, bf16[2560,640]{1,0:T(8,128)(2,1)S(1)}, u32[]{:S(2)}, u32[]{:S(2)}) collective-permute-start(bf16[2560,640]{1,0:T(8,128)(2,1)} %bitcast.9), channel_id=1, source_target_pairs={{0,128},{128,0},{1,129},{129,1},{2,130},{130,2},{3,131},{131,3},{4... | collective-permute-start | bytes 9830408 | tf_op jit(solution)/shard_map/swap_weight/ppermute | solution.py:368
  4.0 6.5 %collective-permute-start.2 = (bf16[64,640]{1,0:T(8,128)(2,1)S(1)}, bf16[64,640]{1,0:T(8,128)(2,1)}, u32[]{:S(2)}, u32[]{:S(2)}) collective-permute-start(bf16[64,640]{1,0:T(8,128)(2,1)S(1)} %dynamic-slice_bitcast_fusion.refs_0_), channel_id=1, source_target_pairs={{0,3},{1,0},{2,1},{3,2},{4,7},{5,4},{6,5},{7,6},{8,11},{9,8},{10,9... | collective-permute-start | bytes 245768 | tf_op jit(solution)/shard_map/gather_x0/ppermute | solution.py:373
  5.2 5.3 %collective-permute-start.1 = (bf16[64,640]{1,0:T(8,128)(2,1)S(1)}, bf16[64,640]{1,0:T(8,128)(2,1)}, u32[]{:S(2)}, u32[]{:S(2)}) collective-permute-start(bf16[64,640]{1,0:T(8,128)(2,1)S(1)} %dynamic-slice_bitcast_fusion.refs_0_), channel_id=1, source_target_pairs={{0,2},{1,3},{2,0},{3,1},{4,6},{5,7},{6,4},{7,5},{8,10},{9,11},{10,... | collective-permute-start | bytes 245768 | tf_op jit(solution)/shard_map/gather_x0/ppermute | solution.py:373
  5.6 6.7 %collective-permute-start = (bf16[64,640]{1,0:T(8,128)(2,1)S(1)}, bf16[64,640]{1,0:T(8,128)(2,1)}, u32[]{:S(2)}, u32[]{:S(2)}) collective-permute-start(bf16[64,640]{1,0:T(8,128)(2,1)S(1)} %dynamic-slice_bitcast_fusion.refs_0_), channel_id=1, source_target_pairs={{0,1},{1,2},{2,3},{3,0},{4,5},{5,6},{6,7},{7,4},{8,9},{9,10},{10,1... | collective-permute-start | bytes 245768 | tf_op jit(solution)/shard_map/gather_x0/ppermute | solution.py:373
  6.3 1.9 %copy-start.1 = (bf16[1,2560,640]{2,1,0:T(8,128)(2,1)S(1)}, bf16[1,2560,640]{2,1,0:T(8,128)(2,1)}, u32[]{:S(2)}) copy-start(bf16[1,2560,640]{2,1,0:T(8,128)(2,1)} %param.6) | copy-start | bytes 9830404
  8.2 0.7 copy-start.4
  8.9 3.4 %copy-start.2 = (bf16[1,2560,640]{2,1,0:T(8,128)(2,1)S(1)}, bf16[1,2560,640]{2,1,0:T(8,128)(2,1)}, u32[]{:S(2)}) copy-start(bf16[1,2560,640]{2,1,0:T(8,128)(2,1)} %param.6) | copy-start | bytes 9830404
  10.5 10.0 %copy-start.3 = (bf16[1,1,128,640]{3,2,1,0:T(8,128)(2,1)S(1)}, bf16[1,1,128,640]{3,2,1,0:T(8,128)(2,1)}, u32[]{:S(2)}) copy-start(bf16[1,1,128,640]{3,2,1,0:T(8,128)(2,1)} %param.9) | copy-start | bytes 491524
  10.5 10.0 %copy-start.5 = (s32[1,32]{1,0:T(1,128)S(1)}, s32[1,32]{1,0:T(1,128)}, u32[]{:S(2)}) copy-start(s32[1,32]{1,0:T(1,128)} %lengths.1) | copy-start | bytes 388
  13.9 3.4 %collective-permute-start.6 = (bf16[64,640]{1,0:T(8,128)(2,1)S(1)}, bf16[64,640]{1,0:T(8,128)(2,1)S(1)}, u32[]{:S(2)}, u32[]{:S(2)}) collective-permute-start(bf16[64,640]{1,0:T(8,128)(2,1)S(1)} %get-tuple-element.30.refs_4_.x1_ref), channel_id=1, source_target_pairs={{0,3},{1,0},{2,1},{3,2},{4,7},{5,4},{6,5},{7,6},{8,11},{9,8},{10,9... | collective-permute-start | bytes 245768 | tf_op jit(solution)/shard_map/gather_x1/ppermute | solution.py:373
  14.5 4.8 %collective-permute-start.5 = (bf16[64,640]{1,0:T(8,128)(2,1)S(1)}, bf16[64,640]{1,0:T(8,128)(2,1)S(1)}, u32[]{:S(2)}, u32[]{:S(2)}) collective-permute-start(bf16[64,640]{1,0:T(8,128)(2,1)S(1)} %get-tuple-element.30.refs_4_.x1_ref), channel_id=1, source_target_pairs={{0,2},{1,3},{2,0},{3,1},{4,6},{5,7},{6,4},{7,5},{8,10},{9,11},{10,... | collective-permute-start | bytes 245768 | tf_op jit(solution)/shard_map/gather_x1/ppermute | solution.py:373
  15.9 4.5 %collective-permute-start.4 = (bf16[64,640]{1,0:T(8,128)(2,1)S(1)}, bf16[64,640]{1,0:T(8,128)(2,1)S(1)}, u32[]{:S(2)}, u32[]{:S(2)}) collective-permute-start(bf16[64,640]{1,0:T(8,128)(2,1)S(1)} %get-tuple-element.30.refs_4_.x1_ref), channel_id=1, source_target_pairs={{0,1},{1,2},{2,3},{3,0},{4,5},{5,6},{6,7},{7,4},{8,9},{9,10},{10,1... | collective-permute-start | bytes 245768 | tf_op jit(solution)/shard_map/gather_x1/ppermute | solution.py:373
  23.2 11.6 %collective-permute-start.12 = (bf16[64,2560]{1,0:T(8,128)(2,1)S(1)}, bf16[64,2560]{1,0:T(8,128)(2,1)S(1)}, u32[]{:S(2)}, u32[]{:S(2)}) collective-permute-start(bf16[64,2560]{1,0:T(8,128)(2,1)S(1)} %get-tuple-element.36), channel_id=1, source_target_pairs={{0,128},{128,0},{1,129},{129,1},{2,130},{130,2},{3,131},{131,3},{4... | collective-permute-start | bytes 983048 | tf_op jit(solution)/shard_map/swap_rows/ppermute | solution.py:368
  26.5 10.8 %collective-permute-start.9 = (bf16[64,640]{1,0:T(8,128)(2,1)S(1)}, bf16[64,640]{1,0:T(8,128)(2,1)S(1)}, u32[]{:S(2)}, u32[]{:S(2)}) collective-permute-start(bf16[64,640]{1,0:T(8,128)(2,1)S(1)} %get-tuple-element.33), channel_id=1, source_target_pairs={{0,3},{1,0},{2,1},{3,2},{4,7},{5,4},{6,5},{7,6},{8,11},{9,8},{10,9... | collective-permute-start | bytes 245768 | tf_op jit(solution)/shard_map/sum_back/ppermute | solution.py:373
  26.9 12.9 %collective-permute-start.10 = (bf16[64,640]{1,0:T(8,128)(2,1)S(1)}, bf16[64,640]{1,0:T(8,128)(2,1)S(1)}, u32[]{:S(2)}, u32[]{:S(2)}) collective-permute-start(bf16[64,640]{1,0:T(8,128)(2,1)S(1)} %get-tuple-element.34), channel_id=1, source_target_pairs={{0,2},{1,3},{2,0},{3,1},{4,6},{5,7},{6,4},{7,5},{8,10},{9,11},{10,... | collective-permute-start | bytes 245768 | tf_op jit(solution)/shard_map/sum_back/ppermute | solution.py:373
  27.7 13.3 %collective-permute-start.11 = (bf16[64,640]{1,0:T(8,128)(2,1)S(1)}, bf16[64,640]{1,0:T(8,128)(2,1)S(1)}, u32[]{:S(2)}, u32[]{:S(2)}) collective-permute-start(bf16[64,640]{1,0:T(8,128)(2,1)S(1)} %get-tuple-element.35), channel_id=1, source_target_pairs={{0,1},{1,2},{2,3},{3,0},{4,5},{5,6},{6,7},{7,4},{8,9},{9,10},{10,1... | collective-permute-start | bytes 245768 | tf_op jit(solution)/shard_map/sum_back/ppermute | solution.py:373
  28.3 13.3 %collective-permute-start.8 = (bf16[64,640]{1,0:T(8,128)(2,1)S(1)}, bf16[64,640]{1,0:T(8,128)(2,1)S(1)}, u32[]{:S(2)}, u32[]{:S(2)}) collective-permute-start(bf16[64,640]{1,0:T(8,128)(2,1)S(1)} %get-tuple-element.31.refs_0_.a_ref), channel_id=1, source_target_pairs={{0,80},{4,84},{8,88},{12,92},{16,96},{20,100},{24,104},{28,108},{3... | collective-permute-start | bytes 245768 | tf_op jit(solution)/shard_map/route_far/ppermute | solution.py:391
  36.1 12.7 %collective-permute-start.14 = (bf16[640,128]{1,0:T(8,128)(2,1)S(1)}, bf16[640,128]{1,0:T(8,128)(2,1)S(1)}, u32[]{:S(2)}, u32[]{:S(2)}) collective-permute-start(bf16[640,128]{1,0:T(8,128)(2,1)S(1)} %get-tuple-element.43), channel_id=1, source_target_pairs={{0,4},{4,8},{8,12},{12,0},{16,20},{20,24},{24,28},{28,16},{32,36},... | collective-permute-start | bytes 491528 | tf_op jit(solution)/shard_map/spread_rows/ppermute | solution.py:382
  37.4 11.4 %collective-permute-start.15 = (bf16[640,128]{1,0:T(8,128)(2,1)S(1)}, bf16[640,128]{1,0:T(8,128)(2,1)S(1)}, u32[]{:S(2)}, u32[]{:S(2)}) collective-permute-start(bf16[640,128]{1,0:T(8,128)(2,1)S(1)} %get-tuple-element.44), channel_id=1, source_target_pairs={{0,8},{4,12},{8,0},{12,4},{16,24},{20,28},{24,16},{28,20},{32,40},... | collective-permute-start | bytes 491528 | tf_op jit(solution)/shard_map/spread_rows/ppermute | solution.py:382
  39.8 9.0 %collective-permute-start.16 = (bf16[640,128]{1,0:T(8,128)(2,1)S(1)}, bf16[640,128]{1,0:T(8,128)(2,1)S(1)}, u32[]{:S(2)}, u32[]{:S(2)}) collective-permute-start(bf16[640,128]{1,0:T(8,128)(2,1)S(1)} %get-tuple-element.45), channel_id=1, source_target_pairs={{0,12},{4,0},{8,4},{12,8},{16,28},{20,16},{24,20},{28,24},{32,44},... | collective-permute-start | bytes 491528 | tf_op jit(solution)/shard_map/spread_rows/ppermute | solution.py:382
  41.0 7.8 %collective-permute-start.7 = (bf16[64,640]{1,0:T(8,128)(2,1)S(1)}, bf16[64,640]{1,0:T(8,128)(2,1)S(1)}, u32[]{:S(2)}, u32[]{:S(2)}) collective-permute-start(bf16[64,640]{1,0:T(8,128)(2,1)S(1)} %get-tuple-element.31.refs_0_.a_ref), channel_id=1, source_target_pairs={{0,48},{4,52},{8,56},{12,60},{16,64},{20,68},{24,72},{28,76},{32,8... | collective-permute-start | bytes 245768 | tf_op jit(solution)/shard_map/route_far/ppermute | solution.py:391
  41.6 7.2 %collective-permute-start.13 = (bf16[64,640]{1,0:T(8,128)(2,1)S(1)}, bf16[64,640]{1,0:T(8,128)(2,1)S(1)}, u32[]{:S(2)}, u32[]{:S(2)}) collective-permute-start(bf16[64,640]{1,0:T(8,128)(2,1)S(1)} %get-tuple-element.42), channel_id=1, source_target_pairs={{0,128},{128,0},{1,129},{129,1},{2,130},{130,2},{3,131},{131,3},{4... | collective-permute-start | bytes 245768 | tf_op jit(solution)/shard_map/swap_delta/ppermute | solution.py:368
  48.8 5.5 %collective-permute-start.17 = (bf16[128,640]{1,0:T(8,128)(2,1)S(1)}, bf16[128,640]{1,0:T(8,128)(2,1)S(1)}, u32[]{:S(2)}, u32[]{:S(2)}) collective-permute-start(bf16[128,640]{1,0:T(8,128)(2,1)S(1)} %join.1.refs_4_), channel_id=1, source_target_pairs={{0,4},{4,8},{8,12},{12,0},{16,20},{20,24},{24,28},{28,16},{32,36},... | collective-permute-start | bytes 491528 | tf_op jit(solution)/shard_map/gather_delta/ppermute | solution.py:382
  49.6 6.3 %collective-permute-start.24 = (bf16[128,640]{1,0:T(8,128)(2,1)S(1)}, bf16[128,640]{1,0:T(8,128)(2,1)S(1)}, u32[]{:S(2)}, u32[]{:S(2)}) collective-permute-start(bf16[128,640]{1,0:T(8,128)(2,1)S(1)} %join.1.refs_4_), channel_id=1, source_target_pairs={{0,12},{4,0},{8,4},{12,8},{16,28},{20,16},{24,20},{28,24},{32,44},... | collective-permute-start | bytes 491528 | tf_op jit(solution)/shard_map/gather_delta/ppermute | solution.py:382
  51.6 6.8 %collective-permute-start.23 = (bf16[128,640]{1,0:T(8,128)(2,1)S(1)}, bf16[128,640]{1,0:T(8,128)(2,1)S(1)}, u32[]{:S(2)}, u32[]{:S(2)}) collective-permute-start(bf16[128,640]{1,0:T(8,128)(2,1)S(1)} %join.1.refs_4_), channel_id=1, source_target_pairs={{0,8},{4,12},{8,0},{12,4},{16,24},{20,28},{24,16},{28,20},{32,40},... | collective-permute-start | bytes 491528 | tf_op jit(solution)/shard_map/gather_delta/ppermute | solution.py:382
  54.3 8.1 %collective-permute-start.19 = (bf16[3,64,640]{2,1,0:T(8,128)(2,1)S(1)}, bf16[3,64,640]{2,1,0:T(8,128)(2,1)S(1)}, u32[]{:S(2)}, u32[]{:S(2)}) collective-permute-start(bf16[3,64,640]{2,1,0:T(8,128)(2,1)S(1)} %trio.1.refs_0_), channel_id=1, source_target_pairs={{0,112},{4,116},{8,120},{12,124},{16,0},{20,4},{24,8},{28,12},{32,... | collective-permute-start | bytes 737288 | tf_op jit(solution)/shard_map/route_near/ppermute | solution.py:391
  54.4 8.0 %collective-permute-start.18 = (bf16[3,64,640]{2,1,0:T(8,128)(2,1)S(1)}, bf16[3,64,640]{2,1,0:T(8,128)(2,1)S(1)}, u32[]{:S(2)}, u32[]{:S(2)}) collective-permute-start(bf16[3,64,640]{2,1,0:T(8,128)(2,1)S(1)} %trio.1.refs_0_), channel_id=1, source_target_pairs={{0,16},{4,20},{8,24},{12,28},{16,32},{20,36},{24,40},{28,44},{32,4... | collective-permute-start | bytes 737288 | tf_op jit(solution)/shard_map/route_near/ppermute | solution.py:391
  59.7 8.9 %collective-permute-start.25 = (bf16[80,1664]{1,0:T(8,128)(2,1)S(1)}, bf16[80,1664]{1,0:T(8,128)(2,1)S(1)}, u32[]{:S(2)}, u32[]{:S(2)}) collective-permute-start(bf16[80,1664]{1,0:T(8,128)(2,1)S(1)} %get-tuple-element.51), channel_id=1, source_target_pairs={{0,16},{4,20},{8,24},{12,28},{16,32},{20,36},{24,40},{28,44},{32,4... | collective-permute-start | bytes 798728 | tf_op jit(solution)/shard_map/part_near/ppermute | solution.py:391
  60.0 7.6 %collective-permute-start.26 = (bf16[80,1536]{1,0:T(8,128)(2,1)S(1)}, bf16[80,1536]{1,0:T(8,128)(2,1)S(1)}, u32[]{:S(2)}, u32[]{:S(2)}) collective-permute-start(bf16[80,1536]{1,0:T(8,128)(2,1)S(1)} %get-tuple-element.52), channel_id=1, source_target_pairs={{0,112},{4,116},{8,120},{12,124},{16,0},{20,4},{24,8},{28,12},{32,... | collective-permute-start | bytes 737288 | tf_op jit(solution)/shard_map/part_near/ppermute | solution.py:391
  63.3 13.4 %collective-permute-start.20 = (bf16[2,64,640]{2,1,0:T(8,128)(2,1)S(1)}, bf16[2,64,640]{2,1,0:T(8,128)(2,1)S(1)}, u32[]{:S(2)}, u32[]{:S(2)}) collective-permute-start(bf16[2,64,640]{2,1,0:T(8,128)(2,1)S(1)} %get-tuple-element.47), channel_id=1, source_target_pairs={{0,4},{4,8},{8,12},{12,0},{16,20},{20,24},{24,28},{28,16},{32,36},... | collective-permute-start | bytes 491528 | tf_op jit(solution)/shard_map/route_x/ppermute | solution.py:382
  63.4 13.3 %collective-permute-start.21 = (bf16[2,64,640]{2,1,0:T(8,128)(2,1)S(1)}, bf16[2,64,640]{2,1,0:T(8,128)(2,1)S(1)}, u32[]{:S(2)}, u32[]{:S(2)}) collective-permute-start(bf16[2,64,640]{2,1,0:T(8,128)(2,1)S(1)} %get-tuple-element.48), channel_id=1, source_target_pairs={{0,8},{4,12},{8,0},{12,4},{16,24},{20,28},{24,16},{28,20},{32,40},... | collective-permute-start | bytes 491528 | tf_op jit(solution)/shard_map/route_x/ppermute | solution.py:382
  64.9 11.8 %collective-permute-start.22 = (bf16[2,64,640]{2,1,0:T(8,128)(2,1)S(1)}, bf16[2,64,640]{2,1,0:T(8,128)(2,1)S(1)}, u32[]{:S(2)}, u32[]{:S(2)}) collective-permute-start(bf16[2,64,640]{2,1,0:T(8,128)(2,1)S(1)} %get-tuple-element.49), channel_id=1, source_target_pairs={{0,12},{4,0},{8,4},{12,8},{16,28},{20,16},{24,20},{28,24},{32,44},... | collective-permute-start | bytes 491528 | tf_op jit(solution)/shard_map/route_x/ppermute | solution.py:382
  68.6 8.1 %collective-permute-start.27 = (bf16[80,640]{1,0:T(8,128)(2,1)S(1)}, bf16[80,640]{1,0:T(8,128)(2,1)S(1)}, u32[]{:S(2)}, u32[]{:S(2)}) collective-permute-start(bf16[80,640]{1,0:T(8,128)(2,1)S(1)} %get-tuple-element.55), channel_id=1, source_target_pairs={{0,48},{4,52},{8,56},{12,60},{16,64},{20,68},{24,72},{28,76},{32,8... | collective-permute-start | bytes 307208 | tf_op jit(solution)/shard_map/part_far/ppermute | solution.py:391
  69.8 6.9 %collective-permute-start.28 = (bf16[80,640]{1,0:T(8,128)(2,1)S(1)}, bf16[80,640]{1,0:T(8,128)(2,1)S(1)}, u32[]{:S(2)}, u32[]{:S(2)}) collective-permute-start(bf16[80,640]{1,0:T(8,128)(2,1)S(1)} %get-tuple-element.56), channel_id=1, source_target_pairs={{0,80},{4,84},{8,88},{12,92},{16,96},{20,100},{24,104},{28,108},{3... | collective-permute-start | bytes 307208 | tf_op jit(solution)/shard_map/part_far/ppermute | solution.py:391
  77.3 8.7 %collective-permute-start.29 = (bf16[2,64,640]{2,1,0:T(8,128)(2,1)S(1)}, bf16[2,64,640]{2,1,0:T(8,128)(2,1)S(1)}, u32[]{:S(2)}, u32[]{:S(2)}) collective-permute-start(bf16[2,64,640]{2,1,0:T(8,128)(2,1)S(1)} %pick.1._), channel_id=1, source_target_pairs={{0,128},{128,0},{1,129},{129,1},{2,130},{130,2},{3,131},{131,3},{4... | collective-permute-start | bytes 491528 | tf_op jit(solution)/shard_map/swap_acts/ppermute | solution.py:368

commit v4 on v3

--- a/solution.py
+++ b/solution.py
@@ -17,6 +17,7 @@
 SM = pl.BlockSpec(memory_space=pltpu.SMEM)
 AWAY = ((0, 0), (1, 0), (2, 1), (0, 1), (1, 1), (0, 2), (1, 2), (2, 0))
 BF = jnp.bfloat16
+FILL = 20 * 10**9
 F32 = jnp.float32
 
 
@@ -192,13 +193,10 @@
         send_ref[...] = delta
 
 
-def trio_kernel(a_ref, b_ref, c_ref, _, out_ref):
-    for k, ref in enumerate((a_ref, b_ref, c_ref)):
-        out_ref[k] = ref[...]
-
-
 def join_kernel(a_ref, b_ref, *refs):
-    out_ref = refs[-1]
+    out_ref, trio_ref = refs[-2:]
+    for k in range(3):
+        trio_ref[k] = refs[k][...]
     half = a_ref.shape[0]
     out_ref[:half] = a_ref[...]
     out_ref[half:] = b_ref[...]
@@ -206,7 +204,7 @@
 
 def part_kernel(x_count, z_count, info, *refs):
     turned, deltas = refs[:x_count], refs[x_count : 2 * x_count]
-    own_ref, plus_ref, minus_ref, far_ref, wide_ref, parts = refs[2 * x_count :]
+    own_ref, plus_ref, minus_ref, far_ref, wide_ref, parts = refs[2 * x_count + 1 :]
     left = jnp.concatenate([t[...] for t in turned], axis=1)
     right = jnp.concatenate([d[...] for d in deltas], axis=0)
     part = jnp.dot(left, right, preferred_element_type=F32).astype(BF)
@@ -229,7 +227,7 @@
     minus_ref[:, 2 * width :] = chunk(4)[:, split:]
 
 
-def middle_kernel(plus_ref, minus_ref, far_ref, wide_ref, _, up_ref, down_ref):
+def middle_kernel(plus_ref, minus_ref, far_ref, wide_ref, up_ref, down_ref):
     width = far_ref.shape[1]
     split = plus_ref.shape[1] - 2 * width
     up = far_ref[...].astype(F32) + minus_ref[:, width : 2 * width].astype(F32)
@@ -240,7 +238,7 @@
     down_ref[:, split:] = (down[:, split:] + minus_ref[:, 2 * width :].astype(F32)).astype(BF)
 
 
-def sum_kernel(own_ref, plus_ref, minus_ref, up_ref, down_ref, _, out_ref):
+def sum_kernel(own_ref, plus_ref, minus_ref, up_ref, down_ref, out_ref):
     width = own_ref.shape[1]
     total = own_ref[...].astype(F32) + plus_ref[:, :width].astype(F32)
     total = total + minus_ref[:, :width].astype(F32)
@@ -446,11 +444,13 @@
         nbytes=8 * half * width,
     )(info, *back_blocks, slope, delta1)
     come = swap(send, "swap_delta")
-    delta = call(join_kernel, shape(tokens, width), [VM] * (4 + x_count), "join")(
-        keep, come, *far, *lefts[1:]
-    )
+    delta, trio = call(
+        join_kernel,
+        (shape(tokens, width), shape(3, half, width)),
+        [VM] * (4 + x_count),
+        "join",
+    )(keep, come, *far, *lefts[1:])
     rights = [delta] + [x_move(delta, k, "gather_delta") for k in range(1, x_count)]
-    trio = call(trio_kernel, shape(3, half, width), [VM] * 4, "trio")(*far, rights[1])
     near = [
         trio,
         z_move(trio, 1, "route_near"),
@@ -469,27 +469,28 @@
     own, plus, minus, far_part, wide_part = call(
         functools.partial(part_kernel, x_count, z_count),
         (chunk, shape(rows, 2 * width + split), shape(rows, 3 * width - split), chunk, chunk),
-        [SM] + [VM] * (2 * x_count),
+        [SM] + [VM] * (2 * x_count + 1),
         "part",
         scratch=[pltpu.VMEM((z_count, rows, width), BF)],
         flops=2 * flops,
         nbytes=4 * feat * tokens,
-    )(info, *lefts, *rights)
+    )(info, *lefts, *rights, slots[0])
     plus, minus = z_move(plus, 1, "part_near"), z_move(minus, z_count - 1, "part_near")
-    up, down = call(middle_kernel, (chunk, chunk), [VM] * 5, "middle")(
-        plus, minus, far_part, wide_part, slots[0]
+    up, down = call(middle_kernel, (chunk, chunk), [VM] * 4, "middle")(
+        plus, minus, far_part, wide_part
     )
     up, down = z_move(up, 3, "part_far"), z_move(down, z_count - 3, "part_far")
     arrived = [slots[0]] + [x_move(slots[k], k, "route_x") for k in range(1, x_count)]
     sent = call(
         functools.partial(pick_kernel, x_count),
         pair,
-        [SM, SM] + [VM] * (x_count + 3),
+        [SM, SM] + [VM] * (x_count + 1),
         "pick",
+        flops=FILL,
         nbytes=2 * z_count * half * width,
-    )(info, plan, x1, *arrived, up, down)
-    grad_rows = call(sum_kernel, shape(rows, width, dtype=F32), [VM] * 6, "sum")(
-        own, plus, minus, up, down, sent
+    )(info, plan, x1, *arrived)
+    grad_rows = call(sum_kernel, shape(rows, width, dtype=F32), [VM] * 5, "sum")(
+        own, plus, minus, up, down
     )
     acts = pl.pallas_call(
         functools.partial(acts_kernel, x_count),

time: 87.8 us -> 87.2 us (level)
  the two profiles are of different devices: /device:TPU:1 before, /device:TPU:18 now
where the time goes in v4:
time: 87.2 us; the launch traced here: 87 us
  starting transfers between devices  42.8 us (49%)
  waiting for transfers between devices  27.1 us (31%)
  Pallas kernels  12.8 us (15%)
  local copies, waits for them, and re-layouts  3.41 us (4%)
    ppermute x8, waiting for transfers between devices, z_move(): return lax.ppermute(value, 'rep', pairs)  22.1 us
    ppermute x8, starting transfers between devices, z_move(): return lax.ppermute(value, 'rep', pairs)  16.1 us
    ppermute x9, starting transfers between devices, tp_move(): return lax.ppermute(value, 'tp', pairs)  13.9 us
    ppermute x9, starting transfers between devices, x_move(): return lax.ppermute(value, 'rep', pairs)  12.5 us
    ppermute x9, waiting for transfers between devices, tp_move(): return lax.ppermute(value, 'tp', pairs)  3.87 us
    unnamed x12, local copies, waits for them, and re-layouts  3.4 us
    pallas_call x1, Pallas kernels, on_device(): call(functools.partial(second_kernel, tp_count, feat, loss_scale), (shape...  2.72 us
  transfers between devices with their start and end apart: 30, of which 12 were waited for; matrix products, arithmetic and copies ran while one was open for 0% of the time, Pallas kernels for 9%

profile of v4, /device:TPU:18, one launch (start us, length us, event | category | flops | bytes accessed | tf_op | source)
XLA Modules:
  0.0 87.0 jit_solution(11782555199128929164)
XLA Ops:
  0.6 0.0 copy-start
  0.6 0.1 collective-permute-start.3
  0.8 0.8 copy-done
  1.6 0.5 collective-permute-start.2
  2.1 2.9 %collective-permute-start.1 = (bf16[64,640]{1,0:T(8,128)(2,1)S(1)}, bf16[64,640]{1,0:T(8,128)(2,1)}, u32[]{:S(2)}, u32[]{:S(2)}) collective-permute-start(bf16[64,640]{1,0:T(8,128)(2,1)S(1)} %dynamic-slice_bitcast_fusion.refs_0_), channel_id=1, source_target_pairs={{0,2},{1,3},{2,0},{3,1},{4,6},{5,7},{6,4},{7,5},{8,10},{9,11},{10,... | collective-permute-start | bytes 245768 | tf_op jit(solution)/shard_map/gather_x0/ppermute | solution.py:371
  5.0 0.0 collective-permute-start
  5.0 0.1 pad_add_fusion.info
  5.1 1.9 %copy-done.1 = bf16[1,2560,640]{2,1,0:T(8,128)(2,1)S(1)} copy-done((bf16[1,2560,640]{2,1,0:T(8,128)(2,1)S(1)}, bf16[1,2560,640]{2,1,0:T(8,128)(2,1)}, u32[]{:S(2)}) %copy-start.1) | copy-done | bytes 3276824
  7.0 0.7 copy-done.4
  7.7 1.6 %plan.1._ = s32[10]{0:T(128)S(1)} custom-call(s32[3]{0:T(128)S(1)} %pad_add_fusion.info, s32[1,1,32]{2,1,0:T(1,128)S(1)} %copy-done.4, bf16[2560,640]{1,0:T(8,128)(2,1)S(1)} %bitcast.10), custom_call_target="tpu_custom_call" | custom-call | tf_op jit(solution)/shard_map/plan/pallas_call | solution.py:396
  9.2 0.0 copy-start.3
  9.2 0.0 copy-start.5
  9.3 0.0 collective-permute-done.1.refs_2_
  9.3 0.3 collective-permute-done.refs_1_
  9.6 1.6 %first.1 = (bf16[64,640]{1,0:T(8,128)(2,1)S(1)}, f32[64,640]{1,0:T(8,128)S(1)}, f32[64,128]{1,0:T(8,128)S(1)}) custom-call(s32[3]{0:T(128)S(1)} %pad_add_fusion.info, s32[10]{0:T(128)S(1)} %plan.1._, bf16[64,640]{1,0:T(8,128)(2,1)S(1)} %dynamic-slice_bitcast_fusion.refs_0_, bf16[64,640]{1,0:T(8,128)(2,1)} %collective-permute-done.refs_1_, ...), custom_call_target="tpu_custom_call" | custom-call | flops 209715200 | bytes 3276800 | tf_op jit(solution)/shard_map/first/pallas_call | solution.py:407
  11.3 2.1 %collective-permute-start.6 = (bf16[64,640]{1,0:T(8,128)(2,1)S(1)}, bf16[64,640]{1,0:T(8,128)(2,1)S(1)}, u32[]{:S(2)}, u32[]{:S(2)}) collective-permute-start(bf16[64,640]{1,0:T(8,128)(2,1)S(1)} %get-tuple-element.32.refs_4_.x1_ref), channel_id=1, source_target_pairs={{0,3},{1,0},{2,1},{3,2},{4,7},{5,4},{6,5},{7,6},{8,11},{9,8},{10,9... | collective-permute-start | bytes 245768 | tf_op jit(solution)/shard_map/gather_x1/ppermute | solution.py:371
  13.3 1.8 %collective-permute-start.5 = (bf16[64,640]{1,0:T(8,128)(2,1)S(1)}, bf16[64,640]{1,0:T(8,128)(2,1)S(1)}, u32[]{:S(2)}, u32[]{:S(2)}) collective-permute-start(bf16[64,640]{1,0:T(8,128)(2,1)S(1)} %get-tuple-element.32.refs_4_.x1_ref), channel_id=1, source_target_pairs={{0,2},{1,3},{2,0},{3,1},{4,6},{5,7},{6,4},{7,5},{8,10},{9,11},{10,... | collective-permute-start | bytes 245768 | tf_op jit(solution)/shard_map/gather_x1/ppermute | solution.py:371
  15.2 1.5 %collective-permute-start.4 = (bf16[64,640]{1,0:T(8,128)(2,1)S(1)}, bf16[64,640]{1,0:T(8,128)(2,1)S(1)}, u32[]{:S(2)}, u32[]{:S(2)}) collective-permute-start(bf16[64,640]{1,0:T(8,128)(2,1)S(1)} %get-tuple-element.32.refs_4_.x1_ref), channel_id=1, source_target_pairs={{0,1},{1,2},{2,3},{3,0},{4,5},{5,6},{6,7},{7,4},{8,9},{9,10},{10,1... | collective-permute-start | bytes 245768 | tf_op jit(solution)/shard_map/gather_x1/ppermute | solution.py:371
  16.6 2.7 %collective-permute-done.5.refs_6_ = bf16[64,640]{1,0:T(8,128)(2,1)S(1)} collective-permute-done((bf16[64,640]{1,0:T(8,128)(2,1)S(1)}, bf16[64,640]{1,0:T(8,128)(2,1)S(1)}, u32[]{:S(2)}, u32[]{:S(2)}) %collective-permute-start.5) | collective-permute-done | bytes 81952 | tf_op jit(solution)/shard_map/gather_x1/ppermute | solution.py:371
  19.3 0.8 collective-permute-done.4.refs_5_
  20.2 2.7 %second.1 = (bf16[64,640]{1,0:T(8,128)(2,1)S(1)}, bf16[64,640]{1,0:T(8,128)(2,1)S(1)}, bf16[64,2560]{1,0:T(8,128)(2,1)S(1)}, bf16[64,640]{1,0:T(8,128)(2,1)S(1)}...) custom-call(s32[3]{0:T(128)S(1)} %pad_add_fusion.info, ...), custom_call_target="tpu_custom_call" | custom-call | flops 419430400 | bytes 3276800 | tf_op jit(solution)/shard_map/second/pallas_call | solution.py:416
  22.9 0.1 collective-permute-start.10
  23.0 0.6 collective-permute-start.7
  23.6 2.4 %collective-permute-start.8 = (bf16[64,640]{1,0:T(8,128)(2,1)S(1)}, bf16[64,640]{1,0:T(8,128)(2,1)S(1)}, u32[]{:S(2)}, u32[]{:S(2)}) collective-permute-start(bf16[64,640]{1,0:T(8,128)(2,1)S(1)} %get-tuple-element.35), channel_id=1, source_target_pairs={{0,2},{1,3},{2,0},{3,1},{4,6},{5,7},{6,4},{7,5},{8,10},{9,11},{10,... | collective-permute-start | bytes 245768 | tf_op jit(solution)/shard_map/sum_back/ppermute | solution.py:371
  26.1 2.0 %collective-permute-start.9 = (bf16[64,640]{1,0:T(8,128)(2,1)S(1)}, bf16[64,640]{1,0:T(8,128)(2,1)S(1)}, u32[]{:S(2)}, u32[]{:S(2)}) collective-permute-start(bf16[64,640]{1,0:T(8,128)(2,1)S(1)} %get-tuple-element.36), channel_id=1, source_target_pairs={{0,1},{1,2},{2,3},{3,0},{4,5},{5,6},{6,7},{7,4},{8,9},{9,10},{10,1... | collective-permute-start | bytes 245768 | tf_op jit(solution)/shard_map/sum_back/ppermute | solution.py:371
  28.1 6.7 %collective-permute-start.13 = (bf16[64,640]{1,0:T(8,128)(2,1)S(1)}, bf16[64,640]{1,0:T(8,128)(2,1)S(1)}, u32[]{:S(2)}, u32[]{:S(2)}) collective-permute-start(bf16[64,640]{1,0:T(8,128)(2,1)S(1)} %get-tuple-element.44.refs_0_), channel_id=1, source_target_pairs={{0,80},{4,84},{8,88},{12,92},{16,96},{20,100},{24,104},{28,108},{3... | collective-permute-start | bytes 245768 | tf_op jit(solution)/shard_map/route_far/ppermute | solution.py:389
  34.8 1.3 %turn.1 = (bf16[640,128]{1,0:T(8,128)(2,1)S(1)}, bf16[640,128]{1,0:T(8,128)(2,1)S(1)}, bf16[640,128]{1,0:T(8,128)(2,1)S(1)}, bf16[640,128]{1,0:T(8,128)(2,1)S(1)}, f32[64,640]{1,0:T(8,128)S(1)}) custom-call(s32[3]{0:T(128)S(1)} %pad_add_fusion.info, bf16[64,640]{1,0:T(8,128)(2,1)S(1)} %dynamic-slice_bitcast_fusion.refs_0_, ...), custom_call_target="tpu_custom_call" | custom-call | flops 52428800 | bytes 655360 | tf_op jit(solution)/shard_map/turn/pallas_call | solution.py:427
  36.1 1.6 %collective-permute-start.14 = (bf16[640,128]{1,0:T(8,128)(2,1)S(1)}, bf16[640,128]{1,0:T(8,128)(2,1)S(1)}, u32[]{:S(2)}, u32[]{:S(2)}) collective-permute-start(bf16[640,128]{1,0:T(8,128)(2,1)S(1)} %get-tuple-element.45), channel_id=1, source_target_pairs={{0,4},{4,8},{8,12},{12,0},{16,20},{20,24},{24,28},{28,16},{32,36},... | collective-permute-start | bytes 491528 | tf_op jit(solution)/shard_map/spread_rows/ppermute | solution.py:380
  37.7 0.0 collective-permute-done.7.refs_1_
  37.7 1.1 %collective-permute-start.15 = (bf16[640,128]{1,0:T(8,128)(2,1)S(1)}, bf16[640,128]{1,0:T(8,128)(2,1)S(1)}, u32[]{:S(2)}, u32[]{:S(2)}) collective-permute-start(bf16[640,128]{1,0:T(8,128)(2,1)S(1)} %get-tuple-element.46), channel_id=1, source_target_pairs={{0,8},{4,12},{8,0},{12,4},{16,24},{20,28},{24,16},{28,20},{32,40},... | collective-permute-start | bytes 491528 | tf_op jit(solution)/shard_map/spread_rows/ppermute | solution.py:380
  38.8 2.2 %collective-permute-start.16 = (bf16[640,128]{1,0:T(8,128)(2,1)S(1)}, bf16[640,128]{1,0:T(8,128)(2,1)S(1)}, u32[]{:S(2)}, u32[]{:S(2)}) collective-permute-start(bf16[640,128]{1,0:T(8,128)(2,1)S(1)} %get-tuple-element.47), channel_id=1, source_target_pairs={{0,12},{4,0},{8,4},{12,8},{16,28},{20,16},{24,20},{28,24},{32,44},... | collective-permute-start | bytes 491528 | tf_op jit(solution)/shard_map/spread_rows/ppermute | solution.py:380
  41.0 0.0 collective-permute-start.12
  41.0 0.6 delta.1
  41.6 0.1 collective-permute-start.11
  41.7 8.0 %collective-permute-done.12.refs_1_ = bf16[64,640]{1,0:T(8,128)(2,1)S(1)} collective-permute-done((bf16[64,640]{1,0:T(8,128)(2,1)S(1)}, bf16[64,640]{1,0:T(8,128)(2,1)S(1)}, u32[]{:S(2)}, u32[]{:S(2)}) %collective-permute-start.12) | collective-permute-done | bytes 81952 | tf_op jit(solution)/shard_map/route_far/ppermute | solution.py:389
  49.8 0.0 collective-permute-done.11.b_ref
  49.8 0.0 collective-permute-done.14.refs_3_.refs_1_
  49.8 0.0 collective-permute-done.15.refs_4_.refs_2_
  49.8 0.1 collective-permute-start.18
  49.9 2.0 %collective-permute-start.17 = (bf16[3,64,640]{2,1,0:T(8,128)(2,1)S(1)}, bf16[3,64,640]{2,1,0:T(8,128)(2,1)S(1)}, u32[]{:S(2)}, u32[]{:S(2)}) collective-permute-start(bf16[3,64,640]{2,1,0:T(8,128)(2,1)S(1)} %get-tuple-element.48.refs_0_), channel_id=1, source_target_pairs={{0,16},{4,20},{8,24},{12,28},{16,32},{20,36},{24,40},{28,44},{32,4... | collective-permute-start | bytes 737288 | tf_op jit(solution)/shard_map/route_near/ppermute | solution.py:389
  51.9 1.4 %collective-permute-start.25 = (bf16[128,640]{1,0:T(8,128)(2,1)S(1)}, bf16[128,640]{1,0:T(8,128)(2,1)S(1)}, u32[]{:S(2)}, u32[]{:S(2)}) collective-permute-start(bf16[128,640]{1,0:T(8,128)(2,1)S(1)} %get-tuple-element.54.refs_4_), channel_id=1, source_target_pairs={{0,12},{4,0},{8,4},{12,8},{16,28},{20,16},{24,20},{28,24},{32,44},... | collective-permute-start | bytes 491528 | tf_op jit(solution)/shard_map/gather_delta/ppermute | solution.py:380
  53.4 0.0 collective-permute-start.24
  53.4 1.8 %collective-permute-start.23 = (bf16[128,640]{1,0:T(8,128)(2,1)S(1)}, bf16[128,640]{1,0:T(8,128)(2,1)S(1)}, u32[]{:S(2)}, u32[]{:S(2)}) collective-permute-start(bf16[128,640]{1,0:T(8,128)(2,1)S(1)} %get-tuple-element.54.refs_4_), channel_id=1, source_target_pairs={{0,4},{4,8},{8,12},{12,0},{16,20},{20,24},{24,28},{28,16},{32,36},... | collective-permute-start | bytes 491528 | tf_op jit(solution)/shard_map/gather_delta/ppermute | solution.py:380
  55.1 0.9 %collective-permute-done.18.refs_2_ = bf16[3,64,640]{2,1,0:T(8,128)(2,1)S(1)} collective-permute-done((bf16[3,64,640]{2,1,0:T(8,128)(2,1)S(1)}, bf16[3,64,640]{2,1,0:T(8,128)(2,1)S(1)}, u32[]{:S(2)}, u32[]{:S(2)}) %collective-permute-start.18) | collective-permute-done | bytes 245792 | tf_op jit(solution)/shard_map/route_near/ppermute | solution.py:389
  56.1 1.3 %collective-permute-done.17.refs_1_ = bf16[3,64,640]{2,1,0:T(8,128)(2,1)S(1)} collective-permute-done((bf16[3,64,640]{2,1,0:T(8,128)(2,1)S(1)}, bf16[3,64,640]{2,1,0:T(8,128)(2,1)S(1)}, u32[]{:S(2)}, u32[]{:S(2)}) %collective-permute-start.17) | collective-permute-done | bytes 245792 | tf_op jit(solution)/shard_map/route_near/ppermute | solution.py:389
  57.4 0.9 %route.1 = (bf16[2,64,640]{2,1,0:T(8,128)(2,1)S(1)}, bf16[2,64,640]{2,1,0:T(8,128)(2,1)S(1)}, bf16[2,64,640]{2,1,0:T(8,128)(2,1)S(1)}, bf16[2,64,640]{2,1,0:T(8,128)(2,1)S(1)}) custom-call(s32[10]{0:T(128)S(1)} %plan.1._, bf16[3,64,640]{2,1,0:T(8,128)(2,1)S(1)} %get-tuple-element.48.refs_0_, bf16[3,64,640]{2,1,0:T(8,128)(2,1)S(1)} %collective-permute-done.17.refs_1_, ...), custom_call_target="tpu_custom_call" | custom-call | bytes 655360 | tf_op jit(solution)/shard_map/route/pallas_call | solution.py:460
  58.3 0.1 collective-permute-start.19
  58.4 3.4 %collective-permute-start.20 = (bf16[2,64,640]{2,1,0:T(8,128)(2,1)S(1)}, bf16[2,64,640]{2,1,0:T(8,128)(2,1)S(1)}, u32[]{:S(2)}, u32[]{:S(2)}) collective-permute-start(bf16[2,64,640]{2,1,0:T(8,128)(2,1)S(1)} %get-tuple-element.51), channel_id=1, source_target_pairs={{0,8},{4,12},{8,0},{12,4},{16,24},{20,28},{24,16},{28,20},{32,40},... | collective-permute-start | bytes 491528 | tf_op jit(solution)/shard_map/route_x/ppermute | solution.py:380
  61.9 0.8 collective-permute-start.21
  62.7 0.9 %collective-permute-done.23.refs_5_ = bf16[128,640]{1,0:T(8,128)(2,1)S(1)} collective-permute-done((bf16[128,640]{1,0:T(8,128)(2,1)S(1)}, bf16[128,640]{1,0:T(8,128)(2,1)S(1)}, u32[]{:S(2)}, u32[]{:S(2)}) %collective-permute-start.23) | collective-permute-done | bytes 163872 | tf_op jit(solution)/shard_map/gather_delta/ppermute | solution.py:380
  63.6 1.3 %part.1 = (bf16[80,640]{1,0:T(8,128)(2,1)S(1)}, bf16[80,1664]{1,0:T(8,128)(2,1)S(1)}, bf16[80,1536]{1,0:T(8,128)(2,1)S(1)}, bf16[80,640]{1,0:T(8,128)(2,1)S(1)}, bf16[80,640]{1,0:T(8,128)(2,1)S(1)}) custom-call(s32[3]{0:T(128)S(1)} %pad_add_fusion.info, bf16[640,128]{1,0:T(8,128)(2,1)S(1)} %get-tuple-element.53.refs_0_, ...), custom_call_target="tpu_custom_call" | custom-call | flops 419430400 | bytes 1310720 | tf_op jit(solution)/shard_map/part/pallas_call | solution.py:469
  64.9 2.1 %collective-permute-start.27 = (bf16[80,1536]{1,0:T(8,128)(2,1)S(1)}, bf16[80,1536]{1,0:T(8,128)(2,1)S(1)}, u32[]{:S(2)}, u32[]{:S(2)}) collective-permute-start(bf16[80,1536]{1,0:T(8,128)(2,1)S(1)} %get-tuple-element.57), channel_id=1, source_target_pairs={{0,112},{4,116},{8,120},{12,124},{16,0},{20,4},{24,8},{28,12},{32,... | collective-permute-start | bytes 737288 | tf_op jit(solution)/shard_map/part_near/ppermute | solution.py:389
  67.0 0.2 collective-permute-done.21.refs_3_
  67.2 0.6 pick.1
  67.8 0.1 collective-permute-start.22
  67.9 3.3 %collective-permute-done.27.minus_ref = bf16[80,1536]{1,0:T(8,128)(2,1)S(1)} collective-permute-done((bf16[80,1536]{1,0:T(8,128)(2,1)S(1)}, bf16[80,1536]{1,0:T(8,128)(2,1)S(1)}, u32[]{:S(2)}, u32[]{:S(2)}) %collective-permute-start.27) | collective-permute-done | bytes 245792 | tf_op jit(solution)/shard_map/part_near/ppermute | solution.py:389
  71.2 6.8 %collective-permute-done.26.plus_ref = bf16[80,1664]{1,0:T(8,128)(2,1)S(1)} collective-permute-done((bf16[80,1664]{1,0:T(8,128)(2,1)S(1)}, bf16[80,1664]{1,0:T(8,128)(2,1)S(1)}, u32[]{:S(2)}, u32[]{:S(2)}) %collective-permute-start.26) | collective-permute-done | bytes 266272 | tf_op jit(solution)/shard_map/part_near/ppermute | solution.py:389
  77.9 0.1 middle.1
  78.0 0.1 collective-permute-start.28
  78.1 5.0 %collective-permute-start.29 = (bf16[80,640]{1,0:T(8,128)(2,1)S(1)}, bf16[80,640]{1,0:T(8,128)(2,1)S(1)}, u32[]{:S(2)}, u32[]{:S(2)}) collective-permute-start(bf16[80,640]{1,0:T(8,128)(2,1)S(1)} %get-tuple-element.61), channel_id=1, source_target_pairs={{0,80},{4,84},{8,88},{12,92},{16,96},{20,100},{24,104},{28,108},{3... | collective-permute-start | bytes 307208 | tf_op jit(solution)/shard_map/part_far/ppermute | solution.py:389
  83.1 1.3 %acts.1 = bf16[2,128,640]{2,1,0:T(8,128)(2,1)} custom-call(s32[3]{0:T(128)S(1)} %pad_add_fusion.info, s32[10]{0:T(128)S(1)} %plan.1._, bf16[64,640]{1,0:T(8,128)(2,1)S(1)} %get-tuple-element.32.refs_4_.x1_ref, bf16[2,64,640]{2,1,0:T(8,128)(2,1)S(1)} %collective-permute-done.22.come_ref, bf16[2,64,640]{2,1,0:T(8,128)(2,1)S(1)} %get-tuple-element.49.refs_0_.refs_8_, ...), custom_call_target="tpu_custom_call" | custom-call | tf_op jit(solution)/shard_map/acts/pallas_call | solution.py:495
  84.4 1.3 %collective-permute-done.28.up_ref = bf16[80,640]{1,0:T(8,128)(2,1)S(1)} collective-permute-done((bf16[80,640]{1,0:T(8,128)(2,1)S(1)}, bf16[80,640]{1,0:T(8,128)(2,1)S(1)}, u32[]{:S(2)}, u32[]{:S(2)}) %collective-permute-start.28) | collective-permute-done | bytes 102432 | tf_op jit(solution)/shard_map/part_far/ppermute | solution.py:389
  85.8 0.5 collective-permute-done.29.down_ref
  86.2 0.8 sum.1
  (22 shorter events, 0.1 us)
Async XLA Ops:
  0.6 0.9 %copy-start = (bf16[1,1,128,640]{3,2,1,0:T(8,128)(2,1)S(1)}, bf16[1,1,128,640]{3,2,1,0:T(8,128)(2,1)}, u32[]{:S(2)}) copy-start(bf16[1,1,128,640]{3,2,1,0:T(8,128)(2,1)} %param.5) | copy-start | bytes 491524
  0.6 9.0 %collective-permute-start.3 = (bf16[2560,640]{1,0:T(8,128)(2,1)}, bf16[2560,640]{1,0:T(8,128)(2,1)S(1)}, u32[]{:S(2)}, u32[]{:S(2)}) collective-permute-start(bf16[2560,640]{1,0:T(8,128)(2,1)} %bitcast.9), channel_id=1, source_target_pairs={{0,128},{128,0},{1,129},{129,1},{2,130},{130,2},{3,131},{131,3},{4... | collective-permute-start | bytes 9830408 | tf_op jit(solution)/shard_map/swap_weight/ppermute | solution.py:366
  1.6 7.7 %collective-permute-start.2 = (bf16[64,640]{1,0:T(8,128)(2,1)S(1)}, bf16[64,640]{1,0:T(8,128)(2,1)}, u32[]{:S(2)}, u32[]{:S(2)}) collective-permute-start(bf16[64,640]{1,0:T(8,128)(2,1)S(1)} %dynamic-slice_bitcast_fusion.refs_0_), channel_id=1, source_target_pairs={{0,3},{1,0},{2,1},{3,2},{4,7},{5,4},{6,5},{7,6},{8,11},{9,8},{10,9... | collective-permute-start | bytes 245768 | tf_op jit(solution)/shard_map/gather_x0/ppermute | solution.py:371
  2.1 7.2 %collective-permute-start.1 = (bf16[64,640]{1,0:T(8,128)(2,1)S(1)}, bf16[64,640]{1,0:T(8,128)(2,1)}, u32[]{:S(2)}, u32[]{:S(2)}) collective-permute-start(bf16[64,640]{1,0:T(8,128)(2,1)S(1)} %dynamic-slice_bitcast_fusion.refs_0_), channel_id=1, source_target_pairs={{0,2},{1,3},{2,0},{3,1},{4,6},{5,7},{6,4},{7,5},{8,10},{9,11},{10,... | collective-permute-start | bytes 245768 | tf_op jit(solution)/shard_map/gather_x0/ppermute | solution.py:371
  5.0 4.6 %collective-permute-start = (bf16[64,640]{1,0:T(8,128)(2,1)S(1)}, bf16[64,640]{1,0:T(8,128)(2,1)}, u32[]{:S(2)}, u32[]{:S(2)}) collective-permute-start(bf16[64,640]{1,0:T(8,128)(2,1)S(1)} %dynamic-slice_bitcast_fusion.refs_0_), channel_id=1, source_target_pairs={{0,1},{1,2},{2,3},{3,0},{4,5},{5,6},{6,7},{7,4},{8,9},{9,10},{10,1... | collective-permute-start | bytes 245768 | tf_op jit(solution)/shard_map/gather_x0/ppermute | solution.py:371
  5.1 1.9 %copy-start.1 = (bf16[1,2560,640]{2,1,0:T(8,128)(2,1)S(1)}, bf16[1,2560,640]{2,1,0:T(8,128)(2,1)}, u32[]{:S(2)}) copy-start(bf16[1,2560,640]{2,1,0:T(8,128)(2,1)} %param.6) | copy-start | bytes 9830404
  7.0 0.7 copy-start.4
  7.7 1.9 %copy-start.2 = (bf16[1,2560,640]{2,1,0:T(8,128)(2,1)S(1)}, bf16[1,2560,640]{2,1,0:T(8,128)(2,1)}, u32[]{:S(2)}) copy-start(bf16[1,2560,640]{2,1,0:T(8,128)(2,1)} %param.6) | copy-start | bytes 9830404
  9.2 10.9 %copy-start.3 = (bf16[1,1,128,640]{3,2,1,0:T(8,128)(2,1)S(1)}, bf16[1,1,128,640]{3,2,1,0:T(8,128)(2,1)}, u32[]{:S(2)}) copy-start(bf16[1,1,128,640]{3,2,1,0:T(8,128)(2,1)} %param.9) | copy-start | bytes 491524
  9.2 10.9 %copy-start.5 = (s32[1,32]{1,0:T(1,128)S(1)}, s32[1,32]{1,0:T(1,128)}, u32[]{:S(2)}) copy-start(s32[1,32]{1,0:T(1,128)} %lengths.1) | copy-start | bytes 388
  11.3 5.4 %collective-permute-start.6 = (bf16[64,640]{1,0:T(8,128)(2,1)S(1)}, bf16[64,640]{1,0:T(8,128)(2,1)S(1)}, u32[]{:S(2)}, u32[]{:S(2)}) collective-permute-start(bf16[64,640]{1,0:T(8,128)(2,1)S(1)} %get-tuple-element.32.refs_4_.x1_ref), channel_id=1, source_target_pairs={{0,3},{1,0},{2,1},{3,2},{4,7},{5,4},{6,5},{7,6},{8,11},{9,8},{10,9... | collective-permute-start | bytes 245768 | tf_op jit(solution)/shard_map/gather_x1/ppermute | solution.py:371
  13.3 6.0 %collective-permute-start.5 = (bf16[64,640]{1,0:T(8,128)(2,1)S(1)}, bf16[64,640]{1,0:T(8,128)(2,1)S(1)}, u32[]{:S(2)}, u32[]{:S(2)}) collective-permute-start(bf16[64,640]{1,0:T(8,128)(2,1)S(1)} %get-tuple-element.32.refs_4_.x1_ref), channel_id=1, source_target_pairs={{0,2},{1,3},{2,0},{3,1},{4,6},{5,7},{6,4},{7,5},{8,10},{9,11},{10,... | collective-permute-start | bytes 245768 | tf_op jit(solution)/shard_map/gather_x1/ppermute | solution.py:371
  15.2 5.0 %collective-permute-start.4 = (bf16[64,640]{1,0:T(8,128)(2,1)S(1)}, bf16[64,640]{1,0:T(8,128)(2,1)S(1)}, u32[]{:S(2)}, u32[]{:S(2)}) collective-permute-start(bf16[64,640]{1,0:T(8,128)(2,1)S(1)} %get-tuple-element.32.refs_4_.x1_ref), channel_id=1, source_target_pairs={{0,1},{1,2},{2,3},{3,0},{4,5},{5,6},{6,7},{7,4},{8,9},{9,10},{10,1... | collective-permute-start | bytes 245768 | tf_op jit(solution)/shard_map/gather_x1/ppermute | solution.py:371
  22.9 11.9 %collective-permute-start.10 = (bf16[64,2560]{1,0:T(8,128)(2,1)S(1)}, bf16[64,2560]{1,0:T(8,128)(2,1)S(1)}, u32[]{:S(2)}, u32[]{:S(2)}) collective-permute-start(bf16[64,2560]{1,0:T(8,128)(2,1)S(1)} %get-tuple-element.37), channel_id=1, source_target_pairs={{0,128},{128,0},{1,129},{129,1},{2,130},{130,2},{3,131},{131,3},{4... | collective-permute-start | bytes 983048 | tf_op jit(solution)/shard_map/swap_rows/ppermute | solution.py:366
  23.0 14.7 %collective-permute-start.7 = (bf16[64,640]{1,0:T(8,128)(2,1)S(1)}, bf16[64,640]{1,0:T(8,128)(2,1)S(1)}, u32[]{:S(2)}, u32[]{:S(2)}) collective-permute-start(bf16[64,640]{1,0:T(8,128)(2,1)S(1)} %get-tuple-element.34), channel_id=1, source_target_pairs={{0,3},{1,0},{2,1},{3,2},{4,7},{5,4},{6,5},{7,6},{8,11},{9,8},{10,9... | collective-permute-start | bytes 245768 | tf_op jit(solution)/shard_map/sum_back/ppermute | solution.py:371
  23.6 15.2 %collective-permute-start.8 = (bf16[64,640]{1,0:T(8,128)(2,1)S(1)}, bf16[64,640]{1,0:T(8,128)(2,1)S(1)}, u32[]{:S(2)}, u32[]{:S(2)}) collective-permute-start(bf16[64,640]{1,0:T(8,128)(2,1)S(1)} %get-tuple-element.35), channel_id=1, source_target_pairs={{0,2},{1,3},{2,0},{3,1},{4,6},{5,7},{6,4},{7,5},{8,10},{9,11},{10,... | collective-permute-start | bytes 245768 | tf_op jit(solution)/shard_map/sum_back/ppermute | solution.py:371
  26.1 14.9 %collective-permute-start.9 = (bf16[64,640]{1,0:T(8,128)(2,1)S(1)}, bf16[64,640]{1,0:T(8,128)(2,1)S(1)}, u32[]{:S(2)}, u32[]{:S(2)}) collective-permute-start(bf16[64,640]{1,0:T(8,128)(2,1)S(1)} %get-tuple-element.36), channel_id=1, source_target_pairs={{0,1},{1,2},{2,3},{3,0},{4,5},{5,6},{6,7},{7,4},{8,9},{9,10},{10,1... | collective-permute-start | bytes 245768 | tf_op jit(solution)/shard_map/sum_back/ppermute | solution.py:371
  28.1 13.5 %collective-permute-start.13 = (bf16[64,640]{1,0:T(8,128)(2,1)S(1)}, bf16[64,640]{1,0:T(8,128)(2,1)S(1)}, u32[]{:S(2)}, u32[]{:S(2)}) collective-permute-start(bf16[64,640]{1,0:T(8,128)(2,1)S(1)} %get-tuple-element.44.refs_0_), channel_id=1, source_target_pairs={{0,80},{4,84},{8,88},{12,92},{16,96},{20,100},{24,104},{28,108},{3... | collective-permute-start | bytes 245768 | tf_op jit(solution)/shard_map/route_far/ppermute | solution.py:389
  36.1 13.6 %collective-permute-start.14 = (bf16[640,128]{1,0:T(8,128)(2,1)S(1)}, bf16[640,128]{1,0:T(8,128)(2,1)S(1)}, u32[]{:S(2)}, u32[]{:S(2)}) collective-permute-start(bf16[640,128]{1,0:T(8,128)(2,1)S(1)} %get-tuple-element.45), channel_id=1, source_target_pairs={{0,4},{4,8},{8,12},{12,0},{16,20},{20,24},{24,28},{28,16},{32,36},... | collective-permute-start | bytes 491528 | tf_op jit(solution)/shard_map/spread_rows/ppermute | solution.py:380
  37.7 12.1 %collective-permute-start.15 = (bf16[640,128]{1,0:T(8,128)(2,1)S(1)}, bf16[640,128]{1,0:T(8,128)(2,1)S(1)}, u32[]{:S(2)}, u32[]{:S(2)}) collective-permute-start(bf16[640,128]{1,0:T(8,128)(2,1)S(1)} %get-tuple-element.46), channel_id=1, source_target_pairs={{0,8},{4,12},{8,0},{12,4},{16,24},{20,28},{24,16},{28,20},{32,40},... | collective-permute-start | bytes 491528 | tf_op jit(solution)/shard_map/spread_rows/ppermute | solution.py:380
  38.8 11.0 %collective-permute-start.16 = (bf16[640,128]{1,0:T(8,128)(2,1)S(1)}, bf16[640,128]{1,0:T(8,128)(2,1)S(1)}, u32[]{:S(2)}, u32[]{:S(2)}) collective-permute-start(bf16[640,128]{1,0:T(8,128)(2,1)S(1)} %get-tuple-element.47), channel_id=1, source_target_pairs={{0,12},{4,0},{8,4},{12,8},{16,28},{20,16},{24,20},{28,24},{32,44},... | collective-permute-start | bytes 491528 | tf_op jit(solution)/shard_map/spread_rows/ppermute | solution.py:380
  41.0 8.8 %collective-permute-start.12 = (bf16[64,640]{1,0:T(8,128)(2,1)S(1)}, bf16[64,640]{1,0:T(8,128)(2,1)S(1)}, u32[]{:S(2)}, u32[]{:S(2)}) collective-permute-start(bf16[64,640]{1,0:T(8,128)(2,1)S(1)} %get-tuple-element.44.refs_0_), channel_id=1, source_target_pairs={{0,48},{4,52},{8,56},{12,60},{16,64},{20,68},{24,72},{28,76},{32,8... | collective-permute-start | bytes 245768 | tf_op jit(solution)/shard_map/route_far/ppermute | solution.py:389
  41.6 8.2 %collective-permute-start.11 = (bf16[64,640]{1,0:T(8,128)(2,1)S(1)}, bf16[64,640]{1,0:T(8,128)(2,1)S(1)}, u32[]{:S(2)}, u32[]{:S(2)}) collective-permute-start(bf16[64,640]{1,0:T(8,128)(2,1)S(1)} %get-tuple-element.43), channel_id=1, source_target_pairs={{0,128},{128,0},{1,129},{129,1},{2,130},{130,2},{3,131},{131,3},{4... | collective-permute-start | bytes 245768 | tf_op jit(solution)/shard_map/swap_delta/ppermute | solution.py:366
  49.8 6.3 %collective-permute-start.18 = (bf16[3,64,640]{2,1,0:T(8,128)(2,1)S(1)}, bf16[3,64,640]{2,1,0:T(8,128)(2,1)S(1)}, u32[]{:S(2)}, u32[]{:S(2)}) collective-permute-start(bf16[3,64,640]{2,1,0:T(8,128)(2,1)S(1)} %get-tuple-element.48.refs_0_), channel_id=1, source_target_pairs={{0,112},{4,116},{8,120},{12,124},{16,0},{20,4},{24,8},{28,12},{32,... | collective-permute-start | bytes 737288 | tf_op jit(solution)/shard_map/route_near/ppermute | solution.py:389
  49.9 7.5 %collective-permute-start.17 = (bf16[3,64,640]{2,1,0:T(8,128)(2,1)S(1)}, bf16[3,64,640]{2,1,0:T(8,128)(2,1)S(1)}, u32[]{:S(2)}, u32[]{:S(2)}) collective-permute-start(bf16[3,64,640]{2,1,0:T(8,128)(2,1)S(1)} %get-tuple-element.48.refs_0_), channel_id=1, source_target_pairs={{0,16},{4,20},{8,24},{12,28},{16,32},{20,36},{24,40},{28,44},{32,4... | collective-permute-start | bytes 737288 | tf_op jit(solution)/shard_map/route_near/ppermute | solution.py:389
  51.9 9.9 %collective-permute-start.25 = (bf16[128,640]{1,0:T(8,128)(2,1)S(1)}, bf16[128,640]{1,0:T(8,128)(2,1)S(1)}, u32[]{:S(2)}, u32[]{:S(2)}) collective-permute-start(bf16[128,640]{1,0:T(8,128)(2,1)S(1)} %get-tuple-element.54.refs_4_), channel_id=1, source_target_pairs={{0,12},{4,0},{8,4},{12,8},{16,28},{20,16},{24,20},{28,24},{32,44},... | collective-permute-start | bytes 491528 | tf_op jit(solution)/shard_map/gather_delta/ppermute | solution.py:380
  53.4 9.3 %collective-permute-start.24 = (bf16[128,640]{1,0:T(8,128)(2,1)S(1)}, bf16[128,640]{1,0:T(8,128)(2,1)S(1)}, u32[]{:S(2)}, u32[]{:S(2)}) collective-permute-start(bf16[128,640]{1,0:T(8,128)(2,1)S(1)} %get-tuple-element.54.refs_4_), channel_id=1, source_target_pairs={{0,8},{4,12},{8,0},{12,4},{16,24},{20,28},{24,16},{28,20},{32,40},... | collective-permute-start | bytes 491528 | tf_op jit(solution)/shard_map/gather_delta/ppermute | solution.py:380
  53.4 10.3 %collective-permute-start.23 = (bf16[128,640]{1,0:T(8,128)(2,1)S(1)}, bf16[128,640]{1,0:T(8,128)(2,1)S(1)}, u32[]{:S(2)}, u32[]{:S(2)}) collective-permute-start(bf16[128,640]{1,0:T(8,128)(2,1)S(1)} %get-tuple-element.54.refs_4_), channel_id=1, source_target_pairs={{0,4},{4,8},{8,12},{12,0},{16,20},{20,24},{24,28},{28,16},{32,36},... | collective-permute-start | bytes 491528 | tf_op jit(solution)/shard_map/gather_delta/ppermute | solution.py:380
  58.3 8.8 %collective-permute-start.19 = (bf16[2,64,640]{2,1,0:T(8,128)(2,1)S(1)}, bf16[2,64,640]{2,1,0:T(8,128)(2,1)S(1)}, u32[]{:S(2)}, u32[]{:S(2)}) collective-permute-start(bf16[2,64,640]{2,1,0:T(8,128)(2,1)S(1)} %get-tuple-element.50), channel_id=1, source_target_pairs={{0,4},{4,8},{8,12},{12,0},{16,20},{20,24},{24,28},{28,16},{32,36},... | collective-permute-start | bytes 491528 | tf_op jit(solution)/shard_map/route_x/ppermute | solution.py:380
  58.4 8.6 %collective-permute-start.20 = (bf16[2,64,640]{2,1,0:T(8,128)(2,1)S(1)}, bf16[2,64,640]{2,1,0:T(8,128)(2,1)S(1)}, u32[]{:S(2)}, u32[]{:S(2)}) collective-permute-start(bf16[2,64,640]{2,1,0:T(8,128)(2,1)S(1)} %get-tuple-element.51), channel_id=1, source_target_pairs={{0,8},{4,12},{8,0},{12,4},{16,24},{20,28},{24,16},{28,20},{32,40},... | collective-permute-start | bytes 491528 | tf_op jit(solution)/shard_map/route_x/ppermute | solution.py:380
  61.9 5.3 %collective-permute-start.21 = (bf16[2,64,640]{2,1,0:T(8,128)(2,1)S(1)}, bf16[2,64,640]{2,1,0:T(8,128)(2,1)S(1)}, u32[]{:S(2)}, u32[]{:S(2)}) collective-permute-start(bf16[2,64,640]{2,1,0:T(8,128)(2,1)S(1)} %get-tuple-element.52), channel_id=1, source_target_pairs={{0,12},{4,0},{8,4},{12,8},{16,28},{20,16},{24,20},{28,24},{32,44},... | collective-permute-start | bytes 491528 | tf_op jit(solution)/shard_map/route_x/ppermute | solution.py:380
  64.9 6.3 %collective-permute-start.27 = (bf16[80,1536]{1,0:T(8,128)(2,1)S(1)}, bf16[80,1536]{1,0:T(8,128)(2,1)S(1)}, u32[]{:S(2)}, u32[]{:S(2)}) collective-permute-start(bf16[80,1536]{1,0:T(8,128)(2,1)S(1)} %get-tuple-element.57), channel_id=1, source_target_pairs={{0,112},{4,116},{8,120},{12,124},{16,0},{20,4},{24,8},{28,12},{32,... | collective-permute-start | bytes 737288 | tf_op jit(solution)/shard_map/part_near/ppermute | solution.py:389
  67.0 10.9 %collective-permute-start.26 = (bf16[80,1664]{1,0:T(8,128)(2,1)S(1)}, bf16[80,1664]{1,0:T(8,128)(2,1)S(1)}, u32[]{:S(2)}, u32[]{:S(2)}) collective-permute-start(bf16[80,1664]{1,0:T(8,128)(2,1)S(1)} %get-tuple-element.56), channel_id=1, source_target_pairs={{0,16},{4,20},{8,24},{12,28},{16,32},{20,36},{24,40},{28,44},{32,4... | collective-permute-start | bytes 798728 | tf_op jit(solution)/shard_map/part_near/ppermute | solution.py:389
  67.8 15.3 %collective-permute-start.22 = (bf16[2,64,640]{2,1,0:T(8,128)(2,1)S(1)}, bf16[2,64,640]{2,1,0:T(8,128)(2,1)S(1)}, u32[]{:S(2)}, u32[]{:S(2)}) collective-permute-start(bf16[2,64,640]{2,1,0:T(8,128)(2,1)S(1)} %pick.1), channel_id=1, source_target_pairs={{0,128},{128,0},{1,129},{129,1},{2,130},{130,2},{3,131},{131,3},{4... | collective-permute-start | bytes 491528 | tf_op jit(solution)/shard_map/swap_acts/ppermute | solution.py:366
  78.0 7.7 %collective-permute-start.28 = (bf16[80,640]{1,0:T(8,128)(2,1)S(1)}, bf16[80,640]{1,0:T(8,128)(2,1)S(1)}, u32[]{:S(2)}, u32[]{:S(2)}) collective-permute-start(bf16[80,640]{1,0:T(8,128)(2,1)S(1)} %get-tuple-element.60), channel_id=1, source_target_pairs={{0,48},{4,52},{8,56},{12,60},{16,64},{20,68},{24,72},{28,76},{32,8... | collective-permute-start | bytes 307208 | tf_op jit(solution)/shard_map/part_far/ppermute | solution.py:389
  78.1 8.1 %collective-permute-start.29 = (bf16[80,640]{1,0:T(8,128)(2,1)S(1)}, bf16[80,640]{1,0:T(8,128)(2,1)S(1)}, u32[]{:S(2)}, u32[]{:S(2)}) collective-permute-start(bf16[80,640]{1,0:T(8,128)(2,1)S(1)} %get-tuple-element.61), channel_id=1, source_target_pairs={{0,80},{4,84},{8,88},{12,92},{16,96},{20,100},{24,104},{28,108},{3... | collective-permute-start | bytes 307208 | tf_op jit(solution)/shard_map/part_far/ppermute | solution.py:389

commit v5 on v4

--- a/solution.py
+++ b/solution.py
@@ -88,7 +88,7 @@
         run(other_ref)
 
 
-def second_kernel(tp_count, feat, loss_scale, info, lengths, *refs):
+def second_kernel(tp_count, feat, loss_scale, info, lengths, _, *refs):
     early = refs[:tp_count]
     blocks = refs[tp_count : 2 * tp_count]
     own_ref, other_ref, goal_ref, x2_ref, delta_ref, pack_ref = refs[2 * tp_count : 2 * tp_count + 6]
@@ -136,12 +136,16 @@
         pack(early)
 
 
+def slope_kernel(mixed_ref, scale_ref, out_ref):
+    out_ref[...] = gelu_slope(mixed_ref[...]) * scale_ref[:, :1]
+
+
 def turn_kernel(tp_count, x_count, info, *refs):
     first = refs[:tp_count]
     second = refs[tp_count : 2 * tp_count]
-    other_ref, mixed_ref, scale_ref = refs[2 * tp_count : 2 * tp_count + 3]
-    outs = refs[2 * tp_count + 3 : 2 * tp_count + 3 + x_count]
-    slope_ref, turned = refs[2 * tp_count + 3 + x_count :]
+    other_ref = refs[2 * tp_count]
+    outs = refs[2 * tp_count + 1 : 2 * tp_count + 1 + x_count]
+    turned = refs[-1]
     tp_pos = info[2]
     x_pos = lax.rem(info[1], x_count)
     rows = turned.shape[2]
@@ -167,7 +171,6 @@
     def _():
         put(second)
 
-    slope_ref[...] = gelu_slope(mixed_ref[...]) * scale_ref[:, :1]
     for k in range(x_count):
         chunk = turned[lax.rem(x_pos + k, x_count)]
         outs[k][: chunk.shape[0] * rows] = chunk.reshape(-1, chunk.shape[2])
@@ -412,27 +415,28 @@
         flops=flops,
         nbytes=2 * feat * width,
     )(info, plan, *first_blocks, weight, other_weight)
+    slope = call(slope_kernel, shape(half, width, dtype=F32), [VM, VM], "slope")(mixed, scale)
     second_blocks = [x1] + [tp_move(x1, k, "gather_x1") for k in range(1, tp_count)]
     x2, delta1, packed, *back = call(
         functools.partial(second_kernel, tp_count, feat, loss_scale),
         (shape(half, width), shape(half, width), shape(half, feat))
         + (shape(half, width),) * tp_count,
-        [SM, SM] + [VM] * (2 * tp_count + 3),
+        [SM, SM] + [VM] * (2 * tp_count + 4),
         "second",
         flops=2 * flops,
         nbytes=2 * feat * width,
-    )(info, lengths, *first_blocks, *second_blocks, weight, other_weight, goal)
+    )(info, lengths, slope, *first_blocks, *second_blocks, weight, other_weight, goal)
     back_blocks = [back[0]] + [tp_move(back[k], tp_count - k, "sum_back") for k in range(1, tp_count)]
     other_pack = swap(packed, "swap_rows")
-    *turned, slope = call(
+    turned = call(
         functools.partial(turn_kernel, tp_count, x_count),
-        (shape(feat // x_count, tokens),) * x_count + (shape(half, width, dtype=F32),),
-        [SM] + [VM] * (2 * tp_count + 3),
+        (shape(feat // x_count, tokens),) * x_count,
+        [SM] + [VM] * (2 * tp_count + 1),
         "turn",
         scratch=[pltpu.VMEM((x_count, z_count, rows, tokens), BF)],
         flops=flops // 4,
         nbytes=2 * feat * tokens,
-    )(info, *first_blocks, *second_blocks, other_pack, mixed, scale)
+    )(info, *first_blocks, *second_blocks, other_pack)
     far = [x2, z_move(x2, 3, "route_far"), z_move(x2, z_count - 3, "route_far")]
     lefts = [turned[0]] + [x_move(turned[k], k, "spread_rows") for k in range(1, x_count)]
     keep, send = call(

time: 87.2 us -> 87.1 us (level)
  no operation moved by 1% of the time
where the time goes in v5:
time: 87.1 us; the launch traced here: 86.9 us
  starting transfers between devices  42.7 us (49%)
  waiting for transfers between devices  27 us (31%)
  Pallas kernels  12.8 us (15%)
  local copies, waits for them, and re-layouts  3.41 us (4%)
    ppermute x8, waiting for transfers between devices, z_move(): return lax.ppermute(value, 'rep', pairs)  22 us
    ppermute x8, starting transfers between devices, z_move(): return lax.ppermute(value, 'rep', pairs)  16.1 us
    ppermute x9, starting transfers between devices, tp_move(): return lax.ppermute(value, 'tp', pairs)  13.9 us
    ppermute x9, starting transfers between devices, x_move(): return lax.ppermute(value, 'rep', pairs)  12.4 us
    ppermute x9, waiting for transfers between devices, tp_move(): return lax.ppermute(value, 'tp', pairs)  3.78 us
    unnamed x12, local copies, waits for them, and re-layouts  3.4 us
    pallas_call x1, Pallas kernels, on_device(): call(functools.partial(second_kernel, tp_count, feat, loss_scale), (shape...  2.72 us
  transfers between devices with their start and end apart: 30, of which 12 were waited for; matrix products, arithmetic and copies ran while one was open for 0% of the time, Pallas kernels for 9%

profile of v5, /device:TPU:18, one launch (start us, length us, event | category | flops | bytes accessed | tf_op | source)
XLA Modules:
  0.0 86.9 jit_solution(2396746155991481857)
XLA Ops:
  0.6 0.0 copy-start
  0.6 0.1 collective-permute-start.3
  0.8 0.8 copy-done
  1.6 0.5 collective-permute-start.2
  2.1 2.9 %collective-permute-start.1 = (bf16[64,640]{1,0:T(8,128)(2,1)S(1)}, bf16[64,640]{1,0:T(8,128)(2,1)}, u32[]{:S(2)}, u32[]{:S(2)}) collective-permute-start(bf16[64,640]{1,0:T(8,128)(2,1)S(1)} %dynamic-slice_bitcast_fusion.refs_0_), channel_id=1, source_target_pairs={{0,2},{1,3},{2,0},{3,1},{4,6},{5,7},{6,4},{7,5},{8,10},{9,11},{10,... | collective-permute-start | bytes 245768 | tf_op jit(solution)/shard_map/gather_x0/ppermute | solution.py:374
  5.0 0.0 collective-permute-start
  5.0 0.1 pad_add_fusion.info
  5.1 1.9 %copy-done.1 = bf16[1,2560,640]{2,1,0:T(8,128)(2,1)S(1)} copy-done((bf16[1,2560,640]{2,1,0:T(8,128)(2,1)S(1)}, bf16[1,2560,640]{2,1,0:T(8,128)(2,1)}, u32[]{:S(2)}) %copy-start.1) | copy-done | bytes 3276824
  7.0 0.7 copy-done.4
  7.7 1.6 %plan.1._ = s32[10]{0:T(128)S(1)} custom-call(s32[3]{0:T(128)S(1)} %pad_add_fusion.info, s32[1,1,32]{2,1,0:T(1,128)S(1)} %copy-done.4, bf16[2560,640]{1,0:T(8,128)(2,1)S(1)} %bitcast.10), custom_call_target="tpu_custom_call" | custom-call | tf_op jit(solution)/shard_map/plan/pallas_call | solution.py:399
  9.2 0.0 copy-start.3
  9.2 0.0 copy-start.5
  9.3 0.0 collective-permute-done.1.refs_2_
  9.3 0.3 collective-permute-done.refs_1_
  9.6 1.6 %first.1 = (bf16[64,640]{1,0:T(8,128)(2,1)S(1)}, f32[64,640]{1,0:T(8,128)S(1)}, f32[64,128]{1,0:T(8,128)S(1)}) custom-call(s32[3]{0:T(128)S(1)} %pad_add_fusion.info, s32[10]{0:T(128)S(1)} %plan.1._, bf16[64,640]{1,0:T(8,128)(2,1)S(1)} %dynamic-slice_bitcast_fusion.refs_0_, bf16[64,640]{1,0:T(8,128)(2,1)} %collective-permute-done.refs_1_, ...), custom_call_target="tpu_custom_call" | custom-call | flops 209715200 | bytes 3276800 | tf_op jit(solution)/shard_map/first/pallas_call | solution.py:410
  11.3 2.1 %collective-permute-start.6 = (bf16[64,640]{1,0:T(8,128)(2,1)S(1)}, bf16[64,640]{1,0:T(8,128)(2,1)S(1)}, u32[]{:S(2)}, u32[]{:S(2)}) collective-permute-start(bf16[64,640]{1,0:T(8,128)(2,1)S(1)} %get-tuple-element.31.refs_4_.x1_ref), channel_id=1, source_target_pairs={{0,3},{1,0},{2,1},{3,2},{4,7},{5,4},{6,5},{7,6},{8,11},{9,8},{10,9... | collective-permute-start | bytes 245768 | tf_op jit(solution)/shard_map/gather_x1/ppermute | solution.py:374
  13.3 1.8 %collective-permute-start.5 = (bf16[64,640]{1,0:T(8,128)(2,1)S(1)}, bf16[64,640]{1,0:T(8,128)(2,1)S(1)}, u32[]{:S(2)}, u32[]{:S(2)}) collective-permute-start(bf16[64,640]{1,0:T(8,128)(2,1)S(1)} %get-tuple-element.31.refs_4_.x1_ref), channel_id=1, source_target_pairs={{0,2},{1,3},{2,0},{3,1},{4,6},{5,7},{6,4},{7,5},{8,10},{9,11},{10,... | collective-permute-start | bytes 245768 | tf_op jit(solution)/shard_map/gather_x1/ppermute | solution.py:374
  15.2 1.5 %collective-permute-start.4 = (bf16[64,640]{1,0:T(8,128)(2,1)S(1)}, bf16[64,640]{1,0:T(8,128)(2,1)S(1)}, u32[]{:S(2)}, u32[]{:S(2)}) collective-permute-start(bf16[64,640]{1,0:T(8,128)(2,1)S(1)} %get-tuple-element.31.refs_4_.x1_ref), channel_id=1, source_target_pairs={{0,1},{1,2},{2,3},{3,0},{4,5},{5,6},{6,7},{7,4},{8,9},{9,10},{10,1... | collective-permute-start | bytes 245768 | tf_op jit(solution)/shard_map/gather_x1/ppermute | solution.py:374
  16.6 0.1 slope.1._.refs_4_
  16.7 0.0 collective-permute-done.6.refs_7_
  16.7 2.6 %collective-permute-done.5.refs_6_ = bf16[64,640]{1,0:T(8,128)(2,1)S(1)} collective-permute-done((bf16[64,640]{1,0:T(8,128)(2,1)S(1)}, bf16[64,640]{1,0:T(8,128)(2,1)S(1)}, u32[]{:S(2)}, u32[]{:S(2)}) %collective-permute-start.5) | collective-permute-done | bytes 81952 | tf_op jit(solution)/shard_map/gather_x1/ppermute | solution.py:374
  19.3 0.8 collective-permute-done.4.refs_5_
  20.2 2.7 %second.1 = (bf16[64,640]{1,0:T(8,128)(2,1)S(1)}, bf16[64,640]{1,0:T(8,128)(2,1)S(1)}, bf16[64,2560]{1,0:T(8,128)(2,1)S(1)}, bf16[64,640]{1,0:T(8,128)(2,1)S(1)}...) custom-call(s32[3]{0:T(128)S(1)} %pad_add_fusion.info, ...), custom_call_target="tpu_custom_call" | custom-call | flops 419430400 | bytes 3276800 | tf_op jit(solution)/shard_map/second/pallas_call | solution.py:420
  22.9 0.1 collective-permute-start.13
  23.0 0.6 collective-permute-start.7
  23.6 2.4 %collective-permute-start.8 = (bf16[64,640]{1,0:T(8,128)(2,1)S(1)}, bf16[64,640]{1,0:T(8,128)(2,1)S(1)}, u32[]{:S(2)}, u32[]{:S(2)}) collective-permute-start(bf16[64,640]{1,0:T(8,128)(2,1)S(1)} %get-tuple-element.36), channel_id=1, source_target_pairs={{0,2},{1,3},{2,0},{3,1},{4,6},{5,7},{6,4},{7,5},{8,10},{9,11},{10,... | collective-permute-start | bytes 245768 | tf_op jit(solution)/shard_map/sum_back/ppermute | solution.py:374
  26.1 2.0 %collective-permute-start.9 = (bf16[64,640]{1,0:T(8,128)(2,1)S(1)}, bf16[64,640]{1,0:T(8,128)(2,1)S(1)}, u32[]{:S(2)}, u32[]{:S(2)}) collective-permute-start(bf16[64,640]{1,0:T(8,128)(2,1)S(1)} %get-tuple-element.37), channel_id=1, source_target_pairs={{0,1},{1,2},{2,3},{3,0},{4,5},{5,6},{6,7},{7,4},{8,9},{9,10},{10,1... | collective-permute-start | bytes 245768 | tf_op jit(solution)/shard_map/sum_back/ppermute | solution.py:374
  28.1 6.7 %collective-permute-start.12 = (bf16[64,640]{1,0:T(8,128)(2,1)S(1)}, bf16[64,640]{1,0:T(8,128)(2,1)S(1)}, u32[]{:S(2)}, u32[]{:S(2)}) collective-permute-start(bf16[64,640]{1,0:T(8,128)(2,1)S(1)} %get-tuple-element.41.refs_0_), channel_id=1, source_target_pairs={{0,80},{4,84},{8,88},{12,92},{16,96},{20,100},{24,104},{28,108},{3... | collective-permute-start | bytes 245768 | tf_op jit(solution)/shard_map/route_far/ppermute | solution.py:392
  34.8 1.3 %turn.1 = (bf16[640,128]{1,0:T(8,128)(2,1)S(1)}, bf16[640,128]{1,0:T(8,128)(2,1)S(1)}, bf16[640,128]{1,0:T(8,128)(2,1)S(1)}, bf16[640,128]{1,0:T(8,128)(2,1)S(1)}) custom-call(s32[3]{0:T(128)S(1)} %pad_add_fusion.info, bf16[64,640]{1,0:T(8,128)(2,1)S(1)} %dynamic-slice_bitcast_fusion.refs_0_, bf16[64,640]{1,0:T(8,128)(2,1)} %collective-permute-done.refs_1_, ...), custom_call_target="tpu_custom_call" | custom-call | flops 52428800 | bytes 655360 | tf_op jit(solution)/shard_map/turn/pallas_call | solution.py:431
  36.1 1.6 %collective-permute-start.14 = (bf16[640,128]{1,0:T(8,128)(2,1)S(1)}, bf16[640,128]{1,0:T(8,128)(2,1)S(1)}, u32[]{:S(2)}, u32[]{:S(2)}) collective-permute-start(bf16[640,128]{1,0:T(8,128)(2,1)S(1)} %get-tuple-element.43), channel_id=1, source_target_pairs={{0,4},{4,8},{8,12},{12,0},{16,20},{20,24},{24,28},{28,16},{32,36},... | collective-permute-start | bytes 491528 | tf_op jit(solution)/shard_map/spread_rows/ppermute | solution.py:383
  37.6 1.1 %collective-permute-start.15 = (bf16[640,128]{1,0:T(8,128)(2,1)S(1)}, bf16[640,128]{1,0:T(8,128)(2,1)S(1)}, u32[]{:S(2)}, u32[]{:S(2)}) collective-permute-start(bf16[640,128]{1,0:T(8,128)(2,1)S(1)} %get-tuple-element.44), channel_id=1, source_target_pairs={{0,8},{4,12},{8,0},{12,4},{16,24},{20,28},{24,16},{28,20},{32,40},... | collective-permute-start | bytes 491528 | tf_op jit(solution)/shard_map/spread_rows/ppermute | solution.py:383
  38.8 0.0 collective-permute-done.8.refs_2_
  38.8 2.2 %collective-permute-start.16 = (bf16[640,128]{1,0:T(8,128)(2,1)S(1)}, bf16[640,128]{1,0:T(8,128)(2,1)S(1)}, u32[]{:S(2)}, u32[]{:S(2)}) collective-permute-start(bf16[640,128]{1,0:T(8,128)(2,1)S(1)} %get-tuple-element.45), channel_id=1, source_target_pairs={{0,12},{4,0},{8,4},{12,8},{16,28},{20,16},{24,20},{28,24},{32,44},... | collective-permute-start | bytes 491528 | tf_op jit(solution)/shard_map/spread_rows/ppermute | solution.py:383
  40.9 0.0 collective-permute-done.9.refs_3_
  40.9 0.6 delta.1
  41.5 0.0 collective-permute-done.12.refs_2_
  41.6 0.1 collective-permute-start.10
  41.7 8.1 %collective-permute-done.11.refs_1_ = bf16[64,640]{1,0:T(8,128)(2,1)S(1)} collective-permute-done((bf16[64,640]{1,0:T(8,128)(2,1)S(1)}, bf16[64,640]{1,0:T(8,128)(2,1)S(1)}, u32[]{:S(2)}, u32[]{:S(2)}) %collective-permute-start.11) | collective-permute-done | bytes 81952 | tf_op jit(solution)/shard_map/route_far/ppermute | solution.py:392
  49.8 0.1 collective-permute-start.18
  49.9 2.0 %collective-permute-start.17 = (bf16[3,64,640]{2,1,0:T(8,128)(2,1)S(1)}, bf16[3,64,640]{2,1,0:T(8,128)(2,1)S(1)}, u32[]{:S(2)}, u32[]{:S(2)}) collective-permute-start(bf16[3,64,640]{2,1,0:T(8,128)(2,1)S(1)} %get-tuple-element.46.refs_0_), channel_id=1, source_target_pairs={{0,16},{4,20},{8,24},{12,28},{16,32},{20,36},{24,40},{28,44},{32,4... | collective-permute-start | bytes 737288 | tf_op jit(solution)/shard_map/route_near/ppermute | solution.py:392
  51.9 1.4 %collective-permute-start.25 = (bf16[128,640]{1,0:T(8,128)(2,1)S(1)}, bf16[128,640]{1,0:T(8,128)(2,1)S(1)}, u32[]{:S(2)}, u32[]{:S(2)}) collective-permute-start(bf16[128,640]{1,0:T(8,128)(2,1)S(1)} %get-tuple-element.52.refs_4_), channel_id=1, source_target_pairs={{0,12},{4,0},{8,4},{12,8},{16,28},{20,16},{24,20},{28,24},{32,44},... | collective-permute-start | bytes 491528 | tf_op jit(solution)/shard_map/gather_delta/ppermute | solution.py:383
  53.3 1.8 %collective-permute-start.23 = (bf16[128,640]{1,0:T(8,128)(2,1)S(1)}, bf16[128,640]{1,0:T(8,128)(2,1)S(1)}, u32[]{:S(2)}, u32[]{:S(2)}) collective-permute-start(bf16[128,640]{1,0:T(8,128)(2,1)S(1)} %get-tuple-element.52.refs_4_), channel_id=1, source_target_pairs={{0,4},{4,8},{8,12},{12,0},{16,20},{20,24},{24,28},{28,16},{32,36},... | collective-permute-start | bytes 491528 | tf_op jit(solution)/shard_map/gather_delta/ppermute | solution.py:383
  55.1 1.0 %collective-permute-done.18.refs_2_ = bf16[3,64,640]{2,1,0:T(8,128)(2,1)S(1)} collective-permute-done((bf16[3,64,640]{2,1,0:T(8,128)(2,1)S(1)}, bf16[3,64,640]{2,1,0:T(8,128)(2,1)S(1)}, u32[]{:S(2)}, u32[]{:S(2)}) %collective-permute-start.18) | collective-permute-done | bytes 245792 | tf_op jit(solution)/shard_map/route_near/ppermute | solution.py:392
  56.1 1.3 %collective-permute-done.17.refs_1_ = bf16[3,64,640]{2,1,0:T(8,128)(2,1)S(1)} collective-permute-done((bf16[3,64,640]{2,1,0:T(8,128)(2,1)S(1)}, bf16[3,64,640]{2,1,0:T(8,128)(2,1)S(1)}, u32[]{:S(2)}, u32[]{:S(2)}) %collective-permute-start.17) | collective-permute-done | bytes 245792 | tf_op jit(solution)/shard_map/route_near/ppermute | solution.py:392
  57.4 0.9 route.1
  58.2 0.1 collective-permute-start.19
  58.4 3.4 %collective-permute-start.20 = (bf16[2,64,640]{2,1,0:T(8,128)(2,1)S(1)}, bf16[2,64,640]{2,1,0:T(8,128)(2,1)S(1)}, u32[]{:S(2)}, u32[]{:S(2)}) collective-permute-start(bf16[2,64,640]{2,1,0:T(8,128)(2,1)S(1)} %get-tuple-element.49), channel_id=1, source_target_pairs={{0,8},{4,12},{8,0},{12,4},{16,24},{20,28},{24,16},{28,20},{32,40},... | collective-permute-start | bytes 491528 | tf_op jit(solution)/shard_map/route_x/ppermute | solution.py:383
  61.8 0.7 collective-permute-start.21
  62.6 1.0 %collective-permute-done.23.refs_5_ = bf16[128,640]{1,0:T(8,128)(2,1)S(1)} collective-permute-done((bf16[128,640]{1,0:T(8,128)(2,1)S(1)}, bf16[128,640]{1,0:T(8,128)(2,1)S(1)}, u32[]{:S(2)}, u32[]{:S(2)}) %collective-permute-start.23) | collective-permute-done | bytes 163872 | tf_op jit(solution)/shard_map/gather_delta/ppermute | solution.py:383
  63.5 1.3 %part.1 = (bf16[80,640]{1,0:T(8,128)(2,1)S(1)}, bf16[80,1664]{1,0:T(8,128)(2,1)S(1)}, bf16[80,1536]{1,0:T(8,128)(2,1)S(1)}, bf16[80,640]{1,0:T(8,128)(2,1)S(1)}, bf16[80,640]{1,0:T(8,128)(2,1)S(1)}) custom-call(s32[3]{0:T(128)S(1)} %pad_add_fusion.info, bf16[640,128]{1,0:T(8,128)(2,1)S(1)} %get-tuple-element.51.refs_0_, ...), custom_call_target="tpu_custom_call" | custom-call | flops 419430400 | bytes 1310720 | tf_op jit(solution)/shard_map/part/pallas_call | solution.py:473
  64.8 2.1 %collective-permute-start.27 = (bf16[80,1536]{1,0:T(8,128)(2,1)S(1)}, bf16[80,1536]{1,0:T(8,128)(2,1)S(1)}, u32[]{:S(2)}, u32[]{:S(2)}) collective-permute-start(bf16[80,1536]{1,0:T(8,128)(2,1)S(1)} %get-tuple-element.55), channel_id=1, source_target_pairs={{0,112},{4,116},{8,120},{12,124},{16,0},{20,4},{24,8},{28,12},{32,... | collective-permute-start | bytes 737288 | tf_op jit(solution)/shard_map/part_near/ppermute | solution.py:392
  66.9 0.0 collective-permute-start.26
  67.0 0.2 collective-permute-done.21.refs_3_
  67.2 0.6 pick.1
  67.8 0.1 collective-permute-start.22
  67.9 3.2 %collective-permute-done.27.minus_ref = bf16[80,1536]{1,0:T(8,128)(2,1)S(1)} collective-permute-done((bf16[80,1536]{1,0:T(8,128)(2,1)S(1)}, bf16[80,1536]{1,0:T(8,128)(2,1)S(1)}, u32[]{:S(2)}, u32[]{:S(2)}) %collective-permute-start.27) | collective-permute-done | bytes 245792 | tf_op jit(solution)/shard_map/part_near/ppermute | solution.py:392
  71.1 6.7 %collective-permute-done.26.plus_ref = bf16[80,1664]{1,0:T(8,128)(2,1)S(1)} collective-permute-done((bf16[80,1664]{1,0:T(8,128)(2,1)S(1)}, bf16[80,1664]{1,0:T(8,128)(2,1)S(1)}, u32[]{:S(2)}, u32[]{:S(2)}) %collective-permute-start.26) | collective-permute-done | bytes 266272 | tf_op jit(solution)/shard_map/part_near/ppermute | solution.py:392
  77.8 0.1 middle.1
  77.9 0.1 collective-permute-start.28
  78.0 5.0 %collective-permute-start.29 = (bf16[80,640]{1,0:T(8,128)(2,1)S(1)}, bf16[80,640]{1,0:T(8,128)(2,1)S(1)}, u32[]{:S(2)}, u32[]{:S(2)}) collective-permute-start(bf16[80,640]{1,0:T(8,128)(2,1)S(1)} %get-tuple-element.59), channel_id=1, source_target_pairs={{0,80},{4,84},{8,88},{12,92},{16,96},{20,100},{24,104},{28,108},{3... | collective-permute-start | bytes 307208 | tf_op jit(solution)/shard_map/part_far/ppermute | solution.py:392
  83.0 1.3 %acts.1 = bf16[2,128,640]{2,1,0:T(8,128)(2,1)} custom-call(s32[3]{0:T(128)S(1)} %pad_add_fusion.info, s32[10]{0:T(128)S(1)} %plan.1._, bf16[64,640]{1,0:T(8,128)(2,1)S(1)} %get-tuple-element.31.refs_4_.x1_ref, bf16[2,64,640]{2,1,0:T(8,128)(2,1)S(1)} %collective-permute-done.22.come_ref, bf16[2,64,640]{2,1,0:T(8,128)(2,1)S(1)} %get-tuple-element.47.refs_0_.refs_8_, ...), custom_call_target="tpu_custom_call" | custom-call | tf_op jit(solution)/shard_map/acts/pallas_call | solution.py:499
  84.3 1.3 %collective-permute-done.28.up_ref = bf16[80,640]{1,0:T(8,128)(2,1)S(1)} collective-permute-done((bf16[80,640]{1,0:T(8,128)(2,1)S(1)}, bf16[80,640]{1,0:T(8,128)(2,1)S(1)}, u32[]{:S(2)}, u32[]{:S(2)}) %collective-permute-start.28) | collective-permute-done | bytes 102432 | tf_op jit(solution)/shard_map/part_far/ppermute | solution.py:392
  85.6 0.5 collective-permute-done.29.down_ref
  86.1 0.8 sum.1
  (23 shorter events, 0.1 us)
Async XLA Ops:
  0.6 0.9 %copy-start = (bf16[1,1,128,640]{3,2,1,0:T(8,128)(2,1)S(1)}, bf16[1,1,128,640]{3,2,1,0:T(8,128)(2,1)}, u32[]{:S(2)}) copy-start(bf16[1,1,128,640]{3,2,1,0:T(8,128)(2,1)} %param.5) | copy-start | bytes 491524
  0.6 9.0 %collective-permute-start.3 = (bf16[2560,640]{1,0:T(8,128)(2,1)}, bf16[2560,640]{1,0:T(8,128)(2,1)S(1)}, u32[]{:S(2)}, u32[]{:S(2)}) collective-permute-start(bf16[2560,640]{1,0:T(8,128)(2,1)} %bitcast.9), channel_id=1, source_target_pairs={{0,128},{128,0},{1,129},{129,1},{2,130},{130,2},{3,131},{131,3},{4... | collective-permute-start | bytes 9830408 | tf_op jit(solution)/shard_map/swap_weight/ppermute | solution.py:369
  1.6 7.7 %collective-permute-start.2 = (bf16[64,640]{1,0:T(8,128)(2,1)S(1)}, bf16[64,640]{1,0:T(8,128)(2,1)}, u32[]{:S(2)}, u32[]{:S(2)}) collective-permute-start(bf16[64,640]{1,0:T(8,128)(2,1)S(1)} %dynamic-slice_bitcast_fusion.refs_0_), channel_id=1, source_target_pairs={{0,3},{1,0},{2,1},{3,2},{4,7},{5,4},{6,5},{7,6},{8,11},{9,8},{10,9... | collective-permute-start | bytes 245768 | tf_op jit(solution)/shard_map/gather_x0/ppermute | solution.py:374
  2.1 7.2 %collective-permute-start.1 = (bf16[64,640]{1,0:T(8,128)(2,1)S(1)}, bf16[64,640]{1,0:T(8,128)(2,1)}, u32[]{:S(2)}, u32[]{:S(2)}) collective-permute-start(bf16[64,640]{1,0:T(8,128)(2,1)S(1)} %dynamic-slice_bitcast_fusion.refs_0_), channel_id=1, source_target_pairs={{0,2},{1,3},{2,0},{3,1},{4,6},{5,7},{6,4},{7,5},{8,10},{9,11},{10,... | collective-permute-start | bytes 245768 | tf_op jit(solution)/shard_map/gather_x0/ppermute | solution.py:374
  5.0 4.6 %collective-permute-start = (bf16[64,640]{1,0:T(8,128)(2,1)S(1)}, bf16[64,640]{1,0:T(8,128)(2,1)}, u32[]{:S(2)}, u32[]{:S(2)}) collective-permute-start(bf16[64,640]{1,0:T(8,128)(2,1)S(1)} %dynamic-slice_bitcast_fusion.refs_0_), channel_id=1, source_target_pairs={{0,1},{1,2},{2,3},{3,0},{4,5},{5,6},{6,7},{7,4},{8,9},{9,10},{10,1... | collective-permute-start | bytes 245768 | tf_op jit(solution)/shard_map/gather_x0/ppermute | solution.py:374
  5.1 1.9 %copy-start.1 = (bf16[1,2560,640]{2,1,0:T(8,128)(2,1)S(1)}, bf16[1,2560,640]{2,1,0:T(8,128)(2,1)}, u32[]{:S(2)}) copy-start(bf16[1,2560,640]{2,1,0:T(8,128)(2,1)} %param.6) | copy-start | bytes 9830404
  7.0 0.7 copy-start.4
  7.7 1.9 %copy-start.2 = (bf16[1,2560,640]{2,1,0:T(8,128)(2,1)S(1)}, bf16[1,2560,640]{2,1,0:T(8,128)(2,1)}, u32[]{:S(2)}) copy-start(bf16[1,2560,640]{2,1,0:T(8,128)(2,1)} %param.6) | copy-start | bytes 9830404
  9.2 10.9 %copy-start.3 = (bf16[1,1,128,640]{3,2,1,0:T(8,128)(2,1)S(1)}, bf16[1,1,128,640]{3,2,1,0:T(8,128)(2,1)}, u32[]{:S(2)}) copy-start(bf16[1,1,128,640]{3,2,1,0:T(8,128)(2,1)} %param.9) | copy-start | bytes 491524
  9.2 10.9 %copy-start.5 = (s32[1,32]{1,0:T(1,128)S(1)}, s32[1,32]{1,0:T(1,128)}, u32[]{:S(2)}) copy-start(s32[1,32]{1,0:T(1,128)} %lengths.1) | copy-start | bytes 388
  11.3 5.5 %collective-permute-start.6 = (bf16[64,640]{1,0:T(8,128)(2,1)S(1)}, bf16[64,640]{1,0:T(8,128)(2,1)S(1)}, u32[]{:S(2)}, u32[]{:S(2)}) collective-permute-start(bf16[64,640]{1,0:T(8,128)(2,1)S(1)} %get-tuple-element.31.refs_4_.x1_ref), channel_id=1, source_target_pairs={{0,3},{1,0},{2,1},{3,2},{4,7},{5,4},{6,5},{7,6},{8,11},{9,8},{10,9... | collective-permute-start | bytes 245768 | tf_op jit(solution)/shard_map/gather_x1/ppermute | solution.py:374
  13.3 6.0 %collective-permute-start.5 = (bf16[64,640]{1,0:T(8,128)(2,1)S(1)}, bf16[64,640]{1,0:T(8,128)(2,1)S(1)}, u32[]{:S(2)}, u32[]{:S(2)}) collective-permute-start(bf16[64,640]{1,0:T(8,128)(2,1)S(1)} %get-tuple-element.31.refs_4_.x1_ref), channel_id=1, source_target_pairs={{0,2},{1,3},{2,0},{3,1},{4,6},{5,7},{6,4},{7,5},{8,10},{9,11},{10,... | collective-permute-start | bytes 245768 | tf_op jit(solution)/shard_map/gather_x1/ppermute | solution.py:374
  15.2 5.0 %collective-permute-start.4 = (bf16[64,640]{1,0:T(8,128)(2,1)S(1)}, bf16[64,640]{1,0:T(8,128)(2,1)S(1)}, u32[]{:S(2)}, u32[]{:S(2)}) collective-permute-start(bf16[64,640]{1,0:T(8,128)(2,1)S(1)} %get-tuple-element.31.refs_4_.x1_ref), channel_id=1, source_target_pairs={{0,1},{1,2},{2,3},{3,0},{4,5},{5,6},{6,7},{7,4},{8,9},{9,10},{10,1... | collective-permute-start | bytes 245768 | tf_op jit(solution)/shard_map/gather_x1/ppermute | solution.py:374
  22.9 11.9 %collective-permute-start.13 = (bf16[64,2560]{1,0:T(8,128)(2,1)S(1)}, bf16[64,2560]{1,0:T(8,128)(2,1)S(1)}, u32[]{:S(2)}, u32[]{:S(2)}) collective-permute-start(bf16[64,2560]{1,0:T(8,128)(2,1)S(1)} %get-tuple-element.42), channel_id=1, source_target_pairs={{0,128},{128,0},{1,129},{129,1},{2,130},{130,2},{3,131},{131,3},{4... | collective-permute-start | bytes 983048 | tf_op jit(solution)/shard_map/swap_rows/ppermute | solution.py:369
  23.0 14.7 %collective-permute-start.7 = (bf16[64,640]{1,0:T(8,128)(2,1)S(1)}, bf16[64,640]{1,0:T(8,128)(2,1)S(1)}, u32[]{:S(2)}, u32[]{:S(2)}) collective-permute-start(bf16[64,640]{1,0:T(8,128)(2,1)S(1)} %get-tuple-element.35), channel_id=1, source_target_pairs={{0,3},{1,0},{2,1},{3,2},{4,7},{5,4},{6,5},{7,6},{8,11},{9,8},{10,9... | collective-permute-start | bytes 245768 | tf_op jit(solution)/shard_map/sum_back/ppermute | solution.py:374
  23.6 15.1 %collective-permute-start.8 = (bf16[64,640]{1,0:T(8,128)(2,1)S(1)}, bf16[64,640]{1,0:T(8,128)(2,1)S(1)}, u32[]{:S(2)}, u32[]{:S(2)}) collective-permute-start(bf16[64,640]{1,0:T(8,128)(2,1)S(1)} %get-tuple-element.36), channel_id=1, source_target_pairs={{0,2},{1,3},{2,0},{3,1},{4,6},{5,7},{6,4},{7,5},{8,10},{9,11},{10,... | collective-permute-start | bytes 245768 | tf_op jit(solution)/shard_map/sum_back/ppermute | solution.py:374
  26.1 14.9 %collective-permute-start.9 = (bf16[64,640]{1,0:T(8,128)(2,1)S(1)}, bf16[64,640]{1,0:T(8,128)(2,1)S(1)}, u32[]{:S(2)}, u32[]{:S(2)}) collective-permute-start(bf16[64,640]{1,0:T(8,128)(2,1)S(1)} %get-tuple-element.37), channel_id=1, source_target_pairs={{0,1},{1,2},{2,3},{3,0},{4,5},{5,6},{6,7},{7,4},{8,9},{9,10},{10,1... | collective-permute-start | bytes 245768 | tf_op jit(solution)/shard_map/sum_back/ppermute | solution.py:374
  28.1 13.5 %collective-permute-start.12 = (bf16[64,640]{1,0:T(8,128)(2,1)S(1)}, bf16[64,640]{1,0:T(8,128)(2,1)S(1)}, u32[]{:S(2)}, u32[]{:S(2)}) collective-permute-start(bf16[64,640]{1,0:T(8,128)(2,1)S(1)} %get-tuple-element.41.refs_0_), channel_id=1, source_target_pairs={{0,80},{4,84},{8,88},{12,92},{16,96},{20,100},{24,104},{28,108},{3... | collective-permute-start | bytes 245768 | tf_op jit(solution)/shard_map/route_far/ppermute | solution.py:392
  36.1 13.7 %collective-permute-start.14 = (bf16[640,128]{1,0:T(8,128)(2,1)S(1)}, bf16[640,128]{1,0:T(8,128)(2,1)S(1)}, u32[]{:S(2)}, u32[]{:S(2)}) collective-permute-start(bf16[640,128]{1,0:T(8,128)(2,1)S(1)} %get-tuple-element.43), channel_id=1, source_target_pairs={{0,4},{4,8},{8,12},{12,0},{16,20},{20,24},{24,28},{28,16},{32,36},... | collective-permute-start | bytes 491528 | tf_op jit(solution)/shard_map/spread_rows/ppermute | solution.py:383
  37.6 12.1 %collective-permute-start.15 = (bf16[640,128]{1,0:T(8,128)(2,1)S(1)}, bf16[640,128]{1,0:T(8,128)(2,1)S(1)}, u32[]{:S(2)}, u32[]{:S(2)}) collective-permute-start(bf16[640,128]{1,0:T(8,128)(2,1)S(1)} %get-tuple-element.44), channel_id=1, source_target_pairs={{0,8},{4,12},{8,0},{12,4},{16,24},{20,28},{24,16},{28,20},{32,40},... | collective-permute-start | bytes 491528 | tf_op jit(solution)/shard_map/spread_rows/ppermute | solution.py:383
  38.8 11.0 %collective-permute-start.16 = (bf16[640,128]{1,0:T(8,128)(2,1)S(1)}, bf16[640,128]{1,0:T(8,128)(2,1)S(1)}, u32[]{:S(2)}, u32[]{:S(2)}) collective-permute-start(bf16[640,128]{1,0:T(8,128)(2,1)S(1)} %get-tuple-element.45), channel_id=1, source_target_pairs={{0,12},{4,0},{8,4},{12,8},{16,28},{20,16},{24,20},{28,24},{32,44},... | collective-permute-start | bytes 491528 | tf_op jit(solution)/shard_map/spread_rows/ppermute | solution.py:383
  40.9 8.8 %collective-permute-start.11 = (bf16[64,640]{1,0:T(8,128)(2,1)S(1)}, bf16[64,640]{1,0:T(8,128)(2,1)S(1)}, u32[]{:S(2)}, u32[]{:S(2)}) collective-permute-start(bf16[64,640]{1,0:T(8,128)(2,1)S(1)} %get-tuple-element.41.refs_0_), channel_id=1, source_target_pairs={{0,48},{4,52},{8,56},{12,60},{16,64},{20,68},{24,72},{28,76},{32,8... | collective-permute-start | bytes 245768 | tf_op jit(solution)/shard_map/route_far/ppermute | solution.py:392
  41.6 8.2 %collective-permute-start.10 = (bf16[64,640]{1,0:T(8,128)(2,1)S(1)}, bf16[64,640]{1,0:T(8,128)(2,1)S(1)}, u32[]{:S(2)}, u32[]{:S(2)}) collective-permute-start(bf16[64,640]{1,0:T(8,128)(2,1)S(1)} %get-tuple-element.40), channel_id=1, source_target_pairs={{0,128},{128,0},{1,129},{129,1},{2,130},{130,2},{3,131},{131,3},{4... | collective-permute-start | bytes 245768 | tf_op jit(solution)/shard_map/swap_delta/ppermute | solution.py:369
  49.8 6.3 %collective-permute-start.18 = (bf16[3,64,640]{2,1,0:T(8,128)(2,1)S(1)}, bf16[3,64,640]{2,1,0:T(8,128)(2,1)S(1)}, u32[]{:S(2)}, u32[]{:S(2)}) collective-permute-start(bf16[3,64,640]{2,1,0:T(8,128)(2,1)S(1)} %get-tuple-element.46.refs_0_), channel_id=1, source_target_pairs={{0,112},{4,116},{8,120},{12,124},{16,0},{20,4},{24,8},{28,12},{32,... | collective-permute-start | bytes 737288 | tf_op jit(solution)/shard_map/route_near/ppermute | solution.py:392
  49.9 7.5 %collective-permute-start.17 = (bf16[3,64,640]{2,1,0:T(8,128)(2,1)S(1)}, bf16[3,64,640]{2,1,0:T(8,128)(2,1)S(1)}, u32[]{:S(2)}, u32[]{:S(2)}) collective-permute-start(bf16[3,64,640]{2,1,0:T(8,128)(2,1)S(1)} %get-tuple-element.46.refs_0_), channel_id=1, source_target_pairs={{0,16},{4,20},{8,24},{12,28},{16,32},{20,36},{24,40},{28,44},{32,4... | collective-permute-start | bytes 737288 | tf_op jit(solution)/shard_map/route_near/ppermute | solution.py:392
  51.9 9.9 %collective-permute-start.25 = (bf16[128,640]{1,0:T(8,128)(2,1)S(1)}, bf16[128,640]{1,0:T(8,128)(2,1)S(1)}, u32[]{:S(2)}, u32[]{:S(2)}) collective-permute-start(bf16[128,640]{1,0:T(8,128)(2,1)S(1)} %get-tuple-element.52.refs_4_), channel_id=1, source_target_pairs={{0,12},{4,0},{8,4},{12,8},{16,28},{20,16},{24,20},{28,24},{32,44},... | collective-permute-start | bytes 491528 | tf_op jit(solution)/shard_map/gather_delta/ppermute | solution.py:383
  53.3 9.3 %collective-permute-start.24 = (bf16[128,640]{1,0:T(8,128)(2,1)S(1)}, bf16[128,640]{1,0:T(8,128)(2,1)S(1)}, u32[]{:S(2)}, u32[]{:S(2)}) collective-permute-start(bf16[128,640]{1,0:T(8,128)(2,1)S(1)} %get-tuple-element.52.refs_4_), channel_id=1, source_target_pairs={{0,8},{4,12},{8,0},{12,4},{16,24},{20,28},{24,16},{28,20},{32,40},... | collective-permute-start | bytes 491528 | tf_op jit(solution)/shard_map/gather_delta/ppermute | solution.py:383
  53.3 10.2 %collective-permute-start.23 = (bf16[128,640]{1,0:T(8,128)(2,1)S(1)}, bf16[128,640]{1,0:T(8,128)(2,1)S(1)}, u32[]{:S(2)}, u32[]{:S(2)}) collective-permute-start(bf16[128,640]{1,0:T(8,128)(2,1)S(1)} %get-tuple-element.52.refs_4_), channel_id=1, source_target_pairs={{0,4},{4,8},{8,12},{12,0},{16,20},{20,24},{24,28},{28,16},{32,36},... | collective-permute-start | bytes 491528 | tf_op jit(solution)/shard_map/gather_delta/ppermute | solution.py:383
  58.2 8.7 %collective-permute-start.19 = (bf16[2,64,640]{2,1,0:T(8,128)(2,1)S(1)}, bf16[2,64,640]{2,1,0:T(8,128)(2,1)S(1)}, u32[]{:S(2)}, u32[]{:S(2)}) collective-permute-start(bf16[2,64,640]{2,1,0:T(8,128)(2,1)S(1)} %get-tuple-element.48), channel_id=1, source_target_pairs={{0,4},{4,8},{8,12},{12,0},{16,20},{20,24},{24,28},{28,16},{32,36},... | collective-permute-start | bytes 491528 | tf_op jit(solution)/shard_map/route_x/ppermute | solution.py:383
  58.4 8.6 %collective-permute-start.20 = (bf16[2,64,640]{2,1,0:T(8,128)(2,1)S(1)}, bf16[2,64,640]{2,1,0:T(8,128)(2,1)S(1)}, u32[]{:S(2)}, u32[]{:S(2)}) collective-permute-start(bf16[2,64,640]{2,1,0:T(8,128)(2,1)S(1)} %get-tuple-element.49), channel_id=1, source_target_pairs={{0,8},{4,12},{8,0},{12,4},{16,24},{20,28},{24,16},{28,20},{32,40},... | collective-permute-start | bytes 491528 | tf_op jit(solution)/shard_map/route_x/ppermute | solution.py:383
  61.8 5.3 %collective-permute-start.21 = (bf16[2,64,640]{2,1,0:T(8,128)(2,1)S(1)}, bf16[2,64,640]{2,1,0:T(8,128)(2,1)S(1)}, u32[]{:S(2)}, u32[]{:S(2)}) collective-permute-start(bf16[2,64,640]{2,1,0:T(8,128)(2,1)S(1)} %get-tuple-element.50), channel_id=1, source_target_pairs={{0,12},{4,0},{8,4},{12,8},{16,28},{20,16},{24,20},{28,24},{32,44},... | collective-permute-start | bytes 491528 | tf_op jit(solution)/shard_map/route_x/ppermute | solution.py:383
  64.8 6.3 %collective-permute-start.27 = (bf16[80,1536]{1,0:T(8,128)(2,1)S(1)}, bf16[80,1536]{1,0:T(8,128)(2,1)S(1)}, u32[]{:S(2)}, u32[]{:S(2)}) collective-permute-start(bf16[80,1536]{1,0:T(8,128)(2,1)S(1)} %get-tuple-element.55), channel_id=1, source_target_pairs={{0,112},{4,116},{8,120},{12,124},{16,0},{20,4},{24,8},{28,12},{32,... | collective-permute-start | bytes 737288 | tf_op jit(solution)/shard_map/part_near/ppermute | solution.py:392
  66.9 10.9 %collective-permute-start.26 = (bf16[80,1664]{1,0:T(8,128)(2,1)S(1)}, bf16[80,1664]{1,0:T(8,128)(2,1)S(1)}, u32[]{:S(2)}, u32[]{:S(2)}) collective-permute-start(bf16[80,1664]{1,0:T(8,128)(2,1)S(1)} %get-tuple-element.54), channel_id=1, source_target_pairs={{0,16},{4,20},{8,24},{12,28},{16,32},{20,36},{24,40},{28,44},{32,4... | collective-permute-start | bytes 798728 | tf_op jit(solution)/shard_map/part_near/ppermute | solution.py:392
  67.8 15.2 %collective-permute-start.22 = (bf16[2,64,640]{2,1,0:T(8,128)(2,1)S(1)}, bf16[2,64,640]{2,1,0:T(8,128)(2,1)S(1)}, u32[]{:S(2)}, u32[]{:S(2)}) collective-permute-start(bf16[2,64,640]{2,1,0:T(8,128)(2,1)S(1)} %pick.1), channel_id=1, source_target_pairs={{0,128},{128,0},{1,129},{129,1},{2,130},{130,2},{3,131},{131,3},{4... | collective-permute-start | bytes 491528 | tf_op jit(solution)/shard_map/swap_acts/ppermute | solution.py:369
  77.9 7.7 %collective-permute-start.28 = (bf16[80,640]{1,0:T(8,128)(2,1)S(1)}, bf16[80,640]{1,0:T(8,128)(2,1)S(1)}, u32[]{:S(2)}, u32[]{:S(2)}) collective-permute-start(bf16[80,640]{1,0:T(8,128)(2,1)S(1)} %get-tuple-element.58), channel_id=1, source_target_pairs={{0,48},{4,52},{8,56},{12,60},{16,64},{20,68},{24,72},{28,76},{32,8... | collective-permute-start | bytes 307208 | tf_op jit(solution)/shard_map/part_far/ppermute | solution.py:392
  78.0 8.1 %collective-permute-start.29 = (bf16[80,640]{1,0:T(8,128)(2,1)S(1)}, bf16[80,640]{1,0:T(8,128)(2,1)S(1)}, u32[]{:S(2)}, u32[]{:S(2)}) collective-permute-start(bf16[80,640]{1,0:T(8,128)(2,1)S(1)} %get-tuple-element.59), channel_id=1, source_target_pairs={{0,80},{4,84},{8,88},{12,92},{16,96},{20,100},{24,104},{28,108},{3... | collective-permute-start | bytes 307208 | tf_op jit(solution)/shard_map/part_far/ppermute | solution.py:392
